TPU v7x, 256 devices: a whole 4x4x8 slice. The times are simulated.
256 devices in a mesh: animal: 8 (over x, core), marker: 32 (over y, z).
Axes of the slice: x: 4, y: 4, z: 8, core: 2. Of those that a mesh axis runs over, the one named last changes fastest.
Arguments:
- genotype: float32 [12288, 49152], P('animal', 'marker'), may hold values from 0 to 2, as said below
- allele_freq: float32 [49152], P('marker'), may hold values from 0.05 to 0.5
- shrink: float32 [49152], P('marker'), may hold values from 0.05 to 0.6
- right_side: float32 [32, 49152], P(None, 'marker'), may hold values from -6 to 6
Outputs:
- solution: float32 [32, 49152], P(None, 'marker')
- residual: float32 [32, 49152], P(None, 'marker')
Inputs may be any that keep to these rules, and one draw needn't show every extreme that they name: genotype codes are 0, 1 or 2.
All inputs are finite; a program needn't handle non-finite values.
Results may differ from a plain program's by a relative error of at most 0.002.
Values sent between devices are 32-bit elements; how exact they have to be, the bound alone decides.
No kernel may reach another device: no remote copies, remote signals or barrier semaphores. Data moves between devices by JAX's collectives and lax.ppermute only.
A program may use at most 64 MiB of HBM per device.

v0:
```python
import jax
import jax.numpy as jnp
from jax import lax
from jax.sharding import PartitionSpec as P

ITERS = 4


def body(genotype, allele_freq, shrink, right_side):
    a_rows = genotype.shape[0]
    count = jnp.float32(a_rows * lax.axis_size("animal"))
    inv_count = jnp.float32(1.0) / count
    precond_full = 2.0 * allele_freq * (1.0 - allele_freq) + shrink
    freq_own, shrink_own, precond = (allele_freq, shrink, precond_full)
    residual = right_side

    def inner(left, right):
        local_dot = jnp.sum(left * right, axis=1)
        return lax.psum(local_dot, "marker")

    solution = jnp.zeros_like(residual)
    scaled = residual / precond[None, :]
    direction = scaled
    rho_now = inner(residual, scaled)
    for step in range(ITERS):
        offset = jnp.sum(2.0 * allele_freq[None, :] * direction, axis=1)
        partial_value = (
            lax.dot_general(
                direction,
                genotype,
                (((1,), (1,)), ((), ())),
                precision=lax.Precision.HIGHEST,
                preferred_element_type=jnp.float32,
            )
            - offset[:, None]
        )
        row_values = lax.psum(partial_value, "marker")
        col_part = jnp.dot(
            row_values,
            genotype,
            precision=lax.Precision.HIGHEST,
            preferred_element_type=jnp.float32,
        )
        row_total = jnp.sum(row_values, axis=1)
        col_part, row_total = (col_part, row_total)
        col_terms, row_sum = lax.psum((col_part, row_total), "animal")
        image = (col_terms - 2.0 * freq_own[None, :] * row_sum[:, None]) * inv_count + shrink_own[
            None, :
        ] * direction
        curve = inner(direction, image)
        step_len = rho_now / curve
        solution = solution + step_len[:, None] * direction
        residual = residual - step_len[:, None] * image
        scaled = residual / precond[None, :]
        rho_new = inner(residual, scaled)
        direction = scaled + (rho_new / rho_now)[:, None] * direction
        rho_now = rho_new
    return (solution, residual)


def solution(mesh):
    placed = (P("animal", "marker"), P("marker"), P("marker"), P(None, "marker"))
    return jax.shard_map(
        body,
        mesh=mesh,
        in_specs=placed,
        out_specs=(P(None, "marker"), P(None, "marker")),
        check_vma=False,
    )
```

profile of v0, /device:TPU:1, one launch (start us, length us, event | category | flops | bytes accessed | tf_op | source)
XLA Modules:
  0.0 1411.0 jit_solution(13749185263158881050)
XLA Ops:
  7.2 0.0 all-reduce.10.cloned.1.call-start
  7.2 0.7 multiply_add_fusion.8
  7.9 1.1 multiply_reduce_fusion.10
  9.0 0.0 copy-start
  9.0 0.0 copy-start.5
  9.0 13.0 convolution_subtract_fusion.3
  22.0 0.0 all-reduce.10.cloned.1.call-update
  22.0 0.0 all-reduce.12.cloned.1.call-start
  22.1 142.0 %all-reduce.10.cloned.1.call-done = f32[32,1536]{1,0:T(8,128)} async-done(((f32[32,1536]{1,0:T(8,128)}), f32[32,1536]{1,0:T(8,128)}) %all-reduce.10.cloned.1.call-update) | async-done | bytes 196624 | tf_op jit(solution)/shard_map/psum | solution.py:37
  164.0 10.0 fusion
  174.0 0.0 all-reduce.12.cloned.1.call-update
  174.0 0.0 all-reduce.14.cloned.1.call-start
  174.1 0.1 reduce_sum.146
  174.2 16.9 %psum.143 = f32[32]{0:T(128)S(1)} all-reduce(f32[32]{0:T(128)S(1)} %reduce_sum.146), channel_id=1, replica_groups=mesh['animal'=8,'marker'=32] {'animal'}, use_global_device_ids=true, to_apply=%region_6.0 | all-reduce | flops 32 | bytes 256 | tf_op jit(solution)/shard_map/psum | solution.py:46
  191.1 47.6 %all-reduce.12.cloned.1.call-done = f32[32,1536]{1,0:T(8,128)} async-done(((f32[32,1536]{1,0:T(8,128)}), f32[32,1536]{1,0:T(8,128)}) %all-reduce.12.cloned.1.call-update) | async-done | bytes 196624 | tf_op jit(solution)/shard_map/psum | solution.py:46
  238.7 1.1 multiply_reduce_fusion.9
  239.9 61.3 %all-reduce = (f32[32]{0:T(128)S(1)}, f32[32]{0:T(128)S(1)}) all-reduce(f32[32]{0:T(128)S(1)} %get-tuple-element.3, f32[32]{0:T(128)S(1)} %get-tuple-element.2), channel_id=1, replica_groups=mesh['animal'=8,'marker'=32] {'marker'}, use_global_device_ids=true, to_apply=%region_1.0 | all-reduce | flops 64 | bytes 512 | tf_op jit(solution)/shard_map/psum | solution.py:19
  301.2 1.2 multiply_reduce_fusion.8
  302.4 56.1 %psum.145 = f32[32]{0:T(128)S(1)} all-reduce(f32[32]{0:T(128)S(1)} %get-tuple-element.16), channel_id=1, replica_groups=mesh['animal'=8,'marker'=32] {'marker'}, use_global_device_ids=true, to_apply=%region_10.0 | all-reduce | flops 32 | bytes 256 | tf_op jit(solution)/shard_map/psum | solution.py:19
  358.5 0.2 multiply_reduce_fusion.7
  358.7 11.7 convolution_subtract_fusion.2
  370.4 0.0 all-reduce.14.cloned.1.call-update
  370.4 0.0 all-reduce.16.cloned.1.call-start
  370.4 160.5 %all-reduce.14.cloned.1.call-done = f32[32,1536]{1,0:T(8,128)} async-done(((f32[32,1536]{1,0:T(8,128)}), f32[32,1536]{1,0:T(8,128)}) %all-reduce.14.cloned.1.call-update) | async-done | bytes 196624 | tf_op jit(solution)/shard_map/psum | solution.py:37
  530.9 9.9 fusion.1
  540.9 0.0 all-reduce.16.cloned.1.call-update
  540.9 0.0 all-reduce.18.cloned.1.call-start
  540.9 0.0 copy-done.2
  541.0 0.1 reduce_sum.150
  541.1 16.9 %psum.148 = f32[32]{0:T(128)S(1)} all-reduce(f32[32]{0:T(128)S(1)} %reduce_sum.150), channel_id=1, replica_groups=mesh['animal'=8,'marker'=32] {'animal'}, use_global_device_ids=true, to_apply=%region_15.0 | all-reduce | flops 32 | bytes 256 | tf_op jit(solution)/shard_map/psum | solution.py:46
  558.0 47.6 %all-reduce.16.cloned.1.call-done = f32[32,1536]{1,0:T(8,128)} async-done(((f32[32,1536]{1,0:T(8,128)}), f32[32,1536]{1,0:T(8,128)}) %all-reduce.16.cloned.1.call-update) | async-done | bytes 196624 | tf_op jit(solution)/shard_map/psum | solution.py:46
  605.6 1.1 multiply_reduce_fusion.6
  606.7 61.1 %psum.149 = f32[32]{0:T(128)S(1)} all-reduce(f32[32]{0:T(128)S(1)} %multiply_reduce_fusion.6), channel_id=1, replica_groups=mesh['animal'=8,'marker'=32] {'marker'}, use_global_device_ids=true, to_apply=%region_17.0 | all-reduce | flops 32 | bytes 256 | tf_op jit(solution)/shard_map/psum | solution.py:19
  667.9 1.2 multiply_reduce_fusion.5
  669.1 56.4 %psum.150 = f32[32]{0:T(128)S(1)} all-reduce(f32[32]{0:T(128)S(1)} %get-tuple-element.12), channel_id=1, replica_groups=mesh['animal'=8,'marker'=32] {'marker'}, use_global_device_ids=true, to_apply=%region_19.0 | all-reduce | flops 32 | bytes 256 | tf_op jit(solution)/shard_map/psum | solution.py:19
  725.5 0.2 multiply_reduce_fusion.4
  725.7 11.7 convolution_subtract_fusion.1
  737.4 0.0 all-reduce.18.cloned.1.call-update
  737.4 0.0 all-reduce.20.cloned.1.call-start
  737.5 160.4 %all-reduce.18.cloned.1.call-done = f32[32,1536]{1,0:T(8,128)} async-done(((f32[32,1536]{1,0:T(8,128)}), f32[32,1536]{1,0:T(8,128)}) %all-reduce.18.cloned.1.call-update) | async-done | bytes 196624 | tf_op jit(solution)/shard_map/psum | solution.py:37
  897.9 10.0 fusion.2
  907.9 0.0 all-reduce.20.cloned.1.call-update
  907.9 0.0 all-reduce.22.cloned.1.call-start
  907.9 0.1 reduce_sum.154
  908.1 16.9 %psum.153 = f32[32]{0:T(128)S(1)} all-reduce(f32[32]{0:T(128)S(1)} %reduce_sum.154), channel_id=1, replica_groups=mesh['animal'=8,'marker'=32] {'animal'}, use_global_device_ids=true, to_apply=%region_24.0 | all-reduce | flops 32 | bytes 256 | tf_op jit(solution)/shard_map/psum | solution.py:46
  925.0 47.6 %all-reduce.20.cloned.1.call-done = f32[32,1536]{1,0:T(8,128)} async-done(((f32[32,1536]{1,0:T(8,128)}), f32[32,1536]{1,0:T(8,128)}) %all-reduce.20.cloned.1.call-update) | async-done | bytes 196624 | tf_op jit(solution)/shard_map/psum | solution.py:46
  972.6 1.1 multiply_reduce_fusion.3
  973.7 61.1 %psum.154 = f32[32]{0:T(128)S(1)} all-reduce(f32[32]{0:T(128)S(1)} %multiply_reduce_fusion.3), channel_id=1, replica_groups=mesh['animal'=8,'marker'=32] {'marker'}, use_global_device_ids=true, to_apply=%region_26.0 | all-reduce | flops 32 | bytes 256 | tf_op jit(solution)/shard_map/psum | solution.py:19
  1034.9 1.2 multiply_reduce_fusion.2
  1036.0 56.5 %psum.155 = f32[32]{0:T(128)S(1)} all-reduce(f32[32]{0:T(128)S(1)} %get-tuple-element.8), channel_id=1, replica_groups=mesh['animal'=8,'marker'=32] {'marker'}, use_global_device_ids=true, to_apply=%region_28.0 | all-reduce | flops 32 | bytes 256 | tf_op jit(solution)/shard_map/psum | solution.py:19
  1092.5 0.2 multiply_reduce_fusion.1
  1092.7 11.7 convolution_subtract_fusion
  1104.4 0.0 all-reduce.22.cloned.1.call-update
  1104.4 0.0 all-reduce.24.cloned.1.call-start
  1104.5 160.4 %all-reduce.22.cloned.1.call-done = f32[32,1536]{1,0:T(8,128)} async-done(((f32[32,1536]{1,0:T(8,128)}), f32[32,1536]{1,0:T(8,128)}) %all-reduce.22.cloned.1.call-update) | async-done | bytes 196624 | tf_op jit(solution)/shard_map/psum | solution.py:37
  1264.9 9.9 fusion.3
  1274.8 0.0 all-reduce.24.cloned.1.call-update
  1274.8 0.0 copy-done.4
  1274.8 0.1 reduce_sum.158
  1275.0 16.9 %psum.158 = f32[32]{0:T(128)S(1)} all-reduce(f32[32]{0:T(128)S(1)} %reduce_sum.158), channel_id=1, replica_groups=mesh['animal'=8,'marker'=32] {'animal'}, use_global_device_ids=true, to_apply=%region_33.0 | all-reduce | flops 32 | bytes 256 | tf_op jit(solution)/shard_map/psum | solution.py:46
  1291.9 47.7 %all-reduce.24.cloned.1.call-done = f32[32,1536]{1,0:T(8,128)} async-done(((f32[32,1536]{1,0:T(8,128)}), f32[32,1536]{1,0:T(8,128)}) %all-reduce.24.cloned.1.call-update) | async-done | bytes 196624 | tf_op jit(solution)/shard_map/psum | solution.py:46
  1339.5 1.1 multiply_reduce_fusion
  1340.7 61.1 %psum.159 = f32[32]{0:T(128)S(1)} all-reduce(f32[32]{0:T(128)S(1)} %multiply_reduce_fusion), channel_id=1, replica_groups=mesh['animal'=8,'marker'=32] {'marker'}, use_global_device_ids=true, to_apply=%region_35.0 | all-reduce | flops 32 | bytes 256 | tf_op jit(solution)/shard_map/psum | solution.py:19
  1401.8 1.8 multiply_subtract_fusion
  (15 shorter events, 0.1 us)
Async XLA Ops:
  7.2 156.9 %all-reduce.10.cloned.1.call-start = ((), (), s32[]{:S(2)}) async-start(), calls=%async_computation | async-start | bytes 393216 | tf_op jit(solution)/shard_map/psum | solution.py:37
  9.0 229.7 %copy-start = (f32[32,1536]{1,0:T(8,128)S(1)}, f32[32,1536]{1,0:T(8,128)}, u32[]{:S(2)}) copy-start(f32[32,1536]{1,0:T(8,128)} %param.7) | copy-start | bytes 589828
  9.0 229.7 %copy-start.5 = (f32[1536]{0:T(1024)S(1)}, f32[1536]{0:T(1024)}, u32[]{:S(2)}) copy-start(f32[1536]{0:T(1024)} %param.6) | copy-start | bytes 18436
  22.0 216.7 %all-reduce.12.cloned.1.call-start = ((), (), s32[]{:S(2)}) async-start(), calls=%async_computation.1 | async-start | bytes 393216 | tf_op jit(solution)/shard_map/psum | solution.py:46
  164.0 10.0 copy-start.1
  174.0 356.9 %all-reduce.14.cloned.1.call-start = ((), (), s32[]{:S(2)}) async-start(), calls=%async_computation.2 | async-start | bytes 393216 | tf_op jit(solution)/shard_map/psum | solution.py:37
  370.4 235.2 %all-reduce.16.cloned.1.call-start = ((), (), s32[]{:S(2)}) async-start(), calls=%async_computation.3 | async-start | bytes 393216 | tf_op jit(solution)/shard_map/psum | solution.py:46
  530.9 10.0 copy-start.2
  540.9 357.0 %all-reduce.18.cloned.1.call-start = ((), (), s32[]{:S(2)}) async-start(), calls=%async_computation.4 | async-start | bytes 393216 | tf_op jit(solution)/shard_map/psum | solution.py:37
  737.4 235.2 %all-reduce.20.cloned.1.call-start = ((), (), s32[]{:S(2)}) async-start(), calls=%async_computation.5 | async-start | bytes 393216 | tf_op jit(solution)/shard_map/psum | solution.py:46
  897.9 10.0 copy-start.3
  907.9 357.0 %all-reduce.22.cloned.1.call-start = ((), (), s32[]{:S(2)}) async-start(), calls=%async_computation.6 | async-start | bytes 393216 | tf_op jit(solution)/shard_map/psum | solution.py:37
  1104.4 235.1 %all-reduce.24.cloned.1.call-start = ((), (), s32[]{:S(2)}) async-start(), calls=%async_computation.7 | async-start | bytes 393216 | tf_op jit(solution)/shard_map/psum | solution.py:46
  1264.9 10.0 copy-start.4
Sparse Core Ops, SparseCore 0:
  22.1 141.8 all-reduce.9
  174.1 64.5 all-reduce.11
  370.5 160.3 all-reduce.13
  541.0 64.5 all-reduce.15
  737.5 160.3 all-reduce.17
  908.0 64.5 all-reduce.19
  1104.6 160.2 all-reduce.21
  1275.0 64.5 all-reduce.23
where the time goes:
time: 1430 us; the launch traced here: 1410 us
  waiting for transfers between devices  814 us (57%)
  blocking collectives  481 us (34%)
  matrix products  87.8 us (6%)
  between operations  14.6 us (1%)
    psum x4, waiting for transfers between devices, body(): row_values = lax.psum(partial_value, 'marker')  623 us
    psum x7, blocking collectives, inner(): return lax.psum(local_dot, 'marker')  414 us
    psum x4, waiting for transfers between devices, body(): col_terms, row_sum = lax.psum((col_part, row_total), 'animal')  191 us
    psum x4, blocking collectives, body(): col_terms, row_sum = lax.psum((col_part, row_total), 'animal')  67.6 us
    dot_general x4, matrix products, body(): lax.dot_general(direction, genotype, (((1,), (1,)), ((), ())), precision=...  48 us
    dot_general x4, matrix products, body(): jnp.dot(row_values, genotype, precision=lax.Precision.HIGHEST, preferred_...  39.8 us
  transfers between devices with their start and end apart: 8, of which 8 were waited for; matrix products, arithmetic and copies ran while one was open for 0% of the time, Pallas kernels for 0%

commit v1 on v0

v1 whole, which is shorter than its diff:
```python
import jax
import jax.numpy as jnp
from jax import lax
from jax.sharding import PartitionSpec as P

ITERS = 4


def split2(v):
    hi = lax.reduce_precision(v, 8, 7)
    lo = lax.reduce_precision(v - hi, 8, 7)
    return jnp.concatenate([hi, lo], axis=0).astype(jnp.bfloat16)


def body(genotype, allele_freq, shrink, right_side):
    cores = 2
    xs = lax.axis_size("animal") // cores
    count = genotype.shape[0] * lax.axis_size("animal")
    inv_count = jnp.float32(1.0) / jnp.float32(count)
    rhs, width = right_side.shape
    geno = genotype.astype(jnp.bfloat16)
    twice = 2.0 * allele_freq[None, :]
    own_shrink = shrink[None, :]
    precond = 2.0 * allele_freq * (1.0 - allele_freq) + shrink
    precond = precond[None, :]

    def product(vec, dim):
        both = lax.dot_general(
            split2(vec), geno, (((1,), (dim,)), ((), ())), preferred_element_type=jnp.float32
        )
        return both[:rhs] + both[rhs:]

    def extend(main, scalars):
        pad = jnp.stack(scalars, axis=1)
        pad = jnp.pad(pad, ((0, 0), (0, 128 - len(scalars))))
        return jnp.concatenate([main, pad], axis=1)

    def marker_sum(part):
        got = lax.all_to_all(part, "marker", 0, 0, tiled=True)
        total = jnp.sum(got, axis=0, keepdims=True)
        return lax.all_to_all(jnp.broadcast_to(total, part.shape), "marker", 0, 0, tiled=True)

    def animal_sum(part):
        swap = [(x * cores + c, x * cores + 1 - c) for x in range(xs) for c in range(cores)]
        part = part + lax.ppermute(part, "animal", swap)
        moved = [
            lax.ppermute(
                part,
                "animal",
                [(x * cores + c, (x + d) % xs * cores + c) for x in range(xs) for c in range(cores)],
            )
            for d in range(1, xs)
        ]
        return part + sum(moved[1:], moved[0])

    residual = right_side
    solution = jnp.zeros_like(residual)
    direction = jnp.zeros_like(residual)
    row_values = jnp.zeros((rhs, genotype.shape[0]), jnp.float32)
    rho = None
    for step in range(ITERS):
        scaled = residual / precond
        part = product(scaled, 1) - jnp.sum(twice * scaled, axis=1)[:, None]
        weighted = own_shrink * scaled
        scalars = [
            jnp.sum(residual * scaled, axis=1),
            jnp.sum(weighted * scaled, axis=1),
            jnp.sum(weighted * direction, axis=1),
        ]
        total = marker_sum(extend(part, scalars))
        new_rows = total[:, : part.shape[1]]
        new_rho, square, cross = (total[:, part.shape[1] + i] for i in range(3))
        if step == 0:
            direction, row_values, shrunk = scaled, new_rows, square
        else:
            beta = new_rho / rho
            direction = scaled + beta[:, None] * direction
            row_values = new_rows + beta[:, None] * row_values
            shrunk = square + beta * (2.0 * cross + beta * shrunk)
        rho = new_rho
        cols = product(row_values, 0) - twice * jnp.sum(row_values, axis=1)[:, None]
        total = animal_sum(extend(cols, [jnp.sum(row_values * row_values, axis=1)]))
        image = total[:, :width] * inv_count + own_shrink * direction
        curve = total[:, width] * inv_count + shrunk
        step_len = (rho / curve)[:, None]
        solution = solution + step_len * direction
        residual = residual - step_len * image
    return solution, residual


def solution(mesh):
    placed = (P("animal", "marker"), P("marker"), P("marker"), P(None, "marker"))
    return jax.shard_map(
        body,
        mesh=mesh,
        in_specs=placed,
        out_specs=(P(None, "marker"), P(None, "marker")),
        check_vma=False,
    )
```

time: 1430 us -> 238 us (0.17); the launches traced: 1410 us -> 237 us
  waiting for transfers between devices: 814 us -> 52.1 us
  blocking collectives: 481 us -> 120 us
  matrix products: 87.8 us -> 26.1 us
  starting transfers between devices: 0.33 us -> 21.3 us
    psum x8 -> x0, waiting for transfers between devices: 814 us -> none  [the longest x4 623 us: body(): row_values = lax.psum(partial_value, 'marker')]
    psum x11 -> x0, blocking collectives: 481 us -> none  [the longest x7 414 us: inner(): return lax.psum(local_dot, 'marker')]
    all_to_all x0 -> x8, blocking collectives: none -> 120 us  [the longest x4 60.7 us: marker_sum(): got = lax.all_to_all(part, 'marker', 0, 0, tiled=True)]
    dot_general x8, matrix products: 87.8 us -> 26.1 us  [product(): lax.dot_general(split2(vec), geno, (((1,), (dim,)), ((), ())), preferred_...]
    ppermute x0 -> x16, waiting for transfers between devices: none -> 52.1 us  [the longest x12 47.7 us: animal_sum(): lax.ppermute(part, 'animal', [(x * cores + c, (x + d) % xs * cores + c) f...]
    ppermute x0 -> x16, starting transfers between devices: none -> 21.3 us  [the longest x4 13 us: animal_sum(): part = part + lax.ppermute(part, 'animal', swap)]
  transfers between devices with their start and end apart: 8 -> 16, of which waited for: 8 -> 15; matrix products, arithmetic and copies ran while one was open for 0% -> 0% of each run, Pallas kernels for 0% -> 0%
where the time goes in v1:
time: 238 us; the launch traced here: 237 us
  blocking collectives  120 us (50%)
  waiting for transfers between devices  52.1 us (22%)
  matrix products  26.1 us (11%)
  starting transfers between devices  21.3 us (9%)
  other arithmetic  12 us (5%)
  local copies, waits for them, and re-layouts  4.23 us (2%)
    all_to_all x4, blocking collectives, marker_sum(): got = lax.all_to_all(part, 'marker', 0, 0, tiled=True)  60.7 us
    all_to_all x4, blocking collectives, marker_sum(): lax.all_to_all(jnp.broadcast_to(total, part.shape), 'marker', 0, 0, tiled...  59.7 us
    ppermute x12, waiting for transfers between devices, animal_sum(): lax.ppermute(part, 'animal', [(x * cores + c, (x + d) % xs * cores + c) f...  47.7 us
    dot_general x8, matrix products, product(): lax.dot_general(split2(vec), geno, (((1,), (dim,)), ((), ())), preferred_...  26.1 us
    ppermute x4, starting transfers between devices, animal_sum(): part = part + lax.ppermute(part, 'animal', swap)  13 us
    ppermute x12, starting transfers between devices, animal_sum(): lax.ppermute(part, 'animal', [(x * cores + c, (x + d) % xs * cores + c) f...  8.31 us
  transfers between devices with their start and end apart: 16, of which 15 were waited for; matrix products, arithmetic and copies ran while one was open for 0% of the time, Pallas kernels for 0%

profile of v1, /device:TPU:1, one launch (start us, length us, event | category | flops | bytes accessed | tf_op | source)
XLA Modules:
  0.0 237.1 jit_solution(14584539467374505016)
XLA Ops:
  0.6 0.7 broadcast_multiply_fusion
  1.3 1.2 fusion.4
  2.6 4.3 %convert_element_type.12 = bf16[1536,1536]{1,0:T(8,128)(2,1)S(1)} convert(f32[1536,1536]{1,0:T(8,128)} %param.4) | non-fusion elementwise | flops 2359296 | bytes 14155776 | tf_op jit(solution)/shard_map/convert_element_type | solution.py:21
  6.9 2.1 copy-done
  9.0 1.5 fusion.47
  10.7 0.2 copy.39
  10.9 21.3 %all_to_all.72 = f32[32,1,1664]{2,1,0:T(1,128)S(1)} all-to-all(f32[32,1,1664]{2,1,0:T(1,128)S(1)} %copy.39), channel_id=1, replica_groups=mesh['animal'=8,'marker'=32] {'marker'}, dimensions={0} | all-to-all | bytes 425984 | tf_op jit(solution)/shard_map/all_to_all | solution.py:39
  32.5 14.9 %all_to_all.73 = f32[32,1,1664]{2,1,0:T(1,128)S(1)} all-to-all(f32[32,1,1664]{2,1,0:T(1,128)S(1)} %broadcast_in_dim.11), channel_id=1, replica_groups=mesh['animal'=8,'marker'=32] {'marker'}, dimensions={0} | all-to-all | bytes 425984 | tf_op jit(solution)/shard_map/all_to_all | solution.py:41
  47.5 0.2 reduce-precision_convert_fusion.6
  47.7 3.3 %fusion.51 = f32[64,1536]{1,0:T(8,128)S(1)} fusion(bf16[1536,1536]{1,0:T(8,128)(2,1)} %copy-done, bf16[32,1536]{1,0:T(8,128)(2,1)S(1)} %get-tuple-element.46, bf16[32,1536]{1,0:T(8,128)(2,1)S(1)} %get-tuple-element.45), kind=kOutput, calls=%fused_computation.108 | convolution fusion | flops 302383104 | bytes 5308416 | tf_op jit(solution)/shard_map/dot_general | solution.py:28
  51.1 3.3 %collective-permute-start = (f32[32,1664]{1,0:T(8,128)S(1)}, f32[32,1664]{1,0:T(8,128)S(1)}, u32[]{:S(2)}, u32[]{:S(2)}) collective-permute-start(f32[32,1664]{1,0:T(8,128)S(1)} %select_maximum_fusion.6), channel_id=1, source_target_pairs={{0,32},{32,0},{64,96},{96,64},{128,160},{160,128},{192,224},{224,1... | collective-permute-start | bytes 638984 | tf_op jit(solution)/shard_map/ppermute | solution.py:45
  54.4 1.1 collective-permute-done
  55.5 2.6 %collective-permute-start.3 = (f32[32,1664]{1,0:T(8,128)S(1)}, f32[32,1664]{1,0:T(8,128)S(1)}, u32[]{:S(2)}, u32[]{:S(2)}) collective-permute-start(f32[32,1664]{1,0:T(8,128)S(1)} %fusion.111), channel_id=1, source_target_pairs={{0,192},{32,224},{64,0},{96,32},{128,64},{160,96},{192,128},{224,1... | collective-permute-start | bytes 638984 | tf_op jit(solution)/shard_map/ppermute | solution.py:47
  58.0 0.5 collective-permute-start.2
  58.6 0.6 collective-permute-start.1
  59.2 7.6 %collective-permute-done.3 = f32[32,1664]{1,0:T(8,128)S(1)} collective-permute-done((f32[32,1664]{1,0:T(8,128)S(1)}, f32[32,1664]{1,0:T(8,128)S(1)}, u32[]{:S(2)}, u32[]{:S(2)}) %collective-permute-start.3) | collective-permute-done | bytes 213024 | tf_op jit(solution)/shard_map/ppermute | solution.py:47
  66.7 4.6 %collective-permute-done.1 = f32[32,1664]{1,0:T(8,128)S(1)} collective-permute-done((f32[32,1664]{1,0:T(8,128)S(1)}, f32[32,1664]{1,0:T(8,128)S(1)}, u32[]{:S(2)}, u32[]{:S(2)}) %collective-permute-start.1) | collective-permute-done | bytes 213024 | tf_op jit(solution)/shard_map/ppermute | solution.py:47
  71.3 0.2 fusion.96
  71.7 0.2 fusion.14
  72.0 3.9 %fusion.55 = f32[64,1536]{1,0:T(8,128)S(1)} fusion(bf16[1536,1536]{1,0:T(8,128)(2,1)} %copy-done, bf16[32,1536]{1,0:T(8,128)(2,1)S(1)} %get-tuple-element.51, bf16[32,1536]{1,0:T(8,128)(2,1)S(1)} %get-tuple-element.41), kind=kOutput, calls=%fused_computation.112 | convolution fusion | flops 302383104 | bytes 5308416 | tf_op jit(solution)/shard_map/dot_general | solution.py:28
  76.0 0.2 copy.42
  76.2 13.1 %all_to_all.74 = f32[32,1,1664]{2,1,0:T(1,128)S(1)} all-to-all(f32[32,1,1664]{2,1,0:T(1,128)S(1)} %copy.42), channel_id=1, replica_groups=mesh['animal'=8,'marker'=32] {'marker'}, dimensions={0} | all-to-all | bytes 425984 | tf_op jit(solution)/shard_map/all_to_all | solution.py:39
  89.5 14.9 %all_to_all.75 = f32[32,1,1664]{2,1,0:T(1,128)S(1)} all-to-all(f32[32,1,1664]{2,1,0:T(1,128)S(1)} %broadcast_in_dim.12), channel_id=1, replica_groups=mesh['animal'=8,'marker'=32] {'marker'}, dimensions={0} | all-to-all | bytes 425984 | tf_op jit(solution)/shard_map/all_to_all | solution.py:41
  104.7 0.2 fusion.117
  104.9 3.3 %fusion.59 = f32[64,1536]{1,0:T(8,128)S(1)} fusion(bf16[1536,1536]{1,0:T(8,128)(2,1)} %copy-done, bf16[32,1536]{1,0:T(8,128)(2,1)S(1)} %get-tuple-element.56, bf16[32,1536]{1,0:T(8,128)(2,1)S(1)} %get-tuple-element.39), kind=kOutput, calls=%fused_computation.116 | convolution fusion | flops 302383104 | bytes 5308416 | tf_op jit(solution)/shard_map/dot_general | solution.py:28
  108.3 3.2 %collective-permute-start.4 = (f32[32,1664]{1,0:T(8,128)S(1)}, f32[32,1664]{1,0:T(8,128)S(1)}, u32[]{:S(2)}, u32[]{:S(2)}) collective-permute-start(f32[32,1664]{1,0:T(8,128)S(1)} %select_maximum_fusion.4), channel_id=1, source_target_pairs={{0,32},{32,0},{64,96},{96,64},{128,160},{160,128},{192,224},{224,1... | collective-permute-start | bytes 638984 | tf_op jit(solution)/shard_map/ppermute | solution.py:45
  111.5 1.1 collective-permute-done.4
  112.7 0.6 collective-permute-start.6
  113.4 0.8 collective-permute-start.5
  114.2 5.0 %collective-permute-done.7 = f32[32,1664]{1,0:T(8,128)S(1)} collective-permute-done((f32[32,1664]{1,0:T(8,128)S(1)}, f32[32,1664]{1,0:T(8,128)S(1)}, u32[]{:S(2)}, u32[]{:S(2)}) %collective-permute-start.7) | collective-permute-done | bytes 213024 | tf_op jit(solution)/shard_map/ppermute | solution.py:47
  119.2 1.6 collective-permute-done.6
  120.8 5.2 %collective-permute-done.5 = f32[32,1664]{1,0:T(8,128)S(1)} collective-permute-done((f32[32,1664]{1,0:T(8,128)S(1)}, f32[32,1664]{1,0:T(8,128)S(1)}, u32[]{:S(2)}, u32[]{:S(2)}) %collective-permute-start.5) | collective-permute-done | bytes 213024 | tf_op jit(solution)/shard_map/ppermute | solution.py:47
  126.1 0.2 fusion.97
  126.3 0.2 reduce-precision_convert_fusion.3
  126.5 0.3 fusion.20
  126.8 3.9 %fusion.63 = f32[64,1536]{1,0:T(8,128)S(1)} fusion(bf16[1536,1536]{1,0:T(8,128)(2,1)} %copy-done, bf16[32,1536]{1,0:T(8,128)(2,1)S(1)} %get-tuple-element.50, bf16[32,1536]{1,0:T(8,128)(2,1)S(1)} %get-tuple-element.35), kind=kOutput, calls=%fused_computation.120 | convolution fusion | flops 302383104 | bytes 5308416 | tf_op jit(solution)/shard_map/dot_general | solution.py:28
  130.8 0.2 copy.45
  131.1 13.1 %all_to_all.76 = f32[32,1,1664]{2,1,0:T(1,128)S(1)} all-to-all(f32[32,1,1664]{2,1,0:T(1,128)S(1)} %copy.45), channel_id=1, replica_groups=mesh['animal'=8,'marker'=32] {'marker'}, dimensions={0} | all-to-all | bytes 425984 | tf_op jit(solution)/shard_map/all_to_all | solution.py:39
  144.4 14.9 %all_to_all.77 = f32[32,1,1664]{2,1,0:T(1,128)S(1)} all-to-all(f32[32,1,1664]{2,1,0:T(1,128)S(1)} %broadcast_in_dim.13), channel_id=1, replica_groups=mesh['animal'=8,'marker'=32] {'marker'}, dimensions={0} | all-to-all | bytes 425984 | tf_op jit(solution)/shard_map/all_to_all | solution.py:41
  159.8 3.3 %fusion.67 = f32[64,1536]{1,0:T(8,128)S(1)} fusion(bf16[1536,1536]{1,0:T(8,128)(2,1)} %copy-done, bf16[32,1536]{1,0:T(8,128)(2,1)S(1)} %get-tuple-element.55, bf16[32,1536]{1,0:T(8,128)(2,1)S(1)} %get-tuple-element.33), kind=kOutput, calls=%fused_computation.124 | convolution fusion | flops 302383104 | bytes 5308416 | tf_op jit(solution)/shard_map/dot_general | solution.py:28
  163.2 3.2 %collective-permute-start.8 = (f32[32,1664]{1,0:T(8,128)S(1)}, f32[32,1664]{1,0:T(8,128)S(1)}, u32[]{:S(2)}, u32[]{:S(2)}) collective-permute-start(f32[32,1664]{1,0:T(8,128)S(1)} %select_maximum_fusion.2), channel_id=1, source_target_pairs={{0,32},{32,0},{64,96},{96,64},{128,160},{160,128},{192,224},{224,1... | collective-permute-start | bytes 638984 | tf_op jit(solution)/shard_map/ppermute | solution.py:45
  166.4 1.1 collective-permute-done.8
  167.7 0.6 collective-permute-start.10
  168.3 0.8 collective-permute-start.9
  169.1 5.0 %collective-permute-done.11 = f32[32,1664]{1,0:T(8,128)S(1)} collective-permute-done((f32[32,1664]{1,0:T(8,128)S(1)}, f32[32,1664]{1,0:T(8,128)S(1)}, u32[]{:S(2)}, u32[]{:S(2)}) %collective-permute-start.11) | collective-permute-done | bytes 213024 | tf_op jit(solution)/shard_map/ppermute | solution.py:47
  174.1 1.4 collective-permute-done.10
  175.5 5.5 %collective-permute-done.9 = f32[32,1664]{1,0:T(8,128)S(1)} collective-permute-done((f32[32,1664]{1,0:T(8,128)S(1)}, f32[32,1664]{1,0:T(8,128)S(1)}, u32[]{:S(2)}, u32[]{:S(2)}) %collective-permute-start.9) | collective-permute-done | bytes 213024 | tf_op jit(solution)/shard_map/ppermute | solution.py:47
  181.0 0.2 fusion.98
  181.2 0.2 reduce-precision_convert_fusion.1
  181.4 0.2 fusion.26
  181.7 3.9 %fusion.71 = f32[64,1536]{1,0:T(8,128)S(1)} fusion(bf16[1536,1536]{1,0:T(8,128)(2,1)} %copy-done, bf16[32,1536]{1,0:T(8,128)(2,1)S(1)} %get-tuple-element.49, bf16[32,1536]{1,0:T(8,128)(2,1)S(1)} %get-tuple-element.28), kind=kOutput, calls=%fused_computation.128 | convolution fusion | flops 302383104 | bytes 5308416 | tf_op jit(solution)/shard_map/dot_general | solution.py:28
  185.7 0.2 copy.48
  185.9 13.1 %all_to_all.78 = f32[32,1,1664]{2,1,0:T(1,128)S(1)} all-to-all(f32[32,1,1664]{2,1,0:T(1,128)S(1)} %copy.48), channel_id=1, replica_groups=mesh['animal'=8,'marker'=32] {'marker'}, dimensions={0} | all-to-all | bytes 425984 | tf_op jit(solution)/shard_map/all_to_all | solution.py:39
  199.3 14.9 %all_to_all.79 = f32[32,1,1664]{2,1,0:T(1,128)S(1)} all-to-all(f32[32,1,1664]{2,1,0:T(1,128)S(1)} %broadcast_in_dim.14), channel_id=1, replica_groups=mesh['animal'=8,'marker'=32] {'marker'}, dimensions={0} | all-to-all | bytes 425984 | tf_op jit(solution)/shard_map/all_to_all | solution.py:41
  214.7 3.3 %fusion.75 = f32[64,1536]{1,0:T(8,128)S(1)} fusion(bf16[1536,1536]{1,0:T(8,128)(2,1)} %copy-done, bf16[32,1536]{1,0:T(8,128)(2,1)S(1)} %get-tuple-element.54, bf16[32,1536]{1,0:T(8,128)(2,1)S(1)} %get-tuple-element.26), kind=kOutput, calls=%fused_computation.132 | convolution fusion | flops 302383104 | bytes 5308416 | tf_op jit(solution)/shard_map/dot_general | solution.py:28
  218.1 3.2 %collective-permute-start.12 = (f32[32,1664]{1,0:T(8,128)S(1)}, f32[32,1664]{1,0:T(8,128)S(1)}, u32[]{:S(2)}, u32[]{:S(2)}) collective-permute-start(f32[32,1664]{1,0:T(8,128)S(1)} %select_maximum_fusion), channel_id=1, source_target_pairs={{0,32},{32,0},{64,96},{96,64},{128,160},{160,128},{192,224},{224,1... | collective-permute-start | bytes 638984 | tf_op jit(solution)/shard_map/ppermute | solution.py:45
  221.3 1.1 collective-permute-done.12
  222.6 0.6 collective-permute-start.14
  223.1 0.8 collective-permute-start.13
  224.0 5.0 %collective-permute-done.15 = f32[32,1664]{1,0:T(8,128)S(1)} collective-permute-done((f32[32,1664]{1,0:T(8,128)S(1)}, f32[32,1664]{1,0:T(8,128)S(1)}, u32[]{:S(2)}, u32[]{:S(2)}) %collective-permute-start.15) | collective-permute-done | bytes 213024 | tf_op jit(solution)/shard_map/ppermute | solution.py:47
  229.0 1.4 collective-permute-done.14
  230.4 5.5 %collective-permute-done.13 = f32[32,1664]{1,0:T(8,128)S(1)} collective-permute-done((f32[32,1664]{1,0:T(8,128)S(1)}, f32[32,1664]{1,0:T(8,128)S(1)}, u32[]{:S(2)}, u32[]{:S(2)}) %collective-permute-start.13) | collective-permute-done | bytes 213024 | tf_op jit(solution)/shard_map/ppermute | solution.py:47
  235.9 0.2 fusion.99
  236.1 1.0 fusion.32
  (66 shorter events, 4.4 us)
Async XLA Ops:
  6.9 2.1 copy-start
  32.5 39.1 %copy-start.1 = (f32[32,1536]{1,0:T(8,128)S(1)}, f32[32,1536]{1,0:T(8,128)}, u32[]{:S(2)}) copy-start(f32[32,1536]{1,0:T(8,128)} %param.7) | copy-start | bytes 589828
  32.5 39.1 %copy-start.2 = (f32[1536]{0:T(1024)S(1)}, f32[1536]{0:T(1024)}, u32[]{:S(2)}) copy-start(f32[1536]{0:T(1024)} %param.6) | copy-start | bytes 18436
  51.1 4.4 %collective-permute-start = (f32[32,1664]{1,0:T(8,128)S(1)}, f32[32,1664]{1,0:T(8,128)S(1)}, u32[]{:S(2)}, u32[]{:S(2)}) collective-permute-start(f32[32,1664]{1,0:T(8,128)S(1)} %select_maximum_fusion.6), channel_id=1, source_target_pairs={{0,32},{32,0},{64,96},{96,64},{128,160},{160,128},{192,224},{224,1... | collective-permute-start | bytes 638984 | tf_op jit(solution)/shard_map/ppermute | solution.py:45
  55.5 11.2 %collective-permute-start.3 = (f32[32,1664]{1,0:T(8,128)S(1)}, f32[32,1664]{1,0:T(8,128)S(1)}, u32[]{:S(2)}, u32[]{:S(2)}) collective-permute-start(f32[32,1664]{1,0:T(8,128)S(1)} %fusion.111), channel_id=1, source_target_pairs={{0,192},{32,224},{64,0},{96,32},{128,64},{160,96},{192,128},{224,1... | collective-permute-start | bytes 638984 | tf_op jit(solution)/shard_map/ppermute | solution.py:47
  58.0 8.7 %collective-permute-start.2 = (f32[32,1664]{1,0:T(8,128)S(1)}, f32[32,1664]{1,0:T(8,128)S(1)}, u32[]{:S(2)}, u32[]{:S(2)}) collective-permute-start(f32[32,1664]{1,0:T(8,128)S(1)} %fusion.111), channel_id=1, source_target_pairs={{0,128},{32,160},{64,192},{96,224},{128,0},{160,32},{192,64},{224,... | collective-permute-start | bytes 638984 | tf_op jit(solution)/shard_map/ppermute | solution.py:47
  58.6 12.7 %collective-permute-start.1 = (f32[32,1664]{1,0:T(8,128)S(1)}, f32[32,1664]{1,0:T(8,128)S(1)}, u32[]{:S(2)}, u32[]{:S(2)}) collective-permute-start(f32[32,1664]{1,0:T(8,128)S(1)} %fusion.111), channel_id=1, source_target_pairs={{0,64},{32,96},{64,128},{96,160},{128,192},{160,224},{192,0},{224,... | collective-permute-start | bytes 638984 | tf_op jit(solution)/shard_map/ppermute | solution.py:47
  108.3 4.3 %collective-permute-start.4 = (f32[32,1664]{1,0:T(8,128)S(1)}, f32[32,1664]{1,0:T(8,128)S(1)}, u32[]{:S(2)}, u32[]{:S(2)}) collective-permute-start(f32[32,1664]{1,0:T(8,128)S(1)} %select_maximum_fusion.4), channel_id=1, source_target_pairs={{0,32},{32,0},{64,96},{96,64},{128,160},{160,128},{192,224},{224,1... | collective-permute-start | bytes 638984 | tf_op jit(solution)/shard_map/ppermute | solution.py:45
  112.7 6.5 %collective-permute-start.7 = (f32[32,1664]{1,0:T(8,128)S(1)}, f32[32,1664]{1,0:T(8,128)S(1)}, u32[]{:S(2)}, u32[]{:S(2)}) collective-permute-start(f32[32,1664]{1,0:T(8,128)S(1)} %fusion.112), channel_id=1, source_target_pairs={{0,192},{32,224},{64,0},{96,32},{128,64},{160,96},{192,128},{224,1... | collective-permute-start | bytes 638984 | tf_op jit(solution)/shard_map/ppermute | solution.py:47
  112.7 8.1 %collective-permute-start.6 = (f32[32,1664]{1,0:T(8,128)S(1)}, f32[32,1664]{1,0:T(8,128)S(1)}, u32[]{:S(2)}, u32[]{:S(2)}) collective-permute-start(f32[32,1664]{1,0:T(8,128)S(1)} %fusion.112), channel_id=1, source_target_pairs={{0,128},{32,160},{64,192},{96,224},{128,0},{160,32},{192,64},{224,... | collective-permute-start | bytes 638984 | tf_op jit(solution)/shard_map/ppermute | solution.py:47
  113.4 12.7 %collective-permute-start.5 = (f32[32,1664]{1,0:T(8,128)S(1)}, f32[32,1664]{1,0:T(8,128)S(1)}, u32[]{:S(2)}, u32[]{:S(2)}) collective-permute-start(f32[32,1664]{1,0:T(8,128)S(1)} %fusion.112), channel_id=1, source_target_pairs={{0,64},{32,96},{64,128},{96,160},{128,192},{160,224},{192,0},{224,... | collective-permute-start | bytes 638984 | tf_op jit(solution)/shard_map/ppermute | solution.py:47
  163.2 4.3 %collective-permute-start.8 = (f32[32,1664]{1,0:T(8,128)S(1)}, f32[32,1664]{1,0:T(8,128)S(1)}, u32[]{:S(2)}, u32[]{:S(2)}) collective-permute-start(f32[32,1664]{1,0:T(8,128)S(1)} %select_maximum_fusion.2), channel_id=1, source_target_pairs={{0,32},{32,0},{64,96},{96,64},{128,160},{160,128},{192,224},{224,1... | collective-permute-start | bytes 638984 | tf_op jit(solution)/shard_map/ppermute | solution.py:45
  167.6 6.5 %collective-permute-start.11 = (f32[32,1664]{1,0:T(8,128)S(1)}, f32[32,1664]{1,0:T(8,128)S(1)}, u32[]{:S(2)}, u32[]{:S(2)}) collective-permute-start(f32[32,1664]{1,0:T(8,128)S(1)} %fusion.113), channel_id=1, source_target_pairs={{0,192},{32,224},{64,0},{96,32},{128,64},{160,96},{192,128},{224,1... | collective-permute-start | bytes 638984 | tf_op jit(solution)/shard_map/ppermute | solution.py:47
  167.7 7.8 %collective-permute-start.10 = (f32[32,1664]{1,0:T(8,128)S(1)}, f32[32,1664]{1,0:T(8,128)S(1)}, u32[]{:S(2)}, u32[]{:S(2)}) collective-permute-start(f32[32,1664]{1,0:T(8,128)S(1)} %fusion.113), channel_id=1, source_target_pairs={{0,128},{32,160},{64,192},{96,224},{128,0},{160,32},{192,64},{224,... | collective-permute-start | bytes 638984 | tf_op jit(solution)/shard_map/ppermute | solution.py:47
  168.3 12.7 %collective-permute-start.9 = (f32[32,1664]{1,0:T(8,128)S(1)}, f32[32,1664]{1,0:T(8,128)S(1)}, u32[]{:S(2)}, u32[]{:S(2)}) collective-permute-start(f32[32,1664]{1,0:T(8,128)S(1)} %fusion.113), channel_id=1, source_target_pairs={{0,64},{32,96},{64,128},{96,160},{128,192},{160,224},{192,0},{224,... | collective-permute-start | bytes 638984 | tf_op jit(solution)/shard_map/ppermute | solution.py:47
  218.1 4.3 %collective-permute-start.12 = (f32[32,1664]{1,0:T(8,128)S(1)}, f32[32,1664]{1,0:T(8,128)S(1)}, u32[]{:S(2)}, u32[]{:S(2)}) collective-permute-start(f32[32,1664]{1,0:T(8,128)S(1)} %select_maximum_fusion), channel_id=1, source_target_pairs={{0,32},{32,0},{64,96},{96,64},{128,160},{160,128},{192,224},{224,1... | collective-permute-start | bytes 638984 | tf_op jit(solution)/shard_map/ppermute | solution.py:45
  222.4 6.5 %collective-permute-start.15 = (f32[32,1664]{1,0:T(8,128)S(1)}, f32[32,1664]{1,0:T(8,128)S(1)}, u32[]{:S(2)}, u32[]{:S(2)}) collective-permute-start(f32[32,1664]{1,0:T(8,128)S(1)} %fusion.114), channel_id=1, source_target_pairs={{0,192},{32,224},{64,0},{96,32},{128,64},{160,96},{192,128},{224,1... | collective-permute-start | bytes 638984 | tf_op jit(solution)/shard_map/ppermute | solution.py:47
  222.6 7.8 %collective-permute-start.14 = (f32[32,1664]{1,0:T(8,128)S(1)}, f32[32,1664]{1,0:T(8,128)S(1)}, u32[]{:S(2)}, u32[]{:S(2)}) collective-permute-start(f32[32,1664]{1,0:T(8,128)S(1)} %fusion.114), channel_id=1, source_target_pairs={{0,128},{32,160},{64,192},{96,224},{128,0},{160,32},{192,64},{224,... | collective-permute-start | bytes 638984 | tf_op jit(solution)/shard_map/ppermute | solution.py:47
  223.1 12.7 %collective-permute-start.13 = (f32[32,1664]{1,0:T(8,128)S(1)}, f32[32,1664]{1,0:T(8,128)S(1)}, u32[]{:S(2)}, u32[]{:S(2)}) collective-permute-start(f32[32,1664]{1,0:T(8,128)S(1)} %fusion.114), channel_id=1, source_target_pairs={{0,64},{32,96},{64,128},{96,160},{128,192},{160,224},{192,0},{224,... | collective-permute-start | bytes 638984 | tf_op jit(solution)/shard_map/ppermute | solution.py:47

commit v2 on v0

v2 whole, which is shorter than its diff:
```python
import functools

import jax
import jax.numpy as jnp
from jax import lax
from jax.experimental import pallas as pl
from jax.experimental.pallas import tpu as pltpu
from jax.sharding import PartitionSpec as P

ITERS = 4
CORES = 2
EXTRA = 128
BLOCK = 256
AHEAD = 2
MIB = 1024 * 1024
VMEM = pl.BlockSpec(memory_space=pltpu.VMEM)
ANY = pl.BlockSpec(memory_space=pl.ANY)


def half_slices(half):
    core = lax.axis_index("animal") % CORES
    return pl.ds(core * half, half), pl.ds((1 - core) * half, half)


def lanes(*columns):
    at = lax.broadcasted_iota(jnp.int32, (columns[0].shape[0], EXTRA), 1)
    out = jnp.zeros(at.shape, jnp.float32)
    for i, column in enumerate(columns):
        out = jnp.where(at == i, column, out)
    return out


def put_terms(v, terms_ref):
    rows = v.shape[0]
    hi = v.astype(jnp.bfloat16)
    terms_ref[:rows] = hi
    terms_ref[rows:] = (v - hi.astype(jnp.float32)).astype(jnp.bfloat16)


def row_sum(v):
    return jnp.sum(v, axis=1, keepdims=True)


def folded(both):
    half = both.shape[0] // 2
    return both[:half] + both[half:]


def row_product(terms_ref, block):
    return folded(
        lax.dot_general(terms_ref[...], block, (((1,), (1,)), ((), ())), preferred_element_type=jnp.float32)
    )


def col_product(terms_ref, block):
    return folded(jnp.dot(terms_ref[...], block, preferred_element_type=jnp.float32))


def blocks(extent):
    return [pl.ds(i * BLOCK, BLOCK) for i in range(extent // BLOCK)]


def first_kernel(
    geno_ref, freq_ref, shrink_ref, right_ref,
    coded_ref, freq_out, shrink_out, residual_out, scaled_out, part_ref,
    stage, right, freq_line, shrink_line, terms_ref, geno_sems, small_sems,
):
    animals = coded_ref.shape[0]
    half = right_ref.shape[0] // 2
    pairs = ((right_ref, right), (freq_ref, freq_line), (shrink_ref, shrink_line))
    small = [pltpu.make_async_copy(src, dst, small_sems.at[i]) for i, (src, dst) in enumerate(pairs)]
    spots = blocks(animals)
    copies = [
        pltpu.make_async_copy(geno_ref.at[at, :], stage.at[at, :], geno_sems.at[i]) for i, at in enumerate(spots)
    ]
    for copy in small + copies[:AHEAD]:
        copy.start()
    for copy in small:
        copy.wait()
    freq = freq_line[...].reshape(1, -1)
    shrink = shrink_line[...].reshape(1, -1)
    freq_out[...] = freq
    shrink_out[...] = shrink
    mine, other = half_slices(half)
    precond = 2.0 * freq * (1.0 - freq) + shrink
    residual_out[:half] = right[mine, :]
    residual_out[half:] = right[other, :]
    scaled_out[...] = residual_out[...] / precond
    residual = right[...]
    scaled = residual / precond
    extra = lanes(row_sum(residual * scaled), row_sum(shrink * scaled * scaled))
    part_ref[:, :, animals:] = extra[:, None, :]
    put_terms(scaled, terms_ref)
    offset = row_sum(2.0 * freq * scaled)
    for i, at in enumerate(spots):
        copies[i].wait()
        if i + AHEAD < len(copies):
            copies[i + AHEAD].start()
        block = stage[at, :].astype(jnp.bfloat16)
        coded_ref[at, :] = block
        part_ref[:, :, at] = (row_product(terms_ref, block) - offset)[:, None, :]


def spread_kernel(got_ref, out_ref):
    out_ref[...] = jnp.broadcast_to(jnp.sum(got_ref[...], axis=0, keepdims=True), out_ref.shape)


def add_kernel(*refs):
    *ins, out_ref = refs
    total = ins[0][...]
    for ref in ins[1:]:
        total += ref[...]
    out_ref[...] = total


def half_columns(vec, coded_ref, freq_ref, out_ref, terms_ref):
    width = coded_ref.shape[1]
    put_terms(vec, terms_ref)
    row_total = row_sum(vec)
    for at in blocks(width):
        out_ref[:, at] = col_product(terms_ref, coded_ref[:, at]) - 2.0 * freq_ref[:, at] * row_total
    out_ref[:, width:] = lanes(row_sum(vec * vec))


def other_columns(first, total_ref, freq_ref, coded_ref, *refs):
    *old, out_ref, terms_ref = refs
    animals = coded_ref.shape[0]
    half = out_ref.shape[0]
    total = total_ref[half_slices(half)[1], 0, :]
    vec = total[:, :animals]
    if not first:
        rows_ref, kept_ref = old
        beta = total[:, animals : animals + 1] / kept_ref[half:, :1]
        vec += beta * rows_ref[half:, :]
    half_columns(vec, coded_ref, freq_ref, out_ref, terms_ref)


def mine_columns(first, total_ref, freq_ref, coded_ref, scaled_ref, *refs):
    *old, direction_out, rows_out, kept_out, out_ref, terms_ref = refs
    animals = coded_ref.shape[0]
    half = out_ref.shape[0]
    for local, at in zip((slice(0, half), slice(half, None)), half_slices(half)):
        total = total_ref[at, 0, :]
        vec = total[:, :animals]
        rho, square, cross = (total[:, animals + i : animals + i + 1] for i in range(3))
        if first:
            direction_out[local] = scaled_ref[local]
            kept_out[local] = lanes(rho, square)
        else:
            direction_ref, rows_ref, kept_ref = old
            beta = rho / kept_ref[local, :1]
            vec += beta * rows_ref[local]
            direction_out[local] = scaled_ref[local] + beta * direction_ref[local]
            kept_out[local] = lanes(rho, square + beta * (2.0 * cross + beta * kept_ref[local, 1:2]))
        rows_out[local] = vec
    half_columns(rows_out[:half], coded_ref, freq_ref, out_ref, terms_ref)


def update(inv_count, local, total_ref, shrink_ref, direction_ref, residual_ref, kept_ref, solution_ref=None):
    width = direction_ref.shape[1]
    direction = direction_ref[local]
    image = total_ref[:, :width] * inv_count + shrink_ref[...] * direction
    curve = total_ref[:, width : width + 1] * inv_count + kept_ref[local, 1:2]
    step = kept_ref[local, :1] / curve
    moved = step * direction
    if solution_ref is not None:
        moved += solution_ref[local]
    return moved, residual_ref[local] - step * image, direction


def half_rows(inv_count, local, state, freq_ref, coded_ref, solution_out, residual_out, scaled_out, write, terms_ref):
    animals = coded_ref.shape[0]
    solution, residual, direction = update(inv_count, local, *state)
    freq, shrink = freq_ref[...], state[1][...]
    scaled = residual / (2.0 * freq * (1.0 - freq) + shrink)
    solution_out[...] = solution
    residual_out[...] = residual
    scaled_out[...] = scaled
    put_terms(scaled, terms_ref)
    weighted = shrink * scaled
    offset = row_sum(2.0 * freq * scaled)
    for at in blocks(animals):
        write(at, row_product(terms_ref, coded_ref[at, :]) - offset)
    write(
        pl.ds(animals, EXTRA),
        lanes(row_sum(residual * scaled), row_sum(weighted * scaled), row_sum(weighted * direction)),
    )


def mine_rows(inv_count, freq_ref, coded_ref, *refs):
    *state, solution_out, residual_out, scaled_out, part_ref, terms_ref = refs
    half = part_ref.shape[0]

    def write(at, value):
        part_ref[:, :, at] = value[:, None, :]

    half_rows(
        inv_count, slice(0, half), state, freq_ref, coded_ref,
        solution_out, residual_out, scaled_out, write, terms_ref,
    )


def other_rows(inv_count, freq_ref, coded_ref, solution_ref, residual_ref, scaled_ref, half_ref, *refs):
    *state, solution_out, residual_out, scaled_out, part_ref, terms_ref = refs
    half = half_ref.shape[0]
    mine, other = half_slices(half)
    part_ref[mine] = half_ref[...]
    solution_out[:half] = solution_ref[...]
    residual_out[:half] = residual_ref[...]
    scaled_out[:half] = scaled_ref[...]

    def write(at, value):
        part_ref[other, :, at] = value[:, None, :]

    top = slice(half, None)
    half_rows(
        inv_count, top, state, freq_ref, coded_ref,
        solution_out.at[top], residual_out.at[top], scaled_out.at[top], write, terms_ref,
    )


def last_kernel(inv_count, mine_ref, other_ref, shrink_ref, *refs):
    *state, solution_out, residual_out = refs
    half = mine_ref.shape[0]
    for local, at, total_ref in zip((slice(0, half), slice(half, None)), half_slices(half), (mine_ref, other_ref)):
        solution_out[at, :], residual_out[at, :], _ = update(inv_count, local, total_ref, shrink_ref, *state)


def body(genotype, allele_freq, shrink, right_side):
    xs = lax.axis_size("animal") // CORES
    inv_count = 1.0 / (genotype.shape[0] * lax.axis_size("animal"))
    animals, width = genotype.shape
    rhs = right_side.shape[0]
    half = rhs // 2

    def f32(*shape):
        return jax.ShapeDtypeStruct(shape, jnp.float32)

    def call(kernel, name, out_shape, args, scratch=(), mib=6):
        return pl.pallas_call(
            kernel,
            in_specs=[VMEM] * len(args),
            out_specs=jax.tree.map(lambda _: VMEM, out_shape),
            out_shape=out_shape,
            scratch_shapes=list(scratch),
            compiler_params=pltpu.CompilerParams(vmem_limit_bytes=mib * MIB),
            name=name,
        )(*args)

    def terms(n):
        return [pltpu.VMEM((rhs, n), jnp.bfloat16)]

    vec, halves, kept_shape = f32(rhs, width), f32(half, width), f32(rhs, EXTRA)
    ext, own = f32(rhs, 1, animals + EXTRA), f32(half, width + EXTRA)
    line = f32(1, width)

    coded, freq, shrink, residual, scaled, part = pl.pallas_call(
        first_kernel,
        in_specs=[ANY] * 4,
        out_specs=[VMEM] * 6,
        out_shape=[pltpu.VMEM((animals, width), jnp.bfloat16), line, line, vec, vec, ext],
        scratch_shapes=[
            pltpu.VMEM((animals, width), jnp.float32),
            pltpu.VMEM((rhs, width), jnp.float32),
            pltpu.VMEM((width,), jnp.float32),
            pltpu.VMEM((width,), jnp.float32),
            pltpu.VMEM((2 * rhs, width), jnp.bfloat16),
            pltpu.SemaphoreType.DMA((animals // BLOCK,)),
            pltpu.SemaphoreType.DMA((3,)),
        ],
        compiler_params=pltpu.CompilerParams(vmem_limit_bytes=32 * MIB),
        name="first_rows",
    )(*[pltpu.with_memory_space_constraint(v, pltpu.HBM) for v in (genotype, allele_freq, shrink, right_side)])
    coded = pltpu.with_memory_space_constraint(coded, pltpu.VMEM)

    def marker_sum(part):
        got = lax.all_to_all(part, "marker", 0, 0, tiled=True)
        spread = call(spread_kernel, "spread", f32(*got.shape), [got])
        return lax.all_to_all(spread, "marker", 0, 0, tiled=True)

    swap = [(x * CORES + c, x * CORES + 1 - c) for x in range(xs) for c in range(CORES)]

    def to_other(v):
        return lax.ppermute(v, "animal", swap)

    def shift(v, d):
        return lax.ppermute(
            v, "animal", [(x * CORES + c, (x + d) % xs * CORES + c) for x in range(xs) for c in range(CORES)]
        )

    solution = ()
    old = []
    for step in range(ITERS):
        total = marker_sum(part)
        first = step == 0
        shared = [total, freq, coded]
        other = call(
            functools.partial(other_columns, first), "other_columns", own, shared + old[1:], terms(animals)
        )
        other = to_other(other)
        *old, mine = call(
            functools.partial(mine_columns, first), "mine_columns",
            [vec, f32(rhs, animals), kept_shape, own], shared + [scaled] + old, terms(animals),
        )
        direction, _, kept = old
        mine = call(add_kernel, "add", own, [mine, other])
        mine = call(add_kernel, "add", own, [mine] + [shift(mine, d) for d in range(1, xs)])
        other = to_other(mine)
        state = [shrink, direction, residual, kept, *solution]
        if step == ITERS - 1:
            return tuple(call(functools.partial(last_kernel, inv_count), "last", [vec, vec], [mine, other] + state))
        half_part = f32(half, 1, animals + EXTRA)
        outs = call(
            functools.partial(mine_rows, inv_count), "mine_rows", [halves, halves, halves, half_part],
            [freq, coded, mine] + state, terms(width),
        )
        *solution, residual, scaled, part = call(
            functools.partial(other_rows, inv_count), "other_rows", [vec, vec, vec, ext],
            [freq, coded, *outs, other] + state, terms(width),
        )


def solution(mesh):
    placed = (P("animal", "marker"), P("marker"), P("marker"), P(None, "marker"))
    return jax.shard_map(
        body,
        mesh=mesh,
        in_specs=placed,
        out_specs=(P(None, "marker"), P(None, "marker")),
        check_vma=False,
    )
```

time: 1430 us -> 203 us (0.14); the launches traced: 1410 us -> 202 us
  waiting for transfers between devices: 814 us -> 31.3 us
  blocking collectives: 481 us -> 122 us
  matrix products: 87.8 us -> 0 us
  Pallas kernels: 0 us -> 24.8 us
  starting transfers between devices: 0.33 us -> 22.9 us
    psum x8 -> x0, waiting for transfers between devices: 814 us -> none  [the longest x4 623 us: body(): row_values = lax.psum(partial_value, 'marker')]
    psum x11 -> x0, blocking collectives: 481 us -> none  [the longest x7 414 us: inner(): return lax.psum(local_dot, 'marker')]
    all_to_all x0 -> x8, blocking collectives: none -> 122 us  [the longest x4 62.2 us: marker_sum(): got = lax.all_to_all(part, 'marker', 0, 0, tiled=True)]
    dot_general x8 -> x0, matrix products: 87.8 us -> none  [the longest x4 48 us: body(): lax.dot_general(direction, genotype, (((1,), (1,)), ((), ())), precision=...]
    ppermute x0 -> x20, waiting for transfers between devices: none -> 31.3 us  [the longest x12 30.3 us: shift(): lax.ppermute(v, 'animal', [(x * CORES + c, (x + d) % xs * CORES + c) for...]
    pallas_call x0 -> x28, Pallas kernels: none -> 24.8 us  [the longest x27 19 us: call(): pl.pallas_call(kernel, in_specs=[VMEM] * len(args), out_specs=jax.tree.ma...]
    ppermute x0 -> x20, starting transfers between devices: none -> 22.9 us  [the longest x8 14.4 us: to_other(): return lax.ppermute(v, 'animal', swap)]
  transfers between devices with their start and end apart: 8 -> 20, of which waited for: 8 -> 14; matrix products, arithmetic and copies ran while one was open for 0% -> 0% of each run, Pallas kernels for 0% -> 4%
where the time goes in v2:
time: 203 us; the launch traced here: 202 us
  blocking collectives  122 us (60%)
  waiting for transfers between devices  31.3 us (15%)
  Pallas kernels  24.8 us (12%)
  starting transfers between devices  22.9 us (11%)
    all_to_all x4, blocking collectives, marker_sum(): got = lax.all_to_all(part, 'marker', 0, 0, tiled=True)  62.2 us
    all_to_all x4, blocking collectives, marker_sum(): return lax.all_to_all(spread, 'marker', 0, 0, tiled=True)  60.1 us
    ppermute x12, waiting for transfers between devices, shift(): lax.ppermute(v, 'animal', [(x * CORES + c, (x + d) % xs * CORES + c) for...  30.3 us
    pallas_call x27, Pallas kernels, call(): pl.pallas_call(kernel, in_specs=[VMEM] * len(args), out_specs=jax.tree.ma...  19 us
    ppermute x8, starting transfers between devices, to_other(): return lax.ppermute(v, 'animal', swap)  14.4 us
    ppermute x12, starting transfers between devices, shift(): lax.ppermute(v, 'animal', [(x * CORES + c, (x + d) % xs * CORES + c) for...  8.5 us
    pallas_call x1, Pallas kernels, body(): pl.pallas_call(first_kernel, in_specs=[ANY] * 4, out_specs=[VMEM] * 6, ou...  5.79 us
  transfers between devices with their start and end apart: 20, of which 14 were waited for; matrix products, arithmetic and copies ran while one was open for 0% of the time, Pallas kernels for 4%

profile of v2, /device:TPU:1, one launch (start us, length us, event | category | flops | bytes accessed | tf_op | source)
XLA Modules:
  0.0 202.1 jit_solution(1870291317072889362)
XLA Ops:
  0.6 5.8 %first_rows.1 = (bf16[1536,1536]{1,0:T(8,128)(2,1)S(1)}, f32[1,1536]{1,0:T(1,128)S(1)}, f32[1,1536]{1,0:T(1,128)S(1)}, f32[32,1536]{1,0:T(8,128)S(1)}, f32[32,15...) custom-call(f32[1536,1536]{1,0:T(8,128)} %geno_ref.1, f32[1536]{0:T(1024)} %freq_ref.1, f32[1536]{0:T(1024)} %shrink_ref.1, ...), custom_call_target="tpu_custom_call" | custom-call | tf_op jit(solution)/shard_map/first_rows/pallas_call | solution.py:257
  6.4 21.3 %all_to_all.40.got_ref = f32[32,1,1664]{2,1,0:T(1,128)S(1)} all-to-all(f32[32,1,1664]{2,1,0:T(1,128)S(1)} %get-tuple-element.49), channel_id=1, replica_groups=mesh['animal'=8,'marker'=32] {'marker'}, dimensions={0} | all-to-all | bytes 425984 | tf_op jit(solution)/shard_map/all_to_all | solution.py:277
  27.8 0.1 spread.4
  27.9 14.8 %all_to_all.41.total_ref = f32[32,1,1664]{2,1,0:T(1,128)S(1)} all-to-all(f32[32,1,1664]{2,1,0:T(1,128)S(1)} %spread.4), channel_id=1, replica_groups=mesh['animal'=8,'marker'=32] {'marker'}, dimensions={0} | all-to-all | bytes 425984 | tf_op jit(solution)/shard_map/all_to_all | solution.py:279
  42.7 0.9 other_columns.4
  43.6 3.2 %collective-permute-start = (f32[16,1664]{1,0:T(8,128)S(1)}, f32[16,1664]{1,0:T(8,128)S(1)}, u32[]{:S(2)}, u32[]{:S(2)}) collective-permute-start(f32[16,1664]{1,0:T(8,128)S(1)} %other_columns.4), channel_id=1, source_target_pairs={{0,32},{32,0},{64,96},{96,64},{128,160},{160,128},{192,224},{224,1... | collective-permute-start | bytes 319496 | tf_op jit(solution)/shard_map/ppermute | solution.py:284
  46.8 0.9 mine_columns.4
  47.7 0.1 collective-permute-done.refs_1_
  47.8 2.6 %collective-permute-start.3 = (f32[16,1664]{1,0:T(8,128)S(1)}, f32[16,1664]{1,0:T(8,128)S(1)}, u32[]{:S(2)}, u32[]{:S(2)}) collective-permute-start(f32[16,1664]{1,0:T(8,128)S(1)} %add.8.refs_0_), channel_id=1, source_target_pairs={{0,192},{32,224},{64,0},{96,32},{128,64},{160,96},{192,128},{224,1... | collective-permute-start | bytes 319496 | tf_op jit(solution)/shard_map/ppermute | solution.py:287
  50.4 0.5 collective-permute-start.2
  50.9 0.6 collective-permute-start.1
  51.5 3.0 %collective-permute-done.3.refs_3_ = f32[16,1664]{1,0:T(8,128)S(1)} collective-permute-done((f32[16,1664]{1,0:T(8,128)S(1)}, f32[16,1664]{1,0:T(8,128)S(1)}, u32[]{:S(2)}, u32[]{:S(2)}) %collective-permute-start.3) | collective-permute-done | bytes 106528 | tf_op jit(solution)/shard_map/ppermute | solution.py:287
  54.5 1.2 collective-permute-done.2.refs_2_
  55.7 3.2 %collective-permute-done.1.refs_1_ = f32[16,1664]{1,0:T(8,128)S(1)} collective-permute-done((f32[16,1664]{1,0:T(8,128)S(1)}, f32[16,1664]{1,0:T(8,128)S(1)}, u32[]{:S(2)}, u32[]{:S(2)}) %collective-permute-start.1) | collective-permute-done | bytes 106528 | tf_op jit(solution)/shard_map/ppermute | solution.py:287
  59.0 0.7 collective-permute-start.4
  59.7 1.6 mine_rows.3
  61.2 0.0 collective-permute-done.4.refs_0_
  61.2 1.6 other_rows.3
  62.8 13.5 %all_to_all.42.got_ref = f32[32,1,1664]{2,1,0:T(1,128)S(1)} all-to-all(f32[32,1,1664]{2,1,0:T(1,128)S(1)} %get-tuple-element.60), channel_id=1, replica_groups=mesh['animal'=8,'marker'=32] {'marker'}, dimensions={0} | all-to-all | bytes 425984 | tf_op jit(solution)/shard_map/all_to_all | solution.py:277
  76.3 0.1 spread.5
  76.5 15.1 %all_to_all.43.total_ref = f32[32,1,1664]{2,1,0:T(1,128)S(1)} all-to-all(f32[32,1,1664]{2,1,0:T(1,128)S(1)} %spread.5), channel_id=1, replica_groups=mesh['animal'=8,'marker'=32] {'marker'}, dimensions={0} | all-to-all | bytes 425984 | tf_op jit(solution)/shard_map/all_to_all | solution.py:279
  91.6 0.9 other_columns.5
  92.5 2.9 %collective-permute-start.5 = (f32[16,1664]{1,0:T(8,128)S(1)}, f32[16,1664]{1,0:T(8,128)S(1)}, u32[]{:S(2)}, u32[]{:S(2)}) collective-permute-start(f32[16,1664]{1,0:T(8,128)S(1)} %other_columns.5), channel_id=1, source_target_pairs={{0,32},{32,0},{64,96},{96,64},{128,160},{160,128},{192,224},{224,1... | collective-permute-start | bytes 319496 | tf_op jit(solution)/shard_map/ppermute | solution.py:284
  95.5 0.9 mine_columns.5
  96.4 0.5 collective-permute-start.8
  97.0 0.5 collective-permute-start.7
  97.5 0.7 collective-permute-start.6
  98.2 2.7 %collective-permute-done.8.refs_3_ = f32[16,1664]{1,0:T(8,128)S(1)} collective-permute-done((f32[16,1664]{1,0:T(8,128)S(1)}, f32[16,1664]{1,0:T(8,128)S(1)}, u32[]{:S(2)}, u32[]{:S(2)}) %collective-permute-start.8) | collective-permute-done | bytes 106528 | tf_op jit(solution)/shard_map/ppermute | solution.py:287
  100.9 1.5 collective-permute-done.7.refs_2_
  102.4 3.3 %collective-permute-done.6.refs_1_ = f32[16,1664]{1,0:T(8,128)S(1)} collective-permute-done((f32[16,1664]{1,0:T(8,128)S(1)}, f32[16,1664]{1,0:T(8,128)S(1)}, u32[]{:S(2)}, u32[]{:S(2)}) %collective-permute-start.6) | collective-permute-done | bytes 106528 | tf_op jit(solution)/shard_map/ppermute | solution.py:287
  105.7 0.6 collective-permute-start.9
  106.3 1.6 mine_rows.4
  107.8 1.6 other_rows.4
  109.4 13.7 %all_to_all.44.got_ref = f32[32,1,1664]{2,1,0:T(1,128)S(1)} all-to-all(f32[32,1,1664]{2,1,0:T(1,128)S(1)} %get-tuple-element.72), channel_id=1, replica_groups=mesh['animal'=8,'marker'=32] {'marker'}, dimensions={0} | all-to-all | bytes 425984 | tf_op jit(solution)/shard_map/all_to_all | solution.py:277
  123.1 0.1 spread.6
  123.2 15.1 %all_to_all.45.total_ref = f32[32,1,1664]{2,1,0:T(1,128)S(1)} all-to-all(f32[32,1,1664]{2,1,0:T(1,128)S(1)} %spread.6), channel_id=1, replica_groups=mesh['animal'=8,'marker'=32] {'marker'}, dimensions={0} | all-to-all | bytes 425984 | tf_op jit(solution)/shard_map/all_to_all | solution.py:279
  138.3 0.9 other_columns.6
  139.3 2.9 %collective-permute-start.10 = (f32[16,1664]{1,0:T(8,128)S(1)}, f32[16,1664]{1,0:T(8,128)S(1)}, u32[]{:S(2)}, u32[]{:S(2)}) collective-permute-start(f32[16,1664]{1,0:T(8,128)S(1)} %other_columns.6), channel_id=1, source_target_pairs={{0,32},{32,0},{64,96},{96,64},{128,160},{160,128},{192,224},{224,1... | collective-permute-start | bytes 319496 | tf_op jit(solution)/shard_map/ppermute | solution.py:284
  142.2 0.9 mine_columns.6
  143.2 0.0 collective-permute-done.10.refs_1_
  143.2 0.7 collective-permute-start.13
  143.9 0.2 collective-permute-start.12
  144.1 0.7 collective-permute-start.11
  144.7 2.7 %collective-permute-done.13.refs_3_ = f32[16,1664]{1,0:T(8,128)S(1)} collective-permute-done((f32[16,1664]{1,0:T(8,128)S(1)}, f32[16,1664]{1,0:T(8,128)S(1)}, u32[]{:S(2)}, u32[]{:S(2)}) %collective-permute-start.13) | collective-permute-done | bytes 106528 | tf_op jit(solution)/shard_map/ppermute | solution.py:287
  147.5 1.8 collective-permute-done.12.refs_2_
  149.3 3.3 %collective-permute-done.11.refs_1_ = f32[16,1664]{1,0:T(8,128)S(1)} collective-permute-done((f32[16,1664]{1,0:T(8,128)S(1)}, f32[16,1664]{1,0:T(8,128)S(1)}, u32[]{:S(2)}, u32[]{:S(2)}) %collective-permute-start.11) | collective-permute-done | bytes 106528 | tf_op jit(solution)/shard_map/ppermute | solution.py:287
  152.6 0.6 collective-permute-start.14
  153.2 1.6 mine_rows.5
  154.8 1.6 other_rows.5
  156.3 13.7 %all_to_all.46.got_ref = f32[32,1,1664]{2,1,0:T(1,128)S(1)} all-to-all(f32[32,1,1664]{2,1,0:T(1,128)S(1)} %get-tuple-element.84), channel_id=1, replica_groups=mesh['animal'=8,'marker'=32] {'marker'}, dimensions={0} | all-to-all | bytes 425984 | tf_op jit(solution)/shard_map/all_to_all | solution.py:277
  170.0 0.1 spread.7
  170.1 15.1 %all_to_all.47.total_ref = f32[32,1,1664]{2,1,0:T(1,128)S(1)} all-to-all(f32[32,1,1664]{2,1,0:T(1,128)S(1)} %spread.7), channel_id=1, replica_groups=mesh['animal'=8,'marker'=32] {'marker'}, dimensions={0} | all-to-all | bytes 425984 | tf_op jit(solution)/shard_map/all_to_all | solution.py:279
  185.2 0.9 other_columns.7
  186.2 2.9 %collective-permute-start.15 = (f32[16,1664]{1,0:T(8,128)S(1)}, f32[16,1664]{1,0:T(8,128)S(1)}, u32[]{:S(2)}, u32[]{:S(2)}) collective-permute-start(f32[16,1664]{1,0:T(8,128)S(1)} %other_columns.7), channel_id=1, source_target_pairs={{0,32},{32,0},{64,96},{96,64},{128,160},{160,128},{192,224},{224,1... | collective-permute-start | bytes 319496 | tf_op jit(solution)/shard_map/ppermute | solution.py:284
  189.1 1.5 mine_columns.7
  190.6 0.4 collective-permute-start.18
  191.0 0.2 collective-permute-start.17
  191.2 1.0 collective-permute-start.16
  192.2 3.1 %collective-permute-done.18.refs_3_ = f32[16,1664]{1,0:T(8,128)S(1)} collective-permute-done((f32[16,1664]{1,0:T(8,128)S(1)}, f32[16,1664]{1,0:T(8,128)S(1)}, u32[]{:S(2)}, u32[]{:S(2)}) %collective-permute-start.18) | collective-permute-done | bytes 106528 | tf_op jit(solution)/shard_map/ppermute | solution.py:287
  195.3 1.5 collective-permute-done.17.refs_2_
  196.8 2.9 %collective-permute-done.16.refs_1_ = f32[16,1664]{1,0:T(8,128)S(1)} collective-permute-done((f32[16,1664]{1,0:T(8,128)S(1)}, f32[16,1664]{1,0:T(8,128)S(1)}, u32[]{:S(2)}, u32[]{:S(2)}) %collective-permute-start.16) | collective-permute-done | bytes 106528 | tf_op jit(solution)/shard_map/ppermute | solution.py:287
  199.7 0.6 collective-permute-start.19
  200.3 1.0 collective-permute-done.19.other_ref
  201.2 0.9 last.1
  (12 shorter events, 0.2 us)
Async XLA Ops:
  43.6 4.2 %collective-permute-start = (f32[16,1664]{1,0:T(8,128)S(1)}, f32[16,1664]{1,0:T(8,128)S(1)}, u32[]{:S(2)}, u32[]{:S(2)}) collective-permute-start(f32[16,1664]{1,0:T(8,128)S(1)} %other_columns.4), channel_id=1, source_target_pairs={{0,32},{32,0},{64,96},{96,64},{128,160},{160,128},{192,224},{224,1... | collective-permute-start | bytes 319496 | tf_op jit(solution)/shard_map/ppermute | solution.py:284
  47.8 6.7 %collective-permute-start.3 = (f32[16,1664]{1,0:T(8,128)S(1)}, f32[16,1664]{1,0:T(8,128)S(1)}, u32[]{:S(2)}, u32[]{:S(2)}) collective-permute-start(f32[16,1664]{1,0:T(8,128)S(1)} %add.8.refs_0_), channel_id=1, source_target_pairs={{0,192},{32,224},{64,0},{96,32},{128,64},{160,96},{192,128},{224,1... | collective-permute-start | bytes 319496 | tf_op jit(solution)/shard_map/ppermute | solution.py:287
  50.4 5.4 %collective-permute-start.2 = (f32[16,1664]{1,0:T(8,128)S(1)}, f32[16,1664]{1,0:T(8,128)S(1)}, u32[]{:S(2)}, u32[]{:S(2)}) collective-permute-start(f32[16,1664]{1,0:T(8,128)S(1)} %add.8.refs_0_), channel_id=1, source_target_pairs={{0,128},{32,160},{64,192},{96,224},{128,0},{160,32},{192,64},{224,... | collective-permute-start | bytes 319496 | tf_op jit(solution)/shard_map/ppermute | solution.py:287
  50.9 8.0 %collective-permute-start.1 = (f32[16,1664]{1,0:T(8,128)S(1)}, f32[16,1664]{1,0:T(8,128)S(1)}, u32[]{:S(2)}, u32[]{:S(2)}) collective-permute-start(f32[16,1664]{1,0:T(8,128)S(1)} %add.8.refs_0_), channel_id=1, source_target_pairs={{0,64},{32,96},{64,128},{96,160},{128,192},{160,224},{192,0},{224,... | collective-permute-start | bytes 319496 | tf_op jit(solution)/shard_map/ppermute | solution.py:287
  59.0 2.3 %collective-permute-start.4 = (f32[16,1664]{1,0:T(8,128)S(1)}, f32[16,1664]{1,0:T(8,128)S(1)}, u32[]{:S(2)}, u32[]{:S(2)}) collective-permute-start(f32[16,1664]{1,0:T(8,128)S(1)} %add.9.refs_0_), channel_id=1, source_target_pairs={{0,32},{32,0},{64,96},{96,64},{128,160},{160,128},{192,224},{224,1... | collective-permute-start | bytes 319496 | tf_op jit(solution)/shard_map/ppermute | solution.py:284
  92.5 3.9 %collective-permute-start.5 = (f32[16,1664]{1,0:T(8,128)S(1)}, f32[16,1664]{1,0:T(8,128)S(1)}, u32[]{:S(2)}, u32[]{:S(2)}) collective-permute-start(f32[16,1664]{1,0:T(8,128)S(1)} %other_columns.5), channel_id=1, source_target_pairs={{0,32},{32,0},{64,96},{96,64},{128,160},{160,128},{192,224},{224,1... | collective-permute-start | bytes 319496 | tf_op jit(solution)/shard_map/ppermute | solution.py:284
  96.4 4.5 %collective-permute-start.8 = (f32[16,1664]{1,0:T(8,128)S(1)}, f32[16,1664]{1,0:T(8,128)S(1)}, u32[]{:S(2)}, u32[]{:S(2)}) collective-permute-start(f32[16,1664]{1,0:T(8,128)S(1)} %add.10.refs_0_), channel_id=1, source_target_pairs={{0,192},{32,224},{64,0},{96,32},{128,64},{160,96},{192,128},{224,1... | collective-permute-start | bytes 319496 | tf_op jit(solution)/shard_map/ppermute | solution.py:287
  97.0 5.4 %collective-permute-start.7 = (f32[16,1664]{1,0:T(8,128)S(1)}, f32[16,1664]{1,0:T(8,128)S(1)}, u32[]{:S(2)}, u32[]{:S(2)}) collective-permute-start(f32[16,1664]{1,0:T(8,128)S(1)} %add.10.refs_0_), channel_id=1, source_target_pairs={{0,128},{32,160},{64,192},{96,224},{128,0},{160,32},{192,64},{224,... | collective-permute-start | bytes 319496 | tf_op jit(solution)/shard_map/ppermute | solution.py:287
  97.5 8.2 %collective-permute-start.6 = (f32[16,1664]{1,0:T(8,128)S(1)}, f32[16,1664]{1,0:T(8,128)S(1)}, u32[]{:S(2)}, u32[]{:S(2)}) collective-permute-start(f32[16,1664]{1,0:T(8,128)S(1)} %add.10.refs_0_), channel_id=1, source_target_pairs={{0,64},{32,96},{64,128},{96,160},{128,192},{160,224},{192,0},{224,... | collective-permute-start | bytes 319496 | tf_op jit(solution)/shard_map/ppermute | solution.py:287
  105.7 2.1 %collective-permute-start.9 = (f32[16,1664]{1,0:T(8,128)S(1)}, f32[16,1664]{1,0:T(8,128)S(1)}, u32[]{:S(2)}, u32[]{:S(2)}) collective-permute-start(f32[16,1664]{1,0:T(8,128)S(1)} %add.11.refs_0_), channel_id=1, source_target_pairs={{0,32},{32,0},{64,96},{96,64},{128,160},{160,128},{192,224},{224,1... | collective-permute-start | bytes 319496 | tf_op jit(solution)/shard_map/ppermute | solution.py:284
  139.3 3.9 %collective-permute-start.10 = (f32[16,1664]{1,0:T(8,128)S(1)}, f32[16,1664]{1,0:T(8,128)S(1)}, u32[]{:S(2)}, u32[]{:S(2)}) collective-permute-start(f32[16,1664]{1,0:T(8,128)S(1)} %other_columns.6), channel_id=1, source_target_pairs={{0,32},{32,0},{64,96},{96,64},{128,160},{160,128},{192,224},{224,1... | collective-permute-start | bytes 319496 | tf_op jit(solution)/shard_map/ppermute | solution.py:284
  143.2 4.3 %collective-permute-start.13 = (f32[16,1664]{1,0:T(8,128)S(1)}, f32[16,1664]{1,0:T(8,128)S(1)}, u32[]{:S(2)}, u32[]{:S(2)}) collective-permute-start(f32[16,1664]{1,0:T(8,128)S(1)} %add.12.refs_0_), channel_id=1, source_target_pairs={{0,192},{32,224},{64,0},{96,32},{128,64},{160,96},{192,128},{224,1... | collective-permute-start | bytes 319496 | tf_op jit(solution)/shard_map/ppermute | solution.py:287
  143.9 5.4 %collective-permute-start.12 = (f32[16,1664]{1,0:T(8,128)S(1)}, f32[16,1664]{1,0:T(8,128)S(1)}, u32[]{:S(2)}, u32[]{:S(2)}) collective-permute-start(f32[16,1664]{1,0:T(8,128)S(1)} %add.12.refs_0_), channel_id=1, source_target_pairs={{0,128},{32,160},{64,192},{96,224},{128,0},{160,32},{192,64},{224,... | collective-permute-start | bytes 319496 | tf_op jit(solution)/shard_map/ppermute | solution.py:287
  144.1 8.5 %collective-permute-start.11 = (f32[16,1664]{1,0:T(8,128)S(1)}, f32[16,1664]{1,0:T(8,128)S(1)}, u32[]{:S(2)}, u32[]{:S(2)}) collective-permute-start(f32[16,1664]{1,0:T(8,128)S(1)} %add.12.refs_0_), channel_id=1, source_target_pairs={{0,64},{32,96},{64,128},{96,160},{128,192},{160,224},{192,0},{224,... | collective-permute-start | bytes 319496 | tf_op jit(solution)/shard_map/ppermute | solution.py:287
  152.6 2.2 %collective-permute-start.14 = (f32[16,1664]{1,0:T(8,128)S(1)}, f32[16,1664]{1,0:T(8,128)S(1)}, u32[]{:S(2)}, u32[]{:S(2)}) collective-permute-start(f32[16,1664]{1,0:T(8,128)S(1)} %add.13.refs_0_), channel_id=1, source_target_pairs={{0,32},{32,0},{64,96},{96,64},{128,160},{160,128},{192,224},{224,1... | collective-permute-start | bytes 319496 | tf_op jit(solution)/shard_map/ppermute | solution.py:284
  186.2 4.4 %collective-permute-start.15 = (f32[16,1664]{1,0:T(8,128)S(1)}, f32[16,1664]{1,0:T(8,128)S(1)}, u32[]{:S(2)}, u32[]{:S(2)}) collective-permute-start(f32[16,1664]{1,0:T(8,128)S(1)} %other_columns.7), channel_id=1, source_target_pairs={{0,32},{32,0},{64,96},{96,64},{128,160},{160,128},{192,224},{224,1... | collective-permute-start | bytes 319496 | tf_op jit(solution)/shard_map/ppermute | solution.py:284
  190.6 4.7 %collective-permute-start.18 = (f32[16,1664]{1,0:T(8,128)S(1)}, f32[16,1664]{1,0:T(8,128)S(1)}, u32[]{:S(2)}, u32[]{:S(2)}) collective-permute-start(f32[16,1664]{1,0:T(8,128)S(1)} %add.14.refs_0_), channel_id=1, source_target_pairs={{0,192},{32,224},{64,0},{96,32},{128,64},{160,96},{192,128},{224,1... | collective-permute-start | bytes 319496 | tf_op jit(solution)/shard_map/ppermute | solution.py:287
  191.0 5.8 %collective-permute-start.17 = (f32[16,1664]{1,0:T(8,128)S(1)}, f32[16,1664]{1,0:T(8,128)S(1)}, u32[]{:S(2)}, u32[]{:S(2)}) collective-permute-start(f32[16,1664]{1,0:T(8,128)S(1)} %add.14.refs_0_), channel_id=1, source_target_pairs={{0,128},{32,160},{64,192},{96,224},{128,0},{160,32},{192,64},{224,... | collective-permute-start | bytes 319496 | tf_op jit(solution)/shard_map/ppermute | solution.py:287
  191.2 8.5 %collective-permute-start.16 = (f32[16,1664]{1,0:T(8,128)S(1)}, f32[16,1664]{1,0:T(8,128)S(1)}, u32[]{:S(2)}, u32[]{:S(2)}) collective-permute-start(f32[16,1664]{1,0:T(8,128)S(1)} %add.14.refs_0_), channel_id=1, source_target_pairs={{0,64},{32,96},{64,128},{96,160},{128,192},{160,224},{192,0},{224,... | collective-permute-start | bytes 319496 | tf_op jit(solution)/shard_map/ppermute | solution.py:287
  199.7 1.5 collective-permute-start.19

commit v3 on v2

--- a/solution.py
+++ b/solution.py
@@ -9,8 +9,10 @@
 
 ITERS = 4
 CORES = 2
+DEPTH = 8
 EXTRA = 128
 BLOCK = 256
+PIECE = 512
 AHEAD = 2
 MIB = 1024 * 1024
 VMEM = pl.BlockSpec(memory_space=pltpu.VMEM)
@@ -46,30 +48,24 @@
     return both[:half] + both[half:]
 
 
-def row_product(terms_ref, block):
-    return folded(
-        lax.dot_general(terms_ref[...], block, (((1,), (1,)), ((), ())), preferred_element_type=jnp.float32)
-    )
-
-
-def col_product(terms_ref, block):
+def product(terms_ref, block):
     return folded(jnp.dot(terms_ref[...], block, preferred_element_type=jnp.float32))
 
 
-def blocks(extent):
-    return [pl.ds(i * BLOCK, BLOCK) for i in range(extent // BLOCK)]
+def blocks(extent, block=BLOCK):
+    return [pl.ds(i * block, block) for i in range(extent // block)]
 
 
 def first_kernel(
     geno_ref, freq_ref, shrink_ref, right_ref,
-    coded_ref, freq_out, shrink_out, residual_out, scaled_out, part_ref,
+    coded_ref, turned_ref, freq_out, shrink_out, residual_out, scaled_out, part_ref,
     stage, right, freq_line, shrink_line, terms_ref, geno_sems, small_sems,
 ):
     animals = coded_ref.shape[0]
     half = right_ref.shape[0] // 2
     pairs = ((right_ref, right), (freq_ref, freq_line), (shrink_ref, shrink_line))
     small = [pltpu.make_async_copy(src, dst, small_sems.at[i]) for i, (src, dst) in enumerate(pairs)]
-    spots = blocks(animals)
+    spots = blocks(animals, PIECE)
     copies = [
         pltpu.make_async_copy(geno_ref.at[at, :], stage.at[at, :], geno_sems.at[i]) for i, at in enumerate(spots)
     ]
@@ -98,11 +94,27 @@
             copies[i + AHEAD].start()
         block = stage[at, :].astype(jnp.bfloat16)
         coded_ref[at, :] = block
-        part_ref[:, :, at] = (row_product(terms_ref, block) - offset)[:, None, :]
-
-
-def spread_kernel(got_ref, out_ref):
-    out_ref[...] = jnp.broadcast_to(jnp.sum(got_ref[...], axis=0, keepdims=True), out_ref.shape)
+        turned = block.T
+        turned_ref[:, at] = turned
+        part_ref[:, :, at] = (product(terms_ref, turned) - offset)[:, None, :]
+
+
+def collect_kernel(got_ref, out_ref):
+    own = out_ref.shape[0]
+    total = got_ref[:own]
+    for i in range(own, got_ref.shape[0], own):
+        total += got_ref[i : i + own]
+    out_ref[...] = total
+
+
+def spread_kernel(*refs):
+    *ins, out_ref = refs
+    own = ins[0].shape[0]
+    total = ins[0][...]
+    for ref in ins[1:]:
+        total += ref[...]
+    for i in range(0, out_ref.shape[0], own):
+        out_ref[i : i + own] = total
 
 
 def add_kernel(*refs):
@@ -118,7 +130,7 @@
     put_terms(vec, terms_ref)
     row_total = row_sum(vec)
     for at in blocks(width):
-        out_ref[:, at] = col_product(terms_ref, coded_ref[:, at]) - 2.0 * freq_ref[:, at] * row_total
+        out_ref[:, at] = product(terms_ref, coded_ref[:, at]) - 2.0 * freq_ref[:, at] * row_total
     out_ref[:, width:] = lanes(row_sum(vec * vec))
 
 
@@ -135,8 +147,11 @@
     half_columns(vec, coded_ref, freq_ref, out_ref, terms_ref)
 
 
-def mine_columns(first, total_ref, freq_ref, coded_ref, scaled_ref, *refs):
-    *old, direction_out, rows_out, kept_out, out_ref, terms_ref = refs
+def mine_columns(first, last, total_ref, freq_ref, coded_ref, scaled_ref, *refs):
+    *refs, terms_ref = refs
+    if not last:
+        *refs, rows_out = refs
+    *old, direction_out, kept_out, out_ref = refs
     animals = coded_ref.shape[0]
     half = out_ref.shape[0]
     for local, at in zip((slice(0, half), slice(half, None)), half_slices(half)):
@@ -152,8 +167,11 @@
             vec += beta * rows_ref[local]
             direction_out[local] = scaled_ref[local] + beta * direction_ref[local]
             kept_out[local] = lanes(rho, square + beta * (2.0 * cross + beta * kept_ref[local, 1:2]))
-        rows_out[local] = vec
-    half_columns(rows_out[:half], coded_ref, freq_ref, out_ref, terms_ref)
+        if local.start == 0:
+            mine = vec
+        if not last:
+            rows_out[local] = vec
+    half_columns(mine, coded_ref, freq_ref, out_ref, terms_ref)
 
 
 def update(inv_count, local, total_ref, shrink_ref, direction_ref, residual_ref, kept_ref, solution_ref=None):
@@ -168,8 +186,8 @@
     return moved, residual_ref[local] - step * image, direction
 
 
-def half_rows(inv_count, local, state, freq_ref, coded_ref, solution_out, residual_out, scaled_out, write, terms_ref):
-    animals = coded_ref.shape[0]
+def half_rows(inv_count, local, state, freq_ref, turned_ref, solution_out, residual_out, scaled_out, write, terms_ref):
+    animals = turned_ref.shape[1]
     solution, residual, direction = update(inv_count, local, *state)
     freq, shrink = freq_ref[...], state[1][...]
     scaled = residual / (2.0 * freq * (1.0 - freq) + shrink)
@@ -180,14 +198,14 @@
     weighted = shrink * scaled
     offset = row_sum(2.0 * freq * scaled)
     for at in blocks(animals):
-        write(at, row_product(terms_ref, coded_ref[at, :]) - offset)
+        write(at, product(terms_ref, turned_ref[:, at]) - offset)
     write(
         pl.ds(animals, EXTRA),
         lanes(row_sum(residual * scaled), row_sum(weighted * scaled), row_sum(weighted * direction)),
     )
 
 
-def mine_rows(inv_count, freq_ref, coded_ref, *refs):
+def mine_rows(inv_count, freq_ref, turned_ref, *refs):
     *state, solution_out, residual_out, scaled_out, part_ref, terms_ref = refs
     half = part_ref.shape[0]
 
@@ -195,12 +213,12 @@
         part_ref[:, :, at] = value[:, None, :]
 
     half_rows(
-        inv_count, slice(0, half), state, freq_ref, coded_ref,
+        inv_count, slice(0, half), state, freq_ref, turned_ref,
         solution_out, residual_out, scaled_out, write, terms_ref,
     )
 
 
-def other_rows(inv_count, freq_ref, coded_ref, solution_ref, residual_ref, scaled_ref, half_ref, *refs):
+def other_rows(inv_count, freq_ref, turned_ref, solution_ref, residual_ref, scaled_ref, half_ref, *refs):
     *state, solution_out, residual_out, scaled_out, part_ref, terms_ref = refs
     half = half_ref.shape[0]
     mine, other = half_slices(half)
@@ -214,7 +232,7 @@
 
     top = slice(half, None)
     half_rows(
-        inv_count, top, state, freq_ref, coded_ref,
+        inv_count, top, state, freq_ref, turned_ref,
         solution_out.at[top], residual_out.at[top], scaled_out.at[top], write, terms_ref,
     )
 
@@ -254,29 +272,40 @@
     ext, own = f32(rhs, 1, animals + EXTRA), f32(half, width + EXTRA)
     line = f32(1, width)
 
-    coded, freq, shrink, residual, scaled, part = pl.pallas_call(
+    coded, turned, freq, shrink, residual, scaled, part = pl.pallas_call(
         first_kernel,
         in_specs=[ANY] * 4,
-        out_specs=[VMEM] * 6,
-        out_shape=[pltpu.VMEM((animals, width), jnp.bfloat16), line, line, vec, vec, ext],
+        out_specs=[VMEM] * 7,
+        out_shape=[
+            pltpu.VMEM((animals, width), jnp.bfloat16), pltpu.VMEM((width, animals), jnp.bfloat16), line, line, vec, vec, ext],
         scratch_shapes=[
             pltpu.VMEM((animals, width), jnp.float32),
             pltpu.VMEM((rhs, width), jnp.float32),
             pltpu.VMEM((width,), jnp.float32),
             pltpu.VMEM((width,), jnp.float32),
             pltpu.VMEM((2 * rhs, width), jnp.bfloat16),
-            pltpu.SemaphoreType.DMA((animals // BLOCK,)),
+            pltpu.SemaphoreType.DMA((animals // PIECE,)),
             pltpu.SemaphoreType.DMA((3,)),
         ],
         compiler_params=pltpu.CompilerParams(vmem_limit_bytes=32 * MIB),
         name="first_rows",
     )(*[pltpu.with_memory_space_constraint(v, pltpu.HBM) for v in (genotype, allele_freq, shrink, right_side)])
-    coded = pltpu.with_memory_space_constraint(coded, pltpu.VMEM)
+    coded, turned = (pltpu.with_memory_space_constraint(v, pltpu.VMEM) for v in (coded, turned))
+
+    ys = lax.axis_size("marker") // DEPTH
+    near = [[y * DEPTH + z + o for y in range(ys) for o in range(2)] for z in range(0, DEPTH, 2)]
+    count = 2 * ys
+
+    def exchange(v):
+        return lax.all_to_all(v, "marker", 0, 0, tiled=True, axis_index_groups=near)
+
+    def far(v, k):
+        return lax.ppermute(v, "marker", [(i, i ^ k) for i in range(ys * DEPTH)])
 
     def marker_sum(part):
-        got = lax.all_to_all(part, "marker", 0, 0, tiled=True)
-        spread = call(spread_kernel, "spread", f32(*got.shape), [got])
-        return lax.all_to_all(spread, "marker", 0, 0, tiled=True)
+        own = call(collect_kernel, "collect", f32(rhs // count, 1, part.shape[2]), [exchange(part)])
+        spread = call(spread_kernel, "spread", ext, [own] + [far(own, k) for k in range(2, DEPTH, 2)])
+        return exchange(spread)
 
     swap = [(x * CORES + c, x * CORES + 1 - c) for x in range(xs) for c in range(CORES)]
 
@@ -292,31 +321,31 @@
     old = []
     for step in range(ITERS):
         total = marker_sum(part)
-        first = step == 0
+        first, last = step == 0, step == ITERS - 1
         shared = [total, freq, coded]
         other = call(
             functools.partial(other_columns, first), "other_columns", own, shared + old[1:], terms(animals)
         )
         other = to_other(other)
-        *old, mine = call(
-            functools.partial(mine_columns, first), "mine_columns",
-            [vec, f32(rhs, animals), kept_shape, own], shared + [scaled] + old, terms(animals),
-        )
-        direction, _, kept = old
+        direction, kept, mine, *rows = call(
+            functools.partial(mine_columns, first, last), "mine_columns",
+            [vec, kept_shape, own] + ([] if last else [f32(rhs, animals)]), shared + [scaled] + old, terms(animals),
+        )
+        old = [direction, *rows, kept]
         mine = call(add_kernel, "add", own, [mine, other])
         mine = call(add_kernel, "add", own, [mine] + [shift(mine, d) for d in range(1, xs)])
         other = to_other(mine)
         state = [shrink, direction, residual, kept, *solution]
-        if step == ITERS - 1:
+        if last:
             return tuple(call(functools.partial(last_kernel, inv_count), "last", [vec, vec], [mine, other] + state))
         half_part = f32(half, 1, animals + EXTRA)
         outs = call(
             functools.partial(mine_rows, inv_count), "mine_rows", [halves, halves, halves, half_part],
-            [freq, coded, mine] + state, terms(width),
+            [freq, turned, mine] + state, terms(width),
         )
         *solution, residual, scaled, part = call(
             functools.partial(other_rows, inv_count), "other_rows", [vec, vec, vec, ext],
-            [freq, coded, *outs, other] + state, terms(width),
+            [freq, turned, *outs, other] + state, terms(width),
         )
 
 

time: 203 us -> 190 us (0.936)
  blocking collectives: 122 us -> 73.3 us
  starting transfers between devices: 22.9 us -> 51.7 us
  waiting for transfers between devices: 31.3 us -> 44.3 us
  Pallas kernels: 24.8 us -> 19.8 us
    all_to_all x8, blocking collectives: 122 us -> 73.3 us  [exchange(): return lax.all_to_all(v, 'marker', 0, 0, tiled=True, axis_index_groups=near)]
    ppermute x0 -> x12, starting transfers between devices: none -> 24.6 us  [far(): return lax.ppermute(v, 'marker', [(i, i ^ k) for i in range(ys * DEPTH)])]
    ppermute x0 -> x12, waiting for transfers between devices: none -> 13.1 us  [far(): return lax.ppermute(v, 'marker', [(i, i ^ k) for i in range(ys * DEPTH)])]
    ppermute x8, starting transfers between devices: 14.4 us -> 18.8 us  [to_other(): return lax.ppermute(v, 'animal', swap)]
    pallas_call x27 -> x31, Pallas kernels: 19 us -> 14.9 us  [call(): pl.pallas_call(kernel, in_specs=[VMEM] * len(args), out_specs=jax.tree.ma...]
  transfers between devices with their start and end apart: 20 -> 32, of which waited for: 14 -> 17; matrix products, arithmetic and copies ran while one was open for 0% -> 0% of each run, Pallas kernels for 4% -> 4%
where the time goes in v3:
time: 190 us
  blocking collectives  73.3 us (39%)
  starting transfers between devices  51.7 us (27%)
  waiting for transfers between devices  44.3 us (23%)
  Pallas kernels  19.8 us (10%)
    all_to_all x8, blocking collectives, exchange(): return lax.all_to_all(v, 'marker', 0, 0, tiled=True, axis_index_groups=near)  73.3 us
    ppermute x12, waiting for transfers between devices, shift(): lax.ppermute(v, 'animal', [(x * CORES + c, (x + d) % xs * CORES + c) for...  30.3 us
    ppermute x12, starting transfers between devices, far(): return lax.ppermute(v, 'marker', [(i, i ^ k) for i in range(ys * DEPTH)])  24.6 us
    ppermute x8, starting transfers between devices, to_other(): return lax.ppermute(v, 'animal', swap)  18.8 us
    pallas_call x31, Pallas kernels, call(): pl.pallas_call(kernel, in_specs=[VMEM] * len(args), out_specs=jax.tree.ma...  14.9 us
    ppermute x12, waiting for transfers between devices, far(): return lax.ppermute(v, 'marker', [(i, i ^ k) for i in range(ys * DEPTH)])  13.1 us
    ppermute x12, starting transfers between devices, shift(): lax.ppermute(v, 'animal', [(x * CORES + c, (x + d) % xs * CORES + c) for...  8.32 us
    pallas_call x1, Pallas kernels, body(): pl.pallas_call(first_kernel, in_specs=[ANY] * 4, out_specs=[VMEM] * 7, ou...  4.9 us
  transfers between devices with their start and end apart: 32, of which 17 were waited for; matrix products, arithmetic and copies ran while one was open for 0% of the time, Pallas kernels for 4%

profile of v3, /device:TPU:1, one launch (start us, length us, event | category | flops | bytes accessed | tf_op | source)
XLA Modules:
  0.0 189.9 jit_solution(10736596250561367581)
XLA Ops:
  0.6 4.9 %first_rows.1 = (bf16[1536,1536]{1,0:T(8,128)(2,1)S(1)}, bf16[1536,1536]{1,0:T(8,128)(2,1)S(1)}, f32[1,1536]{1,0:T(1,128)S(1)}, f32[1,1536]{1,0:T(1,128)S(1)}, f...) custom-call(f32[1536,1536]{1,0:T(8,128)} %geno_ref.1, f32[1536]{0:T(1024)} %freq_ref.1, ...), custom_call_target="tpu_custom_call" | custom-call | tf_op jit(solution)/shard_map/first_rows/pallas_call | solution.py:275
  5.5 12.2 %all_to_all.40.got_ref = f32[32,1,1664]{2,1,0:T(1,128)S(1)} all-to-all(f32[32,1,1664]{2,1,0:T(1,128)S(1)} %get-tuple-element.50), channel_id=1, replica_groups={{0,1,8,9,16,17,24,25},{2,3,10,11,18,19,26,27},{4,5,12,13,20,21,28,29},{..., dimensions={0} | all-to-all | bytes 425984 | tf_op jit(solution)/shard_map/all_to_all | solution.py:300
  17.7 5.2 %collective-permute-start.2 = (f32[4,1,1664]{2,1,0:T(1,128)S(1)}, f32[4,1,1664]{2,1,0:T(1,128)S(1)}, u32[]{:S(2)}, u32[]{:S(2)}) collective-permute-start(f32[4,1,1664]{2,1,0:T(1,128)S(1)} %collect.4.refs_0_), channel_id=1, source_target_pairs={{0,6},{1,7},{2,4},{3,5},{4,2},{5,3},{6,0},{7,1},{8,14},{9,15},{10,... | collective-permute-start | bytes 79880 | tf_op jit(solution)/shard_map/ppermute | solution.py:303
  22.9 1.2 collective-permute-start.1
  24.1 1.0 collective-permute-start
  25.1 4.5 %collective-permute-done.1.refs_2_ = f32[4,1,1664]{2,1,0:T(1,128)S(1)} collective-permute-done((f32[4,1,1664]{2,1,0:T(1,128)S(1)}, f32[4,1,1664]{2,1,0:T(1,128)S(1)}, u32[]{:S(2)}, u32[]{:S(2)}) %collective-permute-start.1) | collective-permute-done | bytes 26656 | tf_op jit(solution)/shard_map/ppermute | solution.py:303
  29.7 8.3 %all_to_all.41.total_ref = f32[32,1,1664]{2,1,0:T(1,128)S(1)} all-to-all(f32[32,1,1664]{2,1,0:T(1,128)S(1)} %spread.4), channel_id=1, replica_groups={{0,1,8,9,16,17,24,25},{2,3,10,11,18,19,26,27},{4,5,12,13,20,21,28,29},{..., dimensions={0} | all-to-all | bytes 425984 | tf_op jit(solution)/shard_map/all_to_all | solution.py:300
  37.9 0.9 other_columns.4
  38.9 4.6 %collective-permute-start.3 = (f32[16,1664]{1,0:T(8,128)S(1)}, f32[16,1664]{1,0:T(8,128)S(1)}, u32[]{:S(2)}, u32[]{:S(2)}) collective-permute-start(f32[16,1664]{1,0:T(8,128)S(1)} %other_columns.4), channel_id=1, source_target_pairs={{0,32},{32,0},{64,96},{96,64},{128,160},{160,128},{192,224},{224,1... | collective-permute-start | bytes 319496 | tf_op jit(solution)/shard_map/ppermute | solution.py:313
  43.5 1.0 mine_columns.4
  44.5 2.6 %collective-permute-start.6 = (f32[16,1664]{1,0:T(8,128)S(1)}, f32[16,1664]{1,0:T(8,128)S(1)}, u32[]{:S(2)}, u32[]{:S(2)}) collective-permute-start(f32[16,1664]{1,0:T(8,128)S(1)} %add.8.refs_0_), channel_id=1, source_target_pairs={{0,192},{32,224},{64,0},{96,32},{128,64},{160,96},{192,128},{224,1... | collective-permute-start | bytes 319496 | tf_op jit(solution)/shard_map/ppermute | solution.py:316
  47.5 0.6 collective-permute-start.4
  48.2 3.0 %collective-permute-done.6.refs_3_ = f32[16,1664]{1,0:T(8,128)S(1)} collective-permute-done((f32[16,1664]{1,0:T(8,128)S(1)}, f32[16,1664]{1,0:T(8,128)S(1)}, u32[]{:S(2)}, u32[]{:S(2)}) %collective-permute-start.6) | collective-permute-done | bytes 106528 | tf_op jit(solution)/shard_map/ppermute | solution.py:316
  51.2 1.2 collective-permute-done.5.refs_2_
  52.4 3.2 %collective-permute-done.4.refs_1_ = f32[16,1664]{1,0:T(8,128)S(1)} collective-permute-done((f32[16,1664]{1,0:T(8,128)S(1)}, f32[16,1664]{1,0:T(8,128)S(1)}, u32[]{:S(2)}, u32[]{:S(2)}) %collective-permute-start.4) | collective-permute-done | bytes 106528 | tf_op jit(solution)/shard_map/ppermute | solution.py:316
  55.6 0.7 collective-permute-start.7
  56.3 1.0 mine_rows.3
  57.3 1.0 other_rows.3
  58.4 8.6 %all_to_all.42.got_ref = f32[32,1,1664]{2,1,0:T(1,128)S(1)} all-to-all(f32[32,1,1664]{2,1,0:T(1,128)S(1)} %get-tuple-element.62), channel_id=1, replica_groups={{0,1,8,9,16,17,24,25},{2,3,10,11,18,19,26,27},{4,5,12,13,20,21,28,29},{..., dimensions={0} | all-to-all | bytes 425984 | tf_op jit(solution)/shard_map/all_to_all | solution.py:300
  67.0 1.8 collective-permute-start.10
  68.8 3.0 %collective-permute-start.9 = (f32[4,1,1664]{2,1,0:T(1,128)S(1)}, f32[4,1,1664]{2,1,0:T(1,128)S(1)}, u32[]{:S(2)}, u32[]{:S(2)}) collective-permute-start(f32[4,1,1664]{2,1,0:T(1,128)S(1)} %collect.5.refs_0_), channel_id=1, source_target_pairs={{0,4},{1,5},{2,6},{3,7},{4,0},{5,1},{6,2},{7,3},{8,12},{9,13},{10,... | collective-permute-start | bytes 79880 | tf_op jit(solution)/shard_map/ppermute | solution.py:303
  71.8 0.9 collective-permute-start.8
  72.7 2.7 %collective-permute-done.9.refs_2_ = f32[4,1,1664]{2,1,0:T(1,128)S(1)} collective-permute-done((f32[4,1,1664]{2,1,0:T(1,128)S(1)}, f32[4,1,1664]{2,1,0:T(1,128)S(1)}, u32[]{:S(2)}, u32[]{:S(2)}) %collective-permute-start.9) | collective-permute-done | bytes 26656 | tf_op jit(solution)/shard_map/ppermute | solution.py:303
  75.4 9.5 %all_to_all.43.total_ref = f32[32,1,1664]{2,1,0:T(1,128)S(1)} all-to-all(f32[32,1,1664]{2,1,0:T(1,128)S(1)} %spread.5), channel_id=1, replica_groups={{0,1,8,9,16,17,24,25},{2,3,10,11,18,19,26,27},{4,5,12,13,20,21,28,29},{..., dimensions={0} | all-to-all | bytes 425984 | tf_op jit(solution)/shard_map/all_to_all | solution.py:300
  84.9 0.9 other_columns.5
  85.9 3.8 %collective-permute-start.11 = (f32[16,1664]{1,0:T(8,128)S(1)}, f32[16,1664]{1,0:T(8,128)S(1)}, u32[]{:S(2)}, u32[]{:S(2)}) collective-permute-start(f32[16,1664]{1,0:T(8,128)S(1)} %other_columns.5), channel_id=1, source_target_pairs={{0,32},{32,0},{64,96},{96,64},{128,160},{160,128},{192,224},{224,1... | collective-permute-start | bytes 319496 | tf_op jit(solution)/shard_map/ppermute | solution.py:313
  89.6 1.0 mine_columns.5
  91.5 0.7 collective-permute-start.12
  92.2 2.8 %collective-permute-done.14.refs_3_ = f32[16,1664]{1,0:T(8,128)S(1)} collective-permute-done((f32[16,1664]{1,0:T(8,128)S(1)}, f32[16,1664]{1,0:T(8,128)S(1)}, u32[]{:S(2)}, u32[]{:S(2)}) %collective-permute-start.14) | collective-permute-done | bytes 106528 | tf_op jit(solution)/shard_map/ppermute | solution.py:316
  94.9 1.5 collective-permute-done.13.refs_2_
  96.4 3.3 %collective-permute-done.12.refs_1_ = f32[16,1664]{1,0:T(8,128)S(1)} collective-permute-done((f32[16,1664]{1,0:T(8,128)S(1)}, f32[16,1664]{1,0:T(8,128)S(1)}, u32[]{:S(2)}, u32[]{:S(2)}) %collective-permute-start.12) | collective-permute-done | bytes 106528 | tf_op jit(solution)/shard_map/ppermute | solution.py:316
  100.3 1.0 mine_rows.4
  101.3 1.0 other_rows.4
  102.3 8.6 %all_to_all.44.got_ref = f32[32,1,1664]{2,1,0:T(1,128)S(1)} all-to-all(f32[32,1,1664]{2,1,0:T(1,128)S(1)} %get-tuple-element.74), channel_id=1, replica_groups={{0,1,8,9,16,17,24,25},{2,3,10,11,18,19,26,27},{4,5,12,13,20,21,28,29},{..., dimensions={0} | all-to-all | bytes 425984 | tf_op jit(solution)/shard_map/all_to_all | solution.py:300
  110.9 1.5 collective-permute-start.18
  112.4 2.6 %collective-permute-start.17 = (f32[4,1,1664]{2,1,0:T(1,128)S(1)}, f32[4,1,1664]{2,1,0:T(1,128)S(1)}, u32[]{:S(2)}, u32[]{:S(2)}) collective-permute-start(f32[4,1,1664]{2,1,0:T(1,128)S(1)} %collect.6.refs_0_), channel_id=1, source_target_pairs={{0,4},{1,5},{2,6},{3,7},{4,0},{5,1},{6,2},{7,3},{8,12},{9,13},{10,... | collective-permute-start | bytes 79880 | tf_op jit(solution)/shard_map/ppermute | solution.py:303
  115.0 1.6 collective-permute-start.16
  116.7 2.6 %collective-permute-done.17.refs_2_ = f32[4,1,1664]{2,1,0:T(1,128)S(1)} collective-permute-done((f32[4,1,1664]{2,1,0:T(1,128)S(1)}, f32[4,1,1664]{2,1,0:T(1,128)S(1)}, u32[]{:S(2)}, u32[]{:S(2)}) %collective-permute-start.17) | collective-permute-done | bytes 26656 | tf_op jit(solution)/shard_map/ppermute | solution.py:303
  119.3 8.4 %all_to_all.45.total_ref = f32[32,1,1664]{2,1,0:T(1,128)S(1)} all-to-all(f32[32,1,1664]{2,1,0:T(1,128)S(1)} %spread.6), channel_id=1, replica_groups={{0,1,8,9,16,17,24,25},{2,3,10,11,18,19,26,27},{4,5,12,13,20,21,28,29},{..., dimensions={0} | all-to-all | bytes 425984 | tf_op jit(solution)/shard_map/all_to_all | solution.py:300
  127.7 0.9 other_columns.6
  128.6 4.0 %collective-permute-start.19 = (f32[16,1664]{1,0:T(8,128)S(1)}, f32[16,1664]{1,0:T(8,128)S(1)}, u32[]{:S(2)}, u32[]{:S(2)}) collective-permute-start(f32[16,1664]{1,0:T(8,128)S(1)} %other_columns.6), channel_id=1, source_target_pairs={{0,32},{32,0},{64,96},{96,64},{128,160},{160,128},{192,224},{224,1... | collective-permute-start | bytes 319496 | tf_op jit(solution)/shard_map/ppermute | solution.py:313
  132.7 1.0 mine_columns.6
  133.7 0.7 collective-permute-start.22
  134.6 0.7 collective-permute-start.20
  135.2 2.8 %collective-permute-done.22.refs_3_ = f32[16,1664]{1,0:T(8,128)S(1)} collective-permute-done((f32[16,1664]{1,0:T(8,128)S(1)}, f32[16,1664]{1,0:T(8,128)S(1)}, u32[]{:S(2)}, u32[]{:S(2)}) %collective-permute-start.22) | collective-permute-done | bytes 106528 | tf_op jit(solution)/shard_map/ppermute | solution.py:316
  138.0 1.8 collective-permute-done.21.refs_2_
  139.8 3.3 %collective-permute-done.20.refs_1_ = f32[16,1664]{1,0:T(8,128)S(1)} collective-permute-done((f32[16,1664]{1,0:T(8,128)S(1)}, f32[16,1664]{1,0:T(8,128)S(1)}, u32[]{:S(2)}, u32[]{:S(2)}) %collective-permute-start.20) | collective-permute-done | bytes 106528 | tf_op jit(solution)/shard_map/ppermute | solution.py:316
  143.1 0.8 collective-permute-start.23
  143.9 1.0 mine_rows.5
  144.9 1.0 other_rows.5
  145.9 8.6 %all_to_all.46.got_ref = f32[32,1,1664]{2,1,0:T(1,128)S(1)} all-to-all(f32[32,1,1664]{2,1,0:T(1,128)S(1)} %get-tuple-element.86), channel_id=1, replica_groups={{0,1,8,9,16,17,24,25},{2,3,10,11,18,19,26,27},{4,5,12,13,20,21,28,29},{..., dimensions={0} | all-to-all | bytes 425984 | tf_op jit(solution)/shard_map/all_to_all | solution.py:300
  154.5 2.1 %collective-permute-start.26 = (f32[4,1,1664]{2,1,0:T(1,128)S(1)}, f32[4,1,1664]{2,1,0:T(1,128)S(1)}, u32[]{:S(2)}, u32[]{:S(2)}) collective-permute-start(f32[4,1,1664]{2,1,0:T(1,128)S(1)} %collect.7.refs_0_), channel_id=1, source_target_pairs={{0,6},{1,7},{2,4},{3,5},{4,2},{5,3},{6,0},{7,1},{8,14},{9,15},{10,... | collective-permute-start | bytes 79880 | tf_op jit(solution)/shard_map/ppermute | solution.py:303
  156.6 3.2 %collective-permute-start.25 = (f32[4,1,1664]{2,1,0:T(1,128)S(1)}, f32[4,1,1664]{2,1,0:T(1,128)S(1)}, u32[]{:S(2)}, u32[]{:S(2)}) collective-permute-start(f32[4,1,1664]{2,1,0:T(1,128)S(1)} %collect.7.refs_0_), channel_id=1, source_target_pairs={{0,4},{1,5},{2,6},{3,7},{4,0},{5,1},{6,2},{7,3},{8,12},{9,13},{10,... | collective-permute-start | bytes 79880 | tf_op jit(solution)/shard_map/ppermute | solution.py:303
  160.3 3.2 %collective-permute-done.25.refs_2_ = f32[4,1,1664]{2,1,0:T(1,128)S(1)} collective-permute-done((f32[4,1,1664]{2,1,0:T(1,128)S(1)}, f32[4,1,1664]{2,1,0:T(1,128)S(1)}, u32[]{:S(2)}, u32[]{:S(2)}) %collective-permute-start.25) | collective-permute-done | bytes 26656 | tf_op jit(solution)/shard_map/ppermute | solution.py:303
  163.5 9.2 %all_to_all.47.total_ref = f32[32,1,1664]{2,1,0:T(1,128)S(1)} all-to-all(f32[32,1,1664]{2,1,0:T(1,128)S(1)} %spread.7), channel_id=1, replica_groups={{0,1,8,9,16,17,24,25},{2,3,10,11,18,19,26,27},{4,5,12,13,20,21,28,29},{..., dimensions={0} | all-to-all | bytes 425984 | tf_op jit(solution)/shard_map/all_to_all | solution.py:300
  172.8 0.9 other_columns.7
  173.7 3.7 %collective-permute-start.27 = (f32[16,1664]{1,0:T(8,128)S(1)}, f32[16,1664]{1,0:T(8,128)S(1)}, u32[]{:S(2)}, u32[]{:S(2)}) collective-permute-start(f32[16,1664]{1,0:T(8,128)S(1)} %other_columns.7), channel_id=1, source_target_pairs={{0,32},{32,0},{64,96},{96,64},{128,160},{160,128},{192,224},{224,1... | collective-permute-start | bytes 319496 | tf_op jit(solution)/shard_map/ppermute | solution.py:313
  177.4 0.9 mine_columns.7
  179.0 1.0 collective-permute-start.28
  180.0 2.7 %collective-permute-done.30.refs_3_ = f32[16,1664]{1,0:T(8,128)S(1)} collective-permute-done((f32[16,1664]{1,0:T(8,128)S(1)}, f32[16,1664]{1,0:T(8,128)S(1)}, u32[]{:S(2)}, u32[]{:S(2)}) %collective-permute-start.30) | collective-permute-done | bytes 106528 | tf_op jit(solution)/shard_map/ppermute | solution.py:316
  182.7 1.5 collective-permute-done.29.refs_2_
  184.2 3.3 %collective-permute-done.28.refs_1_ = f32[16,1664]{1,0:T(8,128)S(1)} collective-permute-done((f32[16,1664]{1,0:T(8,128)S(1)}, f32[16,1664]{1,0:T(8,128)S(1)}, u32[]{:S(2)}, u32[]{:S(2)}) %collective-permute-start.28) | collective-permute-done | bytes 106528 | tf_op jit(solution)/shard_map/ppermute | solution.py:316
  188.1 1.0 collective-permute-done.31.other_ref
  189.0 0.9 last.1
  (40 shorter events, 4.2 us)
Async XLA Ops:
  17.7 7.4 %collective-permute-start.2 = (f32[4,1,1664]{2,1,0:T(1,128)S(1)}, f32[4,1,1664]{2,1,0:T(1,128)S(1)}, u32[]{:S(2)}, u32[]{:S(2)}) collective-permute-start(f32[4,1,1664]{2,1,0:T(1,128)S(1)} %collect.4.refs_0_), channel_id=1, source_target_pairs={{0,6},{1,7},{2,4},{3,5},{4,2},{5,3},{6,0},{7,1},{8,14},{9,15},{10,... | collective-permute-start | bytes 79880 | tf_op jit(solution)/shard_map/ppermute | solution.py:303
  22.9 6.7 %collective-permute-start.1 = (f32[4,1,1664]{2,1,0:T(1,128)S(1)}, f32[4,1,1664]{2,1,0:T(1,128)S(1)}, u32[]{:S(2)}, u32[]{:S(2)}) collective-permute-start(f32[4,1,1664]{2,1,0:T(1,128)S(1)} %collect.4.refs_0_), channel_id=1, source_target_pairs={{0,4},{1,5},{2,6},{3,7},{4,0},{5,1},{6,2},{7,3},{8,12},{9,13},{10,... | collective-permute-start | bytes 79880 | tf_op jit(solution)/shard_map/ppermute | solution.py:303
  24.1 5.6 %collective-permute-start = (f32[4,1,1664]{2,1,0:T(1,128)S(1)}, f32[4,1,1664]{2,1,0:T(1,128)S(1)}, u32[]{:S(2)}, u32[]{:S(2)}) collective-permute-start(f32[4,1,1664]{2,1,0:T(1,128)S(1)} %collect.4.refs_0_), channel_id=1, source_target_pairs={{0,2},{1,3},{2,0},{3,1},{4,6},{5,7},{6,4},{7,5},{8,10},{9,11},{10,... | collective-permute-start | bytes 79880 | tf_op jit(solution)/shard_map/ppermute | solution.py:303
  38.9 5.6 %collective-permute-start.3 = (f32[16,1664]{1,0:T(8,128)S(1)}, f32[16,1664]{1,0:T(8,128)S(1)}, u32[]{:S(2)}, u32[]{:S(2)}) collective-permute-start(f32[16,1664]{1,0:T(8,128)S(1)} %other_columns.4), channel_id=1, source_target_pairs={{0,32},{32,0},{64,96},{96,64},{128,160},{160,128},{192,224},{224,1... | collective-permute-start | bytes 319496 | tf_op jit(solution)/shard_map/ppermute | solution.py:313
  44.5 6.7 %collective-permute-start.6 = (f32[16,1664]{1,0:T(8,128)S(1)}, f32[16,1664]{1,0:T(8,128)S(1)}, u32[]{:S(2)}, u32[]{:S(2)}) collective-permute-start(f32[16,1664]{1,0:T(8,128)S(1)} %add.8.refs_0_), channel_id=1, source_target_pairs={{0,192},{32,224},{64,0},{96,32},{128,64},{160,96},{192,128},{224,1... | collective-permute-start | bytes 319496 | tf_op jit(solution)/shard_map/ppermute | solution.py:316
  47.0 5.4 %collective-permute-start.5 = (f32[16,1664]{1,0:T(8,128)S(1)}, f32[16,1664]{1,0:T(8,128)S(1)}, u32[]{:S(2)}, u32[]{:S(2)}) collective-permute-start(f32[16,1664]{1,0:T(8,128)S(1)} %add.8.refs_0_), channel_id=1, source_target_pairs={{0,128},{32,160},{64,192},{96,224},{128,0},{160,32},{192,64},{224,... | collective-permute-start | bytes 319496 | tf_op jit(solution)/shard_map/ppermute | solution.py:316
  47.5 8.1 %collective-permute-start.4 = (f32[16,1664]{1,0:T(8,128)S(1)}, f32[16,1664]{1,0:T(8,128)S(1)}, u32[]{:S(2)}, u32[]{:S(2)}) collective-permute-start(f32[16,1664]{1,0:T(8,128)S(1)} %add.8.refs_0_), channel_id=1, source_target_pairs={{0,64},{32,96},{64,128},{96,160},{128,192},{160,224},{192,0},{224,... | collective-permute-start | bytes 319496 | tf_op jit(solution)/shard_map/ppermute | solution.py:316
  55.6 1.7 collective-permute-start.7
  67.0 5.7 %collective-permute-start.10 = (f32[4,1,1664]{2,1,0:T(1,128)S(1)}, f32[4,1,1664]{2,1,0:T(1,128)S(1)}, u32[]{:S(2)}, u32[]{:S(2)}) collective-permute-start(f32[4,1,1664]{2,1,0:T(1,128)S(1)} %collect.5.refs_0_), channel_id=1, source_target_pairs={{0,6},{1,7},{2,4},{3,5},{4,2},{5,3},{6,0},{7,1},{8,14},{9,15},{10,... | collective-permute-start | bytes 79880 | tf_op jit(solution)/shard_map/ppermute | solution.py:303
  68.8 6.6 %collective-permute-start.9 = (f32[4,1,1664]{2,1,0:T(1,128)S(1)}, f32[4,1,1664]{2,1,0:T(1,128)S(1)}, u32[]{:S(2)}, u32[]{:S(2)}) collective-permute-start(f32[4,1,1664]{2,1,0:T(1,128)S(1)} %collect.5.refs_0_), channel_id=1, source_target_pairs={{0,4},{1,5},{2,6},{3,7},{4,0},{5,1},{6,2},{7,3},{8,12},{9,13},{10,... | collective-permute-start | bytes 79880 | tf_op jit(solution)/shard_map/ppermute | solution.py:303
  71.8 3.6 %collective-permute-start.8 = (f32[4,1,1664]{2,1,0:T(1,128)S(1)}, f32[4,1,1664]{2,1,0:T(1,128)S(1)}, u32[]{:S(2)}, u32[]{:S(2)}) collective-permute-start(f32[4,1,1664]{2,1,0:T(1,128)S(1)} %collect.5.refs_0_), channel_id=1, source_target_pairs={{0,2},{1,3},{2,0},{3,1},{4,6},{5,7},{6,4},{7,5},{8,10},{9,11},{10,... | collective-permute-start | bytes 79880 | tf_op jit(solution)/shard_map/ppermute | solution.py:303
  85.9 4.7 %collective-permute-start.11 = (f32[16,1664]{1,0:T(8,128)S(1)}, f32[16,1664]{1,0:T(8,128)S(1)}, u32[]{:S(2)}, u32[]{:S(2)}) collective-permute-start(f32[16,1664]{1,0:T(8,128)S(1)} %other_columns.5), channel_id=1, source_target_pairs={{0,32},{32,0},{64,96},{96,64},{128,160},{160,128},{192,224},{224,1... | collective-permute-start | bytes 319496 | tf_op jit(solution)/shard_map/ppermute | solution.py:313
  90.6 4.3 %collective-permute-start.14 = (f32[16,1664]{1,0:T(8,128)S(1)}, f32[16,1664]{1,0:T(8,128)S(1)}, u32[]{:S(2)}, u32[]{:S(2)}) collective-permute-start(f32[16,1664]{1,0:T(8,128)S(1)} %add.10.refs_0_), channel_id=1, source_target_pairs={{0,192},{32,224},{64,0},{96,32},{128,64},{160,96},{192,128},{224,1... | collective-permute-start | bytes 319496 | tf_op jit(solution)/shard_map/ppermute | solution.py:316
  91.0 5.4 %collective-permute-start.13 = (f32[16,1664]{1,0:T(8,128)S(1)}, f32[16,1664]{1,0:T(8,128)S(1)}, u32[]{:S(2)}, u32[]{:S(2)}) collective-permute-start(f32[16,1664]{1,0:T(8,128)S(1)} %add.10.refs_0_), channel_id=1, source_target_pairs={{0,128},{32,160},{64,192},{96,224},{128,0},{160,32},{192,64},{224,... | collective-permute-start | bytes 319496 | tf_op jit(solution)/shard_map/ppermute | solution.py:316
  91.5 8.2 %collective-permute-start.12 = (f32[16,1664]{1,0:T(8,128)S(1)}, f32[16,1664]{1,0:T(8,128)S(1)}, u32[]{:S(2)}, u32[]{:S(2)}) collective-permute-start(f32[16,1664]{1,0:T(8,128)S(1)} %add.10.refs_0_), channel_id=1, source_target_pairs={{0,64},{32,96},{64,128},{96,160},{128,192},{160,224},{192,0},{224,... | collective-permute-start | bytes 319496 | tf_op jit(solution)/shard_map/ppermute | solution.py:316
  99.7 1.6 collective-permute-start.15
  110.9 5.7 %collective-permute-start.18 = (f32[4,1,1664]{2,1,0:T(1,128)S(1)}, f32[4,1,1664]{2,1,0:T(1,128)S(1)}, u32[]{:S(2)}, u32[]{:S(2)}) collective-permute-start(f32[4,1,1664]{2,1,0:T(1,128)S(1)} %collect.6.refs_0_), channel_id=1, source_target_pairs={{0,6},{1,7},{2,4},{3,5},{4,2},{5,3},{6,0},{7,1},{8,14},{9,15},{10,... | collective-permute-start | bytes 79880 | tf_op jit(solution)/shard_map/ppermute | solution.py:303
  112.4 6.9 %collective-permute-start.17 = (f32[4,1,1664]{2,1,0:T(1,128)S(1)}, f32[4,1,1664]{2,1,0:T(1,128)S(1)}, u32[]{:S(2)}, u32[]{:S(2)}) collective-permute-start(f32[4,1,1664]{2,1,0:T(1,128)S(1)} %collect.6.refs_0_), channel_id=1, source_target_pairs={{0,4},{1,5},{2,6},{3,7},{4,0},{5,1},{6,2},{7,3},{8,12},{9,13},{10,... | collective-permute-start | bytes 79880 | tf_op jit(solution)/shard_map/ppermute | solution.py:303
  115.0 4.3 %collective-permute-start.16 = (f32[4,1,1664]{2,1,0:T(1,128)S(1)}, f32[4,1,1664]{2,1,0:T(1,128)S(1)}, u32[]{:S(2)}, u32[]{:S(2)}) collective-permute-start(f32[4,1,1664]{2,1,0:T(1,128)S(1)} %collect.6.refs_0_), channel_id=1, source_target_pairs={{0,2},{1,3},{2,0},{3,1},{4,6},{5,7},{6,4},{7,5},{8,10},{9,11},{10,... | collective-permute-start | bytes 79880 | tf_op jit(solution)/shard_map/ppermute | solution.py:303
  128.6 5.0 %collective-permute-start.19 = (f32[16,1664]{1,0:T(8,128)S(1)}, f32[16,1664]{1,0:T(8,128)S(1)}, u32[]{:S(2)}, u32[]{:S(2)}) collective-permute-start(f32[16,1664]{1,0:T(8,128)S(1)} %other_columns.6), channel_id=1, source_target_pairs={{0,32},{32,0},{64,96},{96,64},{128,160},{160,128},{192,224},{224,1... | collective-permute-start | bytes 319496 | tf_op jit(solution)/shard_map/ppermute | solution.py:313
  133.7 4.3 %collective-permute-start.22 = (f32[16,1664]{1,0:T(8,128)S(1)}, f32[16,1664]{1,0:T(8,128)S(1)}, u32[]{:S(2)}, u32[]{:S(2)}) collective-permute-start(f32[16,1664]{1,0:T(8,128)S(1)} %add.12.refs_0_), channel_id=1, source_target_pairs={{0,192},{32,224},{64,0},{96,32},{128,64},{160,96},{192,128},{224,1... | collective-permute-start | bytes 319496 | tf_op jit(solution)/shard_map/ppermute | solution.py:316
  134.4 5.4 %collective-permute-start.21 = (f32[16,1664]{1,0:T(8,128)S(1)}, f32[16,1664]{1,0:T(8,128)S(1)}, u32[]{:S(2)}, u32[]{:S(2)}) collective-permute-start(f32[16,1664]{1,0:T(8,128)S(1)} %add.12.refs_0_), channel_id=1, source_target_pairs={{0,128},{32,160},{64,192},{96,224},{128,0},{160,32},{192,64},{224,... | collective-permute-start | bytes 319496 | tf_op jit(solution)/shard_map/ppermute | solution.py:316
  134.6 8.5 %collective-permute-start.20 = (f32[16,1664]{1,0:T(8,128)S(1)}, f32[16,1664]{1,0:T(8,128)S(1)}, u32[]{:S(2)}, u32[]{:S(2)}) collective-permute-start(f32[16,1664]{1,0:T(8,128)S(1)} %add.12.refs_0_), channel_id=1, source_target_pairs={{0,64},{32,96},{64,128},{96,160},{128,192},{160,224},{192,0},{224,... | collective-permute-start | bytes 319496 | tf_op jit(solution)/shard_map/ppermute | solution.py:316
  143.1 1.8 collective-permute-start.23
  154.5 5.7 %collective-permute-start.26 = (f32[4,1,1664]{2,1,0:T(1,128)S(1)}, f32[4,1,1664]{2,1,0:T(1,128)S(1)}, u32[]{:S(2)}, u32[]{:S(2)}) collective-permute-start(f32[4,1,1664]{2,1,0:T(1,128)S(1)} %collect.7.refs_0_), channel_id=1, source_target_pairs={{0,6},{1,7},{2,4},{3,5},{4,2},{5,3},{6,0},{7,1},{8,14},{9,15},{10,... | collective-permute-start | bytes 79880 | tf_op jit(solution)/shard_map/ppermute | solution.py:303
  156.6 6.9 %collective-permute-start.25 = (f32[4,1,1664]{2,1,0:T(1,128)S(1)}, f32[4,1,1664]{2,1,0:T(1,128)S(1)}, u32[]{:S(2)}, u32[]{:S(2)}) collective-permute-start(f32[4,1,1664]{2,1,0:T(1,128)S(1)} %collect.7.refs_0_), channel_id=1, source_target_pairs={{0,4},{1,5},{2,6},{3,7},{4,0},{5,1},{6,2},{7,3},{8,12},{9,13},{10,... | collective-permute-start | bytes 79880 | tf_op jit(solution)/shard_map/ppermute | solution.py:303
  159.8 3.7 %collective-permute-start.24 = (f32[4,1,1664]{2,1,0:T(1,128)S(1)}, f32[4,1,1664]{2,1,0:T(1,128)S(1)}, u32[]{:S(2)}, u32[]{:S(2)}) collective-permute-start(f32[4,1,1664]{2,1,0:T(1,128)S(1)} %collect.7.refs_0_), channel_id=1, source_target_pairs={{0,2},{1,3},{2,0},{3,1},{4,6},{5,7},{6,4},{7,5},{8,10},{9,11},{10,... | collective-permute-start | bytes 79880 | tf_op jit(solution)/shard_map/ppermute | solution.py:303
  173.7 4.7 %collective-permute-start.27 = (f32[16,1664]{1,0:T(8,128)S(1)}, f32[16,1664]{1,0:T(8,128)S(1)}, u32[]{:S(2)}, u32[]{:S(2)}) collective-permute-start(f32[16,1664]{1,0:T(8,128)S(1)} %other_columns.7), channel_id=1, source_target_pairs={{0,32},{32,0},{64,96},{96,64},{128,160},{160,128},{192,224},{224,1... | collective-permute-start | bytes 319496 | tf_op jit(solution)/shard_map/ppermute | solution.py:313
  178.4 4.3 %collective-permute-start.30 = (f32[16,1664]{1,0:T(8,128)S(1)}, f32[16,1664]{1,0:T(8,128)S(1)}, u32[]{:S(2)}, u32[]{:S(2)}) collective-permute-start(f32[16,1664]{1,0:T(8,128)S(1)} %add.14.refs_0_), channel_id=1, source_target_pairs={{0,192},{32,224},{64,0},{96,32},{128,64},{160,96},{192,128},{224,1... | collective-permute-start | bytes 319496 | tf_op jit(solution)/shard_map/ppermute | solution.py:316
  178.8 5.4 %collective-permute-start.29 = (f32[16,1664]{1,0:T(8,128)S(1)}, f32[16,1664]{1,0:T(8,128)S(1)}, u32[]{:S(2)}, u32[]{:S(2)}) collective-permute-start(f32[16,1664]{1,0:T(8,128)S(1)} %add.14.refs_0_), channel_id=1, source_target_pairs={{0,128},{32,160},{64,192},{96,224},{128,0},{160,32},{192,64},{224,... | collective-permute-start | bytes 319496 | tf_op jit(solution)/shard_map/ppermute | solution.py:316
  179.0 8.5 %collective-permute-start.28 = (f32[16,1664]{1,0:T(8,128)S(1)}, f32[16,1664]{1,0:T(8,128)S(1)}, u32[]{:S(2)}, u32[]{:S(2)}) collective-permute-start(f32[16,1664]{1,0:T(8,128)S(1)} %add.14.refs_0_), channel_id=1, source_target_pairs={{0,64},{32,96},{64,128},{96,160},{128,192},{160,224},{192,0},{224,... | collective-permute-start | bytes 319496 | tf_op jit(solution)/shard_map/ppermute | solution.py:316
  187.5 1.5 collective-permute-start.31

commit v4 on v3

--- a/solution.py
+++ b/solution.py
@@ -304,7 +304,7 @@
 
     def marker_sum(part):
         own = call(collect_kernel, "collect", f32(rhs // count, 1, part.shape[2]), [exchange(part)])
-        spread = call(spread_kernel, "spread", ext, [own] + [far(own, k) for k in range(2, DEPTH, 2)])
+        spread = call(spread_kernel, "spread", ext, [own] + [far(own, k) for k in (2, 6, 4)])
         return exchange(spread)
 
     swap = [(x * CORES + c, x * CORES + 1 - c) for x in range(xs) for c in range(CORES)]
@@ -314,7 +314,7 @@
 
     def shift(v, d):
         return lax.ppermute(
-            v, "animal", [(x * CORES + c, (x + d) % xs * CORES + c) for x in range(xs) for c in range(CORES)]
+            v, "animal", [(x * CORES + c, (x ^ d) * CORES + c) for x in range(xs) for c in range(CORES)]
         )
 
     solution = ()
@@ -333,7 +333,7 @@
         )
         old = [direction, *rows, kept]
         mine = call(add_kernel, "add", own, [mine, other])
-        mine = call(add_kernel, "add", own, [mine] + [shift(mine, d) for d in range(1, xs)])
+        mine = call(add_kernel, "add", own, [mine] + [shift(mine, d) for d in (1, 3, 2)])
         other = to_other(mine)
         state = [shrink, direction, residual, kept, *solution]
         if last:

time: 190 us -> 185 us (0.974)
  waiting for transfers between devices: 44.3 us -> 33.8 us
  starting transfers between devices: 51.7 us -> 57.6 us
    ppermute x12, waiting for transfers between devices: 30.3 us -> 19.4 us  [shift(): lax.ppermute(v, 'animal', [(x * CORES + c, (x ^ d) * CORES + c) for x in...]
    ppermute x12, starting transfers between devices: 8.32 us -> 14.5 us  [shift(): lax.ppermute(v, 'animal', [(x * CORES + c, (x ^ d) * CORES + c) for x in...]
  transfers between devices with their start and end apart: 32 -> 32, of which waited for: 17 -> 19; matrix products, arithmetic and copies ran while one was open for 0% -> 0% of each run, Pallas kernels for 4% -> 4%
where the time goes in v4:
time: 185 us; the launch traced here: 184 us
  blocking collectives  72.1 us (39%)
  starting transfers between devices  57.6 us (31%)
  waiting for transfers between devices  33.8 us (18%)
  Pallas kernels  19.8 us (11%)
    all_to_all x8, blocking collectives, exchange(): return lax.all_to_all(v, 'marker', 0, 0, tiled=True, axis_index_groups=near)  72.1 us
    ppermute x12, starting transfers between devices, far(): return lax.ppermute(v, 'marker', [(i, i ^ k) for i in range(ys * DEPTH)])  24.8 us
    ppermute x12, waiting for transfers between devices, shift(): lax.ppermute(v, 'animal', [(x * CORES + c, (x ^ d) * CORES + c) for x in...  19.4 us
    ppermute x8, starting transfers between devices, to_other(): return lax.ppermute(v, 'animal', swap)  18.4 us
    pallas_call x31, Pallas kernels, call(): pl.pallas_call(kernel, in_specs=[VMEM] * len(args), out_specs=jax.tree.ma...  14.9 us
    ppermute x12, starting transfers between devices, shift(): lax.ppermute(v, 'animal', [(x * CORES + c, (x ^ d) * CORES + c) for x in...  14.5 us
    ppermute x12, waiting for transfers between devices, far(): return lax.ppermute(v, 'marker', [(i, i ^ k) for i in range(ys * DEPTH)])  13.4 us
    pallas_call x1, Pallas kernels, body(): pl.pallas_call(first_kernel, in_specs=[ANY] * 4, out_specs=[VMEM] * 7, ou...  4.9 us
  transfers between devices with their start and end apart: 32, of which 19 were waited for; matrix products, arithmetic and copies ran while one was open for 0% of the time, Pallas kernels for 4%

profile of v4, /device:TPU:1, one launch (start us, length us, event | category | flops | bytes accessed | tf_op | source)
XLA Modules:
  0.0 184.2 jit_solution(10372174505258165976)
XLA Ops:
  0.6 4.9 %first_rows.1 = (bf16[1536,1536]{1,0:T(8,128)(2,1)S(1)}, bf16[1536,1536]{1,0:T(8,128)(2,1)S(1)}, f32[1,1536]{1,0:T(1,128)S(1)}, f32[1,1536]{1,0:T(1,128)S(1)}, f...) custom-call(f32[1536,1536]{1,0:T(8,128)} %geno_ref.1, f32[1536]{0:T(1024)} %freq_ref.1, ...), custom_call_target="tpu_custom_call" | custom-call | tf_op jit(solution)/shard_map/first_rows/pallas_call | solution.py:275
  5.5 12.2 %all_to_all.40.got_ref = f32[32,1,1664]{2,1,0:T(1,128)S(1)} all-to-all(f32[32,1,1664]{2,1,0:T(1,128)S(1)} %get-tuple-element.50), channel_id=1, replica_groups={{0,1,8,9,16,17,24,25},{2,3,10,11,18,19,26,27},{4,5,12,13,20,21,28,29},{..., dimensions={0} | all-to-all | bytes 425984 | tf_op jit(solution)/shard_map/all_to_all | solution.py:300
  17.7 6.1 %collective-permute-start.2 = (f32[4,1,1664]{2,1,0:T(1,128)S(1)}, f32[4,1,1664]{2,1,0:T(1,128)S(1)}, u32[]{:S(2)}, u32[]{:S(2)}) collective-permute-start(f32[4,1,1664]{2,1,0:T(1,128)S(1)} %collect.4.refs_0_), channel_id=1, source_target_pairs={{0,4},{1,5},{2,6},{3,7},{4,0},{5,1},{6,2},{7,3},{8,12},{9,13},{10,... | collective-permute-start | bytes 79880 | tf_op jit(solution)/shard_map/ppermute | solution.py:303
  24.1 0.9 collective-permute-start
  25.0 3.6 %collective-permute-done.1.refs_2_ = f32[4,1,1664]{2,1,0:T(1,128)S(1)} collective-permute-done((f32[4,1,1664]{2,1,0:T(1,128)S(1)}, f32[4,1,1664]{2,1,0:T(1,128)S(1)}, u32[]{:S(2)}, u32[]{:S(2)}) %collective-permute-start.1) | collective-permute-done | bytes 26656 | tf_op jit(solution)/shard_map/ppermute | solution.py:303
  28.6 8.3 %all_to_all.41.total_ref = f32[32,1,1664]{2,1,0:T(1,128)S(1)} all-to-all(f32[32,1,1664]{2,1,0:T(1,128)S(1)} %spread.4), channel_id=1, replica_groups={{0,1,8,9,16,17,24,25},{2,3,10,11,18,19,26,27},{4,5,12,13,20,21,28,29},{..., dimensions={0} | all-to-all | bytes 425984 | tf_op jit(solution)/shard_map/all_to_all | solution.py:300
  36.9 0.9 other_columns.4
  37.9 4.7 %collective-permute-start.3 = (f32[16,1664]{1,0:T(8,128)S(1)}, f32[16,1664]{1,0:T(8,128)S(1)}, u32[]{:S(2)}, u32[]{:S(2)}) collective-permute-start(f32[16,1664]{1,0:T(8,128)S(1)} %other_columns.4), channel_id=1, source_target_pairs={{0,32},{32,0},{64,96},{96,64},{128,160},{160,128},{192,224},{224,1... | collective-permute-start | bytes 319496 | tf_op jit(solution)/shard_map/ppermute | solution.py:313
  42.6 1.0 mine_columns.4
  43.6 2.8 %collective-permute-start.6 = (f32[16,1664]{1,0:T(8,128)S(1)}, f32[16,1664]{1,0:T(8,128)S(1)}, u32[]{:S(2)}, u32[]{:S(2)}) collective-permute-start(f32[16,1664]{1,0:T(8,128)S(1)} %add.8.refs_0_), channel_id=1, source_target_pairs={{0,128},{32,160},{64,192},{96,224},{128,0},{160,32},{192,64},{224,... | collective-permute-start | bytes 319496 | tf_op jit(solution)/shard_map/ppermute | solution.py:316
  46.4 0.9 collective-permute-start.5
  47.3 2.1 %collective-permute-done.6.refs_3_ = f32[16,1664]{1,0:T(8,128)S(1)} collective-permute-done((f32[16,1664]{1,0:T(8,128)S(1)}, f32[16,1664]{1,0:T(8,128)S(1)}, u32[]{:S(2)}, u32[]{:S(2)}) %collective-permute-start.6) | collective-permute-done | bytes 106528 | tf_op jit(solution)/shard_map/ppermute | solution.py:316
  49.4 2.1 %collective-permute-done.5.refs_2_ = f32[16,1664]{1,0:T(8,128)S(1)} collective-permute-done((f32[16,1664]{1,0:T(8,128)S(1)}, f32[16,1664]{1,0:T(8,128)S(1)}, u32[]{:S(2)}, u32[]{:S(2)}) %collective-permute-start.5) | collective-permute-done | bytes 106528 | tf_op jit(solution)/shard_map/ppermute | solution.py:316
  51.5 1.6 collective-permute-start.7
  53.1 1.0 mine_rows.3
  54.1 1.0 other_rows.3
  55.2 8.6 %all_to_all.42.got_ref = f32[32,1,1664]{2,1,0:T(1,128)S(1)} all-to-all(f32[32,1,1664]{2,1,0:T(1,128)S(1)} %get-tuple-element.62), channel_id=1, replica_groups={{0,1,8,9,16,17,24,25},{2,3,10,11,18,19,26,27},{4,5,12,13,20,21,28,29},{..., dimensions={0} | all-to-all | bytes 425984 | tf_op jit(solution)/shard_map/all_to_all | solution.py:300
  63.8 3.6 %collective-permute-start.10 = (f32[4,1,1664]{2,1,0:T(1,128)S(1)}, f32[4,1,1664]{2,1,0:T(1,128)S(1)}, u32[]{:S(2)}, u32[]{:S(2)}) collective-permute-start(f32[4,1,1664]{2,1,0:T(1,128)S(1)} %collect.5.refs_0_), channel_id=1, source_target_pairs={{0,4},{1,5},{2,6},{3,7},{4,0},{5,1},{6,2},{7,3},{8,12},{9,13},{10,... | collective-permute-start | bytes 79880 | tf_op jit(solution)/shard_map/ppermute | solution.py:303
  67.4 0.9 collective-permute-start.9
  68.3 1.2 collective-permute-start.8
  69.5 0.9 collective-permute-done.10.refs_3_
  70.5 2.1 %collective-permute-done.9.refs_2_ = f32[4,1,1664]{2,1,0:T(1,128)S(1)} collective-permute-done((f32[4,1,1664]{2,1,0:T(1,128)S(1)}, f32[4,1,1664]{2,1,0:T(1,128)S(1)}, u32[]{:S(2)}, u32[]{:S(2)}) %collective-permute-start.9) | collective-permute-done | bytes 26656 | tf_op jit(solution)/shard_map/ppermute | solution.py:303
  72.8 8.7 %all_to_all.43.total_ref = f32[32,1,1664]{2,1,0:T(1,128)S(1)} all-to-all(f32[32,1,1664]{2,1,0:T(1,128)S(1)} %spread.5), channel_id=1, replica_groups={{0,1,8,9,16,17,24,25},{2,3,10,11,18,19,26,27},{4,5,12,13,20,21,28,29},{..., dimensions={0} | all-to-all | bytes 425984 | tf_op jit(solution)/shard_map/all_to_all | solution.py:300
  81.5 0.9 other_columns.5
  82.4 3.4 %collective-permute-start.11 = (f32[16,1664]{1,0:T(8,128)S(1)}, f32[16,1664]{1,0:T(8,128)S(1)}, u32[]{:S(2)}, u32[]{:S(2)}) collective-permute-start(f32[16,1664]{1,0:T(8,128)S(1)} %other_columns.5), channel_id=1, source_target_pairs={{0,32},{32,0},{64,96},{96,64},{128,160},{160,128},{192,224},{224,1... | collective-permute-start | bytes 319496 | tf_op jit(solution)/shard_map/ppermute | solution.py:313
  85.9 1.0 mine_columns.5
  86.9 1.8 collective-permute-start.14
  88.6 1.8 collective-permute-start.13
  90.5 2.2 %collective-permute-done.14.refs_3_ = f32[16,1664]{1,0:T(8,128)S(1)} collective-permute-done((f32[16,1664]{1,0:T(8,128)S(1)}, f32[16,1664]{1,0:T(8,128)S(1)}, u32[]{:S(2)}, u32[]{:S(2)}) %collective-permute-start.14) | collective-permute-done | bytes 106528 | tf_op jit(solution)/shard_map/ppermute | solution.py:316
  92.7 2.8 %collective-permute-done.13.refs_2_ = f32[16,1664]{1,0:T(8,128)S(1)} collective-permute-done((f32[16,1664]{1,0:T(8,128)S(1)}, f32[16,1664]{1,0:T(8,128)S(1)}, u32[]{:S(2)}, u32[]{:S(2)}) %collective-permute-start.13) | collective-permute-done | bytes 106528 | tf_op jit(solution)/shard_map/ppermute | solution.py:316
  96.2 1.0 mine_rows.4
  97.3 1.0 other_rows.4
  98.3 8.6 %all_to_all.44.got_ref = f32[32,1,1664]{2,1,0:T(1,128)S(1)} all-to-all(f32[32,1,1664]{2,1,0:T(1,128)S(1)} %get-tuple-element.74), channel_id=1, replica_groups={{0,1,8,9,16,17,24,25},{2,3,10,11,18,19,26,27},{4,5,12,13,20,21,28,29},{..., dimensions={0} | all-to-all | bytes 425984 | tf_op jit(solution)/shard_map/all_to_all | solution.py:300
  106.9 3.6 %collective-permute-start.18 = (f32[4,1,1664]{2,1,0:T(1,128)S(1)}, f32[4,1,1664]{2,1,0:T(1,128)S(1)}, u32[]{:S(2)}, u32[]{:S(2)}) collective-permute-start(f32[4,1,1664]{2,1,0:T(1,128)S(1)} %collect.6.refs_0_), channel_id=1, source_target_pairs={{0,4},{1,5},{2,6},{3,7},{4,0},{5,1},{6,2},{7,3},{8,12},{9,13},{10,... | collective-permute-start | bytes 79880 | tf_op jit(solution)/shard_map/ppermute | solution.py:303
  110.5 0.9 collective-permute-start.17
  111.4 1.2 collective-permute-start.16
  112.6 0.9 collective-permute-done.18.refs_3_
  113.6 2.0 %collective-permute-done.17.refs_2_ = f32[4,1,1664]{2,1,0:T(1,128)S(1)} collective-permute-done((f32[4,1,1664]{2,1,0:T(1,128)S(1)}, f32[4,1,1664]{2,1,0:T(1,128)S(1)}, u32[]{:S(2)}, u32[]{:S(2)}) %collective-permute-start.17) | collective-permute-done | bytes 26656 | tf_op jit(solution)/shard_map/ppermute | solution.py:303
  115.9 8.7 %all_to_all.45.total_ref = f32[32,1,1664]{2,1,0:T(1,128)S(1)} all-to-all(f32[32,1,1664]{2,1,0:T(1,128)S(1)} %spread.6), channel_id=1, replica_groups={{0,1,8,9,16,17,24,25},{2,3,10,11,18,19,26,27},{4,5,12,13,20,21,28,29},{..., dimensions={0} | all-to-all | bytes 425984 | tf_op jit(solution)/shard_map/all_to_all | solution.py:300
  124.6 0.9 other_columns.6
  125.5 3.3 %collective-permute-start.19 = (f32[16,1664]{1,0:T(8,128)S(1)}, f32[16,1664]{1,0:T(8,128)S(1)}, u32[]{:S(2)}, u32[]{:S(2)}) collective-permute-start(f32[16,1664]{1,0:T(8,128)S(1)} %other_columns.6), channel_id=1, source_target_pairs={{0,32},{32,0},{64,96},{96,64},{128,160},{160,128},{192,224},{224,1... | collective-permute-start | bytes 319496 | tf_op jit(solution)/shard_map/ppermute | solution.py:313
  128.8 1.0 mine_columns.6
  129.8 1.8 collective-permute-start.22
  131.6 1.8 collective-permute-start.21
  133.4 2.2 %collective-permute-done.22.refs_3_ = f32[16,1664]{1,0:T(8,128)S(1)} collective-permute-done((f32[16,1664]{1,0:T(8,128)S(1)}, f32[16,1664]{1,0:T(8,128)S(1)}, u32[]{:S(2)}, u32[]{:S(2)}) %collective-permute-start.22) | collective-permute-done | bytes 106528 | tf_op jit(solution)/shard_map/ppermute | solution.py:316
  135.6 2.8 %collective-permute-done.21.refs_2_ = f32[16,1664]{1,0:T(8,128)S(1)} collective-permute-done((f32[16,1664]{1,0:T(8,128)S(1)}, f32[16,1664]{1,0:T(8,128)S(1)}, u32[]{:S(2)}, u32[]{:S(2)}) %collective-permute-start.21) | collective-permute-done | bytes 106528 | tf_op jit(solution)/shard_map/ppermute | solution.py:316
  139.2 1.0 mine_rows.5
  140.2 1.0 other_rows.5
  141.2 8.6 %all_to_all.46.got_ref = f32[32,1,1664]{2,1,0:T(1,128)S(1)} all-to-all(f32[32,1,1664]{2,1,0:T(1,128)S(1)} %get-tuple-element.86), channel_id=1, replica_groups={{0,1,8,9,16,17,24,25},{2,3,10,11,18,19,26,27},{4,5,12,13,20,21,28,29},{..., dimensions={0} | all-to-all | bytes 425984 | tf_op jit(solution)/shard_map/all_to_all | solution.py:300
  149.8 3.9 %collective-permute-start.26 = (f32[4,1,1664]{2,1,0:T(1,128)S(1)}, f32[4,1,1664]{2,1,0:T(1,128)S(1)}, u32[]{:S(2)}, u32[]{:S(2)}) collective-permute-start(f32[4,1,1664]{2,1,0:T(1,128)S(1)} %collect.7.refs_0_), channel_id=1, source_target_pairs={{0,4},{1,5},{2,6},{3,7},{4,0},{5,1},{6,2},{7,3},{8,12},{9,13},{10,... | collective-permute-start | bytes 79880 | tf_op jit(solution)/shard_map/ppermute | solution.py:303
  153.7 0.9 collective-permute-start.25
  154.6 1.2 collective-permute-start.24
  155.8 0.9 collective-permute-done.26.refs_3_
  156.8 2.1 %collective-permute-done.25.refs_2_ = f32[4,1,1664]{2,1,0:T(1,128)S(1)} collective-permute-done((f32[4,1,1664]{2,1,0:T(1,128)S(1)}, f32[4,1,1664]{2,1,0:T(1,128)S(1)}, u32[]{:S(2)}, u32[]{:S(2)}) %collective-permute-start.25) | collective-permute-done | bytes 26656 | tf_op jit(solution)/shard_map/ppermute | solution.py:303
  159.1 8.7 %all_to_all.47.total_ref = f32[32,1,1664]{2,1,0:T(1,128)S(1)} all-to-all(f32[32,1,1664]{2,1,0:T(1,128)S(1)} %spread.7), channel_id=1, replica_groups={{0,1,8,9,16,17,24,25},{2,3,10,11,18,19,26,27},{4,5,12,13,20,21,28,29},{..., dimensions={0} | all-to-all | bytes 425984 | tf_op jit(solution)/shard_map/all_to_all | solution.py:300
  167.8 0.9 other_columns.7
  168.7 3.3 %collective-permute-start.27 = (f32[16,1664]{1,0:T(8,128)S(1)}, f32[16,1664]{1,0:T(8,128)S(1)}, u32[]{:S(2)}, u32[]{:S(2)}) collective-permute-start(f32[16,1664]{1,0:T(8,128)S(1)} %other_columns.7), channel_id=1, source_target_pairs={{0,32},{32,0},{64,96},{96,64},{128,160},{160,128},{192,224},{224,1... | collective-permute-start | bytes 319496 | tf_op jit(solution)/shard_map/ppermute | solution.py:313
  172.0 0.9 mine_columns.7
  173.0 1.8 collective-permute-start.30
  174.8 1.8 collective-permute-start.29
  176.6 2.2 %collective-permute-done.30.refs_3_ = f32[16,1664]{1,0:T(8,128)S(1)} collective-permute-done((f32[16,1664]{1,0:T(8,128)S(1)}, f32[16,1664]{1,0:T(8,128)S(1)}, u32[]{:S(2)}, u32[]{:S(2)}) %collective-permute-start.30) | collective-permute-done | bytes 106528 | tf_op jit(solution)/shard_map/ppermute | solution.py:316
  178.7 2.8 %collective-permute-done.29.refs_2_ = f32[16,1664]{1,0:T(8,128)S(1)} collective-permute-done((f32[16,1664]{1,0:T(8,128)S(1)}, f32[16,1664]{1,0:T(8,128)S(1)}, u32[]{:S(2)}, u32[]{:S(2)}) %collective-permute-start.29) | collective-permute-done | bytes 106528 | tf_op jit(solution)/shard_map/ppermute | solution.py:316
  182.3 1.0 collective-permute-done.31.other_ref
  183.3 0.9 last.1
  (40 shorter events, 3.6 us)
Async XLA Ops:
  17.7 7.3 %collective-permute-start.2 = (f32[4,1,1664]{2,1,0:T(1,128)S(1)}, f32[4,1,1664]{2,1,0:T(1,128)S(1)}, u32[]{:S(2)}, u32[]{:S(2)}) collective-permute-start(f32[4,1,1664]{2,1,0:T(1,128)S(1)} %collect.4.refs_0_), channel_id=1, source_target_pairs={{0,4},{1,5},{2,6},{3,7},{4,0},{5,1},{6,2},{7,3},{8,12},{9,13},{10,... | collective-permute-start | bytes 79880 | tf_op jit(solution)/shard_map/ppermute | solution.py:303
  23.8 4.8 %collective-permute-start.1 = (f32[4,1,1664]{2,1,0:T(1,128)S(1)}, f32[4,1,1664]{2,1,0:T(1,128)S(1)}, u32[]{:S(2)}, u32[]{:S(2)}) collective-permute-start(f32[4,1,1664]{2,1,0:T(1,128)S(1)} %collect.4.refs_0_), channel_id=1, source_target_pairs={{0,6},{1,7},{2,4},{3,5},{4,2},{5,3},{6,0},{7,1},{8,14},{9,15},{10,... | collective-permute-start | bytes 79880 | tf_op jit(solution)/shard_map/ppermute | solution.py:303
  24.1 4.5 %collective-permute-start = (f32[4,1,1664]{2,1,0:T(1,128)S(1)}, f32[4,1,1664]{2,1,0:T(1,128)S(1)}, u32[]{:S(2)}, u32[]{:S(2)}) collective-permute-start(f32[4,1,1664]{2,1,0:T(1,128)S(1)} %collect.4.refs_0_), channel_id=1, source_target_pairs={{0,2},{1,3},{2,0},{3,1},{4,6},{5,7},{6,4},{7,5},{8,10},{9,11},{10,... | collective-permute-start | bytes 79880 | tf_op jit(solution)/shard_map/ppermute | solution.py:303
  37.9 5.7 %collective-permute-start.3 = (f32[16,1664]{1,0:T(8,128)S(1)}, f32[16,1664]{1,0:T(8,128)S(1)}, u32[]{:S(2)}, u32[]{:S(2)}) collective-permute-start(f32[16,1664]{1,0:T(8,128)S(1)} %other_columns.4), channel_id=1, source_target_pairs={{0,32},{32,0},{64,96},{96,64},{128,160},{160,128},{192,224},{224,1... | collective-permute-start | bytes 319496 | tf_op jit(solution)/shard_map/ppermute | solution.py:313
  43.6 5.8 %collective-permute-start.6 = (f32[16,1664]{1,0:T(8,128)S(1)}, f32[16,1664]{1,0:T(8,128)S(1)}, u32[]{:S(2)}, u32[]{:S(2)}) collective-permute-start(f32[16,1664]{1,0:T(8,128)S(1)} %add.8.refs_0_), channel_id=1, source_target_pairs={{0,128},{32,160},{64,192},{96,224},{128,0},{160,32},{192,64},{224,... | collective-permute-start | bytes 319496 | tf_op jit(solution)/shard_map/ppermute | solution.py:316
  46.4 5.1 %collective-permute-start.5 = (f32[16,1664]{1,0:T(8,128)S(1)}, f32[16,1664]{1,0:T(8,128)S(1)}, u32[]{:S(2)}, u32[]{:S(2)}) collective-permute-start(f32[16,1664]{1,0:T(8,128)S(1)} %add.8.refs_0_), channel_id=1, source_target_pairs={{0,192},{32,224},{64,128},{96,160},{128,64},{160,96},{192,0},{224,... | collective-permute-start | bytes 319496 | tf_op jit(solution)/shard_map/ppermute | solution.py:316
  47.3 4.3 %collective-permute-start.4 = (f32[16,1664]{1,0:T(8,128)S(1)}, f32[16,1664]{1,0:T(8,128)S(1)}, u32[]{:S(2)}, u32[]{:S(2)}) collective-permute-start(f32[16,1664]{1,0:T(8,128)S(1)} %add.8.refs_0_), channel_id=1, source_target_pairs={{0,64},{32,96},{64,0},{96,32},{128,192},{160,224},{192,128},{224,1... | collective-permute-start | bytes 319496 | tf_op jit(solution)/shard_map/ppermute | solution.py:316
  51.5 2.6 %collective-permute-start.7 = (f32[16,1664]{1,0:T(8,128)S(1)}, f32[16,1664]{1,0:T(8,128)S(1)}, u32[]{:S(2)}, u32[]{:S(2)}) collective-permute-start(f32[16,1664]{1,0:T(8,128)S(1)} %add.9.refs_0_), channel_id=1, source_target_pairs={{0,32},{32,0},{64,96},{96,64},{128,160},{160,128},{192,224},{224,1... | collective-permute-start | bytes 319496 | tf_op jit(solution)/shard_map/ppermute | solution.py:313
  63.8 6.7 %collective-permute-start.10 = (f32[4,1,1664]{2,1,0:T(1,128)S(1)}, f32[4,1,1664]{2,1,0:T(1,128)S(1)}, u32[]{:S(2)}, u32[]{:S(2)}) collective-permute-start(f32[4,1,1664]{2,1,0:T(1,128)S(1)} %collect.5.refs_0_), channel_id=1, source_target_pairs={{0,4},{1,5},{2,6},{3,7},{4,0},{5,1},{6,2},{7,3},{8,12},{9,13},{10,... | collective-permute-start | bytes 79880 | tf_op jit(solution)/shard_map/ppermute | solution.py:303
  67.4 5.1 %collective-permute-start.9 = (f32[4,1,1664]{2,1,0:T(1,128)S(1)}, f32[4,1,1664]{2,1,0:T(1,128)S(1)}, u32[]{:S(2)}, u32[]{:S(2)}) collective-permute-start(f32[4,1,1664]{2,1,0:T(1,128)S(1)} %collect.5.refs_0_), channel_id=1, source_target_pairs={{0,6},{1,7},{2,4},{3,5},{4,2},{5,3},{6,0},{7,1},{8,14},{9,15},{10,... | collective-permute-start | bytes 79880 | tf_op jit(solution)/shard_map/ppermute | solution.py:303
  68.3 4.5 %collective-permute-start.8 = (f32[4,1,1664]{2,1,0:T(1,128)S(1)}, f32[4,1,1664]{2,1,0:T(1,128)S(1)}, u32[]{:S(2)}, u32[]{:S(2)}) collective-permute-start(f32[4,1,1664]{2,1,0:T(1,128)S(1)} %collect.5.refs_0_), channel_id=1, source_target_pairs={{0,2},{1,3},{2,0},{3,1},{4,6},{5,7},{6,4},{7,5},{8,10},{9,11},{10,... | collective-permute-start | bytes 79880 | tf_op jit(solution)/shard_map/ppermute | solution.py:303
  82.4 4.4 %collective-permute-start.11 = (f32[16,1664]{1,0:T(8,128)S(1)}, f32[16,1664]{1,0:T(8,128)S(1)}, u32[]{:S(2)}, u32[]{:S(2)}) collective-permute-start(f32[16,1664]{1,0:T(8,128)S(1)} %other_columns.5), channel_id=1, source_target_pairs={{0,32},{32,0},{64,96},{96,64},{128,160},{160,128},{192,224},{224,1... | collective-permute-start | bytes 319496 | tf_op jit(solution)/shard_map/ppermute | solution.py:313
  86.9 5.8 %collective-permute-start.14 = (f32[16,1664]{1,0:T(8,128)S(1)}, f32[16,1664]{1,0:T(8,128)S(1)}, u32[]{:S(2)}, u32[]{:S(2)}) collective-permute-start(f32[16,1664]{1,0:T(8,128)S(1)} %add.10.refs_0_), channel_id=1, source_target_pairs={{0,128},{32,160},{64,192},{96,224},{128,0},{160,32},{192,64},{224,... | collective-permute-start | bytes 319496 | tf_op jit(solution)/shard_map/ppermute | solution.py:316
  88.6 6.9 %collective-permute-start.13 = (f32[16,1664]{1,0:T(8,128)S(1)}, f32[16,1664]{1,0:T(8,128)S(1)}, u32[]{:S(2)}, u32[]{:S(2)}) collective-permute-start(f32[16,1664]{1,0:T(8,128)S(1)} %add.10.refs_0_), channel_id=1, source_target_pairs={{0,192},{32,224},{64,128},{96,160},{128,64},{160,96},{192,0},{224,... | collective-permute-start | bytes 319496 | tf_op jit(solution)/shard_map/ppermute | solution.py:316
  90.5 5.1 %collective-permute-start.12 = (f32[16,1664]{1,0:T(8,128)S(1)}, f32[16,1664]{1,0:T(8,128)S(1)}, u32[]{:S(2)}, u32[]{:S(2)}) collective-permute-start(f32[16,1664]{1,0:T(8,128)S(1)} %add.10.refs_0_), channel_id=1, source_target_pairs={{0,64},{32,96},{64,0},{96,32},{128,192},{160,224},{192,128},{224,1... | collective-permute-start | bytes 319496 | tf_op jit(solution)/shard_map/ppermute | solution.py:316
  95.6 1.7 collective-permute-start.15
  106.9 6.7 %collective-permute-start.18 = (f32[4,1,1664]{2,1,0:T(1,128)S(1)}, f32[4,1,1664]{2,1,0:T(1,128)S(1)}, u32[]{:S(2)}, u32[]{:S(2)}) collective-permute-start(f32[4,1,1664]{2,1,0:T(1,128)S(1)} %collect.6.refs_0_), channel_id=1, source_target_pairs={{0,4},{1,5},{2,6},{3,7},{4,0},{5,1},{6,2},{7,3},{8,12},{9,13},{10,... | collective-permute-start | bytes 79880 | tf_op jit(solution)/shard_map/ppermute | solution.py:303
  110.5 5.1 %collective-permute-start.17 = (f32[4,1,1664]{2,1,0:T(1,128)S(1)}, f32[4,1,1664]{2,1,0:T(1,128)S(1)}, u32[]{:S(2)}, u32[]{:S(2)}) collective-permute-start(f32[4,1,1664]{2,1,0:T(1,128)S(1)} %collect.6.refs_0_), channel_id=1, source_target_pairs={{0,6},{1,7},{2,4},{3,5},{4,2},{5,3},{6,0},{7,1},{8,14},{9,15},{10,... | collective-permute-start | bytes 79880 | tf_op jit(solution)/shard_map/ppermute | solution.py:303
  111.4 4.5 %collective-permute-start.16 = (f32[4,1,1664]{2,1,0:T(1,128)S(1)}, f32[4,1,1664]{2,1,0:T(1,128)S(1)}, u32[]{:S(2)}, u32[]{:S(2)}) collective-permute-start(f32[4,1,1664]{2,1,0:T(1,128)S(1)} %collect.6.refs_0_), channel_id=1, source_target_pairs={{0,2},{1,3},{2,0},{3,1},{4,6},{5,7},{6,4},{7,5},{8,10},{9,11},{10,... | collective-permute-start | bytes 79880 | tf_op jit(solution)/shard_map/ppermute | solution.py:303
  125.5 4.3 %collective-permute-start.19 = (f32[16,1664]{1,0:T(8,128)S(1)}, f32[16,1664]{1,0:T(8,128)S(1)}, u32[]{:S(2)}, u32[]{:S(2)}) collective-permute-start(f32[16,1664]{1,0:T(8,128)S(1)} %other_columns.6), channel_id=1, source_target_pairs={{0,32},{32,0},{64,96},{96,64},{128,160},{160,128},{192,224},{224,1... | collective-permute-start | bytes 319496 | tf_op jit(solution)/shard_map/ppermute | solution.py:313
  129.8 5.8 %collective-permute-start.22 = (f32[16,1664]{1,0:T(8,128)S(1)}, f32[16,1664]{1,0:T(8,128)S(1)}, u32[]{:S(2)}, u32[]{:S(2)}) collective-permute-start(f32[16,1664]{1,0:T(8,128)S(1)} %add.12.refs_0_), channel_id=1, source_target_pairs={{0,128},{32,160},{64,192},{96,224},{128,0},{160,32},{192,64},{224,... | collective-permute-start | bytes 319496 | tf_op jit(solution)/shard_map/ppermute | solution.py:316
  131.6 6.9 %collective-permute-start.21 = (f32[16,1664]{1,0:T(8,128)S(1)}, f32[16,1664]{1,0:T(8,128)S(1)}, u32[]{:S(2)}, u32[]{:S(2)}) collective-permute-start(f32[16,1664]{1,0:T(8,128)S(1)} %add.12.refs_0_), channel_id=1, source_target_pairs={{0,192},{32,224},{64,128},{96,160},{128,64},{160,96},{192,0},{224,... | collective-permute-start | bytes 319496 | tf_op jit(solution)/shard_map/ppermute | solution.py:316
  133.4 5.1 %collective-permute-start.20 = (f32[16,1664]{1,0:T(8,128)S(1)}, f32[16,1664]{1,0:T(8,128)S(1)}, u32[]{:S(2)}, u32[]{:S(2)}) collective-permute-start(f32[16,1664]{1,0:T(8,128)S(1)} %add.12.refs_0_), channel_id=1, source_target_pairs={{0,64},{32,96},{64,0},{96,32},{128,192},{160,224},{192,128},{224,1... | collective-permute-start | bytes 319496 | tf_op jit(solution)/shard_map/ppermute | solution.py:316
  138.5 1.7 collective-permute-start.23
  149.8 6.9 %collective-permute-start.26 = (f32[4,1,1664]{2,1,0:T(1,128)S(1)}, f32[4,1,1664]{2,1,0:T(1,128)S(1)}, u32[]{:S(2)}, u32[]{:S(2)}) collective-permute-start(f32[4,1,1664]{2,1,0:T(1,128)S(1)} %collect.7.refs_0_), channel_id=1, source_target_pairs={{0,4},{1,5},{2,6},{3,7},{4,0},{5,1},{6,2},{7,3},{8,12},{9,13},{10,... | collective-permute-start | bytes 79880 | tf_op jit(solution)/shard_map/ppermute | solution.py:303
  153.7 5.1 %collective-permute-start.25 = (f32[4,1,1664]{2,1,0:T(1,128)S(1)}, f32[4,1,1664]{2,1,0:T(1,128)S(1)}, u32[]{:S(2)}, u32[]{:S(2)}) collective-permute-start(f32[4,1,1664]{2,1,0:T(1,128)S(1)} %collect.7.refs_0_), channel_id=1, source_target_pairs={{0,6},{1,7},{2,4},{3,5},{4,2},{5,3},{6,0},{7,1},{8,14},{9,15},{10,... | collective-permute-start | bytes 79880 | tf_op jit(solution)/shard_map/ppermute | solution.py:303
  154.6 4.5 %collective-permute-start.24 = (f32[4,1,1664]{2,1,0:T(1,128)S(1)}, f32[4,1,1664]{2,1,0:T(1,128)S(1)}, u32[]{:S(2)}, u32[]{:S(2)}) collective-permute-start(f32[4,1,1664]{2,1,0:T(1,128)S(1)} %collect.7.refs_0_), channel_id=1, source_target_pairs={{0,2},{1,3},{2,0},{3,1},{4,6},{5,7},{6,4},{7,5},{8,10},{9,11},{10,... | collective-permute-start | bytes 79880 | tf_op jit(solution)/shard_map/ppermute | solution.py:303
  168.7 4.2 %collective-permute-start.27 = (f32[16,1664]{1,0:T(8,128)S(1)}, f32[16,1664]{1,0:T(8,128)S(1)}, u32[]{:S(2)}, u32[]{:S(2)}) collective-permute-start(f32[16,1664]{1,0:T(8,128)S(1)} %other_columns.7), channel_id=1, source_target_pairs={{0,32},{32,0},{64,96},{96,64},{128,160},{160,128},{192,224},{224,1... | collective-permute-start | bytes 319496 | tf_op jit(solution)/shard_map/ppermute | solution.py:313
  173.0 5.8 %collective-permute-start.30 = (f32[16,1664]{1,0:T(8,128)S(1)}, f32[16,1664]{1,0:T(8,128)S(1)}, u32[]{:S(2)}, u32[]{:S(2)}) collective-permute-start(f32[16,1664]{1,0:T(8,128)S(1)} %add.14.refs_0_), channel_id=1, source_target_pairs={{0,128},{32,160},{64,192},{96,224},{128,0},{160,32},{192,64},{224,... | collective-permute-start | bytes 319496 | tf_op jit(solution)/shard_map/ppermute | solution.py:316
  174.8 6.8 %collective-permute-start.29 = (f32[16,1664]{1,0:T(8,128)S(1)}, f32[16,1664]{1,0:T(8,128)S(1)}, u32[]{:S(2)}, u32[]{:S(2)}) collective-permute-start(f32[16,1664]{1,0:T(8,128)S(1)} %add.14.refs_0_), channel_id=1, source_target_pairs={{0,192},{32,224},{64,128},{96,160},{128,64},{160,96},{192,0},{224,... | collective-permute-start | bytes 319496 | tf_op jit(solution)/shard_map/ppermute | solution.py:316
  176.6 5.0 %collective-permute-start.28 = (f32[16,1664]{1,0:T(8,128)S(1)}, f32[16,1664]{1,0:T(8,128)S(1)}, u32[]{:S(2)}, u32[]{:S(2)}) collective-permute-start(f32[16,1664]{1,0:T(8,128)S(1)} %add.14.refs_0_), channel_id=1, source_target_pairs={{0,64},{32,96},{64,0},{96,32},{128,192},{160,224},{192,128},{224,1... | collective-permute-start | bytes 319496 | tf_op jit(solution)/shard_map/ppermute | solution.py:316
  181.6 1.7 collective-permute-start.31

commit v5 on v4

--- a/solution.py
+++ b/solution.py
@@ -293,7 +293,7 @@
     coded, turned = (pltpu.with_memory_space_constraint(v, pltpu.VMEM) for v in (coded, turned))
 
     ys = lax.axis_size("marker") // DEPTH
-    near = [[y * DEPTH + z + o for y in range(ys) for o in range(2)] for z in range(0, DEPTH, 2)]
+    near = [[y * DEPTH + z + o for o in range(2) for y in (0, 2, 1, 3)] for z in range(0, DEPTH, 2)]
     count = 2 * ys
 
     def exchange(v):

time: 185 us -> 184 us (level)
  no operation moved by 1% of the time
where the time goes in v5:
time: 184 us
  blocking collectives  71.1 us (39%)
  starting transfers between devices  58 us (32%)
  waiting for transfers between devices  33.8 us (18%)
  Pallas kernels  19.8 us (11%)
    all_to_all x8, blocking collectives, exchange(): return lax.all_to_all(v, 'marker', 0, 0, tiled=True, axis_index_groups=near)  71.1 us
    ppermute x12, starting transfers between devices, far(): return lax.ppermute(v, 'marker', [(i, i ^ k) for i in range(ys * DEPTH)])  24.7 us
    ppermute x12, waiting for transfers between devices, shift(): lax.ppermute(v, 'animal', [(x * CORES + c, (x ^ d) * CORES + c) for x in...  19.4 us
    ppermute x8, starting transfers between devices, to_other(): return lax.ppermute(v, 'animal', swap)  18.8 us
    pallas_call x31, Pallas kernels, call(): pl.pallas_call(kernel, in_specs=[VMEM] * len(args), out_specs=jax.tree.ma...  14.9 us
    ppermute x12, starting transfers between devices, shift(): lax.ppermute(v, 'animal', [(x * CORES + c, (x ^ d) * CORES + c) for x in...  14.5 us
    ppermute x12, waiting for transfers between devices, far(): return lax.ppermute(v, 'marker', [(i, i ^ k) for i in range(ys * DEPTH)])  13.4 us
    pallas_call x1, Pallas kernels, body(): pl.pallas_call(first_kernel, in_specs=[ANY] * 4, out_specs=[VMEM] * 7, ou...  4.9 us
  transfers between devices with their start and end apart: 32, of which 19 were waited for; matrix products, arithmetic and copies ran while one was open for 0% of the time, Pallas kernels for 4%

profile of v5, /device:TPU:1, one launch (start us, length us, event | category | flops | bytes accessed | tf_op | source)
XLA Modules:
  0.0 183.5 jit_solution(6761490154264618705)
XLA Ops:
  0.6 4.9 %first_rows.1 = (bf16[1536,1536]{1,0:T(8,128)(2,1)S(1)}, bf16[1536,1536]{1,0:T(8,128)(2,1)S(1)}, f32[1,1536]{1,0:T(1,128)S(1)}, f32[1,1536]{1,0:T(1,128)S(1)}, f...) custom-call(f32[1536,1536]{1,0:T(8,128)} %geno_ref.1, f32[1536]{0:T(1024)} %freq_ref.1, ...), custom_call_target="tpu_custom_call" | custom-call | tf_op jit(solution)/shard_map/first_rows/pallas_call | solution.py:275
  5.5 11.8 %all_to_all.40.got_ref = f32[32,1,1664]{2,1,0:T(1,128)S(1)} all-to-all(f32[32,1,1664]{2,1,0:T(1,128)S(1)} %get-tuple-element.50), channel_id=1, replica_groups={{0,16,8,24,1,17,9,25},{2,18,10,26,3,19,11,27},{4,20,12,28,5,21,13,29},{..., dimensions={0} | all-to-all | bytes 425984 | tf_op jit(solution)/shard_map/all_to_all | solution.py:300
  17.4 6.1 %collective-permute-start.2 = (f32[4,1,1664]{2,1,0:T(1,128)S(1)}, f32[4,1,1664]{2,1,0:T(1,128)S(1)}, u32[]{:S(2)}, u32[]{:S(2)}) collective-permute-start(f32[4,1,1664]{2,1,0:T(1,128)S(1)} %collect.4.refs_0_), channel_id=1, source_target_pairs={{0,4},{1,5},{2,6},{3,7},{4,0},{5,1},{6,2},{7,3},{8,12},{9,13},{10,... | collective-permute-start | bytes 79880 | tf_op jit(solution)/shard_map/ppermute | solution.py:303
  23.7 0.9 collective-permute-start
  24.7 3.6 %collective-permute-done.1.refs_2_ = f32[4,1,1664]{2,1,0:T(1,128)S(1)} collective-permute-done((f32[4,1,1664]{2,1,0:T(1,128)S(1)}, f32[4,1,1664]{2,1,0:T(1,128)S(1)}, u32[]{:S(2)}, u32[]{:S(2)}) %collective-permute-start.1) | collective-permute-done | bytes 26656 | tf_op jit(solution)/shard_map/ppermute | solution.py:303
  28.3 8.4 %all_to_all.41.total_ref = f32[32,1,1664]{2,1,0:T(1,128)S(1)} all-to-all(f32[32,1,1664]{2,1,0:T(1,128)S(1)} %spread.4), channel_id=1, replica_groups={{0,16,8,24,1,17,9,25},{2,18,10,26,3,19,11,27},{4,20,12,28,5,21,13,29},{..., dimensions={0} | all-to-all | bytes 425984 | tf_op jit(solution)/shard_map/all_to_all | solution.py:300
  36.7 0.9 other_columns.4
  37.6 4.7 %collective-permute-start.3 = (f32[16,1664]{1,0:T(8,128)S(1)}, f32[16,1664]{1,0:T(8,128)S(1)}, u32[]{:S(2)}, u32[]{:S(2)}) collective-permute-start(f32[16,1664]{1,0:T(8,128)S(1)} %other_columns.4), channel_id=1, source_target_pairs={{0,32},{32,0},{64,96},{96,64},{128,160},{160,128},{192,224},{224,1... | collective-permute-start | bytes 319496 | tf_op jit(solution)/shard_map/ppermute | solution.py:313
  42.3 1.0 mine_columns.4
  43.3 2.8 %collective-permute-start.6 = (f32[16,1664]{1,0:T(8,128)S(1)}, f32[16,1664]{1,0:T(8,128)S(1)}, u32[]{:S(2)}, u32[]{:S(2)}) collective-permute-start(f32[16,1664]{1,0:T(8,128)S(1)} %add.8.refs_0_), channel_id=1, source_target_pairs={{0,128},{32,160},{64,192},{96,224},{128,0},{160,32},{192,64},{224,... | collective-permute-start | bytes 319496 | tf_op jit(solution)/shard_map/ppermute | solution.py:316
  46.1 0.9 collective-permute-start.5
  47.0 2.1 %collective-permute-done.6.refs_3_ = f32[16,1664]{1,0:T(8,128)S(1)} collective-permute-done((f32[16,1664]{1,0:T(8,128)S(1)}, f32[16,1664]{1,0:T(8,128)S(1)}, u32[]{:S(2)}, u32[]{:S(2)}) %collective-permute-start.6) | collective-permute-done | bytes 106528 | tf_op jit(solution)/shard_map/ppermute | solution.py:316
  49.1 2.1 %collective-permute-done.5.refs_2_ = f32[16,1664]{1,0:T(8,128)S(1)} collective-permute-done((f32[16,1664]{1,0:T(8,128)S(1)}, f32[16,1664]{1,0:T(8,128)S(1)}, u32[]{:S(2)}, u32[]{:S(2)}) %collective-permute-start.5) | collective-permute-done | bytes 106528 | tf_op jit(solution)/shard_map/ppermute | solution.py:316
  51.3 1.6 collective-permute-start.7
  52.8 1.0 mine_rows.3
  53.9 1.0 other_rows.3
  54.9 8.4 %all_to_all.42.got_ref = f32[32,1,1664]{2,1,0:T(1,128)S(1)} all-to-all(f32[32,1,1664]{2,1,0:T(1,128)S(1)} %get-tuple-element.62), channel_id=1, replica_groups={{0,16,8,24,1,17,9,25},{2,18,10,26,3,19,11,27},{4,20,12,28,5,21,13,29},{..., dimensions={0} | all-to-all | bytes 425984 | tf_op jit(solution)/shard_map/all_to_all | solution.py:300
  63.3 3.6 %collective-permute-start.10 = (f32[4,1,1664]{2,1,0:T(1,128)S(1)}, f32[4,1,1664]{2,1,0:T(1,128)S(1)}, u32[]{:S(2)}, u32[]{:S(2)}) collective-permute-start(f32[4,1,1664]{2,1,0:T(1,128)S(1)} %collect.5.refs_0_), channel_id=1, source_target_pairs={{0,4},{1,5},{2,6},{3,7},{4,0},{5,1},{6,2},{7,3},{8,12},{9,13},{10,... | collective-permute-start | bytes 79880 | tf_op jit(solution)/shard_map/ppermute | solution.py:303
  67.0 0.9 collective-permute-start.9
  67.9 1.2 collective-permute-start.8
  69.1 0.9 collective-permute-done.10.refs_3_
  70.0 2.1 %collective-permute-done.9.refs_2_ = f32[4,1,1664]{2,1,0:T(1,128)S(1)} collective-permute-done((f32[4,1,1664]{2,1,0:T(1,128)S(1)}, f32[4,1,1664]{2,1,0:T(1,128)S(1)}, u32[]{:S(2)}, u32[]{:S(2)}) %collective-permute-start.9) | collective-permute-done | bytes 26656 | tf_op jit(solution)/shard_map/ppermute | solution.py:303
  72.4 8.5 %all_to_all.43.total_ref = f32[32,1,1664]{2,1,0:T(1,128)S(1)} all-to-all(f32[32,1,1664]{2,1,0:T(1,128)S(1)} %spread.5), channel_id=1, replica_groups={{0,16,8,24,1,17,9,25},{2,18,10,26,3,19,11,27},{4,20,12,28,5,21,13,29},{..., dimensions={0} | all-to-all | bytes 425984 | tf_op jit(solution)/shard_map/all_to_all | solution.py:300
  80.9 0.9 other_columns.5
  81.8 3.6 %collective-permute-start.11 = (f32[16,1664]{1,0:T(8,128)S(1)}, f32[16,1664]{1,0:T(8,128)S(1)}, u32[]{:S(2)}, u32[]{:S(2)}) collective-permute-start(f32[16,1664]{1,0:T(8,128)S(1)} %other_columns.5), channel_id=1, source_target_pairs={{0,32},{32,0},{64,96},{96,64},{128,160},{160,128},{192,224},{224,1... | collective-permute-start | bytes 319496 | tf_op jit(solution)/shard_map/ppermute | solution.py:313
  85.4 1.0 mine_columns.5
  86.4 1.8 collective-permute-start.14
  88.2 1.8 collective-permute-start.13
  90.0 2.2 %collective-permute-done.14.refs_3_ = f32[16,1664]{1,0:T(8,128)S(1)} collective-permute-done((f32[16,1664]{1,0:T(8,128)S(1)}, f32[16,1664]{1,0:T(8,128)S(1)}, u32[]{:S(2)}, u32[]{:S(2)}) %collective-permute-start.14) | collective-permute-done | bytes 106528 | tf_op jit(solution)/shard_map/ppermute | solution.py:316
  92.2 2.8 %collective-permute-done.13.refs_2_ = f32[16,1664]{1,0:T(8,128)S(1)} collective-permute-done((f32[16,1664]{1,0:T(8,128)S(1)}, f32[16,1664]{1,0:T(8,128)S(1)}, u32[]{:S(2)}, u32[]{:S(2)}) %collective-permute-start.13) | collective-permute-done | bytes 106528 | tf_op jit(solution)/shard_map/ppermute | solution.py:316
  95.8 1.0 mine_rows.4
  96.8 1.0 other_rows.4
  97.9 8.4 %all_to_all.44.got_ref = f32[32,1,1664]{2,1,0:T(1,128)S(1)} all-to-all(f32[32,1,1664]{2,1,0:T(1,128)S(1)} %get-tuple-element.74), channel_id=1, replica_groups={{0,16,8,24,1,17,9,25},{2,18,10,26,3,19,11,27},{4,20,12,28,5,21,13,29},{..., dimensions={0} | all-to-all | bytes 425984 | tf_op jit(solution)/shard_map/all_to_all | solution.py:300
  106.3 3.6 %collective-permute-start.18 = (f32[4,1,1664]{2,1,0:T(1,128)S(1)}, f32[4,1,1664]{2,1,0:T(1,128)S(1)}, u32[]{:S(2)}, u32[]{:S(2)}) collective-permute-start(f32[4,1,1664]{2,1,0:T(1,128)S(1)} %collect.6.refs_0_), channel_id=1, source_target_pairs={{0,4},{1,5},{2,6},{3,7},{4,0},{5,1},{6,2},{7,3},{8,12},{9,13},{10,... | collective-permute-start | bytes 79880 | tf_op jit(solution)/shard_map/ppermute | solution.py:303
  109.9 0.9 collective-permute-start.17
  110.9 1.2 collective-permute-start.16
  112.0 0.9 collective-permute-done.18.refs_3_
  113.0 2.0 %collective-permute-done.17.refs_2_ = f32[4,1,1664]{2,1,0:T(1,128)S(1)} collective-permute-done((f32[4,1,1664]{2,1,0:T(1,128)S(1)}, f32[4,1,1664]{2,1,0:T(1,128)S(1)}, u32[]{:S(2)}, u32[]{:S(2)}) %collective-permute-start.17) | collective-permute-done | bytes 26656 | tf_op jit(solution)/shard_map/ppermute | solution.py:303
  115.3 8.5 %all_to_all.45.total_ref = f32[32,1,1664]{2,1,0:T(1,128)S(1)} all-to-all(f32[32,1,1664]{2,1,0:T(1,128)S(1)} %spread.6), channel_id=1, replica_groups={{0,16,8,24,1,17,9,25},{2,18,10,26,3,19,11,27},{4,20,12,28,5,21,13,29},{..., dimensions={0} | all-to-all | bytes 425984 | tf_op jit(solution)/shard_map/all_to_all | solution.py:300
  123.9 0.9 other_columns.6
  124.8 3.4 %collective-permute-start.19 = (f32[16,1664]{1,0:T(8,128)S(1)}, f32[16,1664]{1,0:T(8,128)S(1)}, u32[]{:S(2)}, u32[]{:S(2)}) collective-permute-start(f32[16,1664]{1,0:T(8,128)S(1)} %other_columns.6), channel_id=1, source_target_pairs={{0,32},{32,0},{64,96},{96,64},{128,160},{160,128},{192,224},{224,1... | collective-permute-start | bytes 319496 | tf_op jit(solution)/shard_map/ppermute | solution.py:313
  128.2 1.0 mine_columns.6
  129.3 1.8 collective-permute-start.22
  131.1 1.8 collective-permute-start.21
  132.9 2.2 %collective-permute-done.22.refs_3_ = f32[16,1664]{1,0:T(8,128)S(1)} collective-permute-done((f32[16,1664]{1,0:T(8,128)S(1)}, f32[16,1664]{1,0:T(8,128)S(1)}, u32[]{:S(2)}, u32[]{:S(2)}) %collective-permute-start.22) | collective-permute-done | bytes 106528 | tf_op jit(solution)/shard_map/ppermute | solution.py:316
  135.1 2.8 %collective-permute-done.21.refs_2_ = f32[16,1664]{1,0:T(8,128)S(1)} collective-permute-done((f32[16,1664]{1,0:T(8,128)S(1)}, f32[16,1664]{1,0:T(8,128)S(1)}, u32[]{:S(2)}, u32[]{:S(2)}) %collective-permute-start.21) | collective-permute-done | bytes 106528 | tf_op jit(solution)/shard_map/ppermute | solution.py:316
  138.6 1.0 mine_rows.5
  139.7 1.0 other_rows.5
  140.7 8.4 %all_to_all.46.got_ref = f32[32,1,1664]{2,1,0:T(1,128)S(1)} all-to-all(f32[32,1,1664]{2,1,0:T(1,128)S(1)} %get-tuple-element.86), channel_id=1, replica_groups={{0,16,8,24,1,17,9,25},{2,18,10,26,3,19,11,27},{4,20,12,28,5,21,13,29},{..., dimensions={0} | all-to-all | bytes 425984 | tf_op jit(solution)/shard_map/all_to_all | solution.py:300
  149.1 3.8 %collective-permute-start.26 = (f32[4,1,1664]{2,1,0:T(1,128)S(1)}, f32[4,1,1664]{2,1,0:T(1,128)S(1)}, u32[]{:S(2)}, u32[]{:S(2)}) collective-permute-start(f32[4,1,1664]{2,1,0:T(1,128)S(1)} %collect.7.refs_0_), channel_id=1, source_target_pairs={{0,4},{1,5},{2,6},{3,7},{4,0},{5,1},{6,2},{7,3},{8,12},{9,13},{10,... | collective-permute-start | bytes 79880 | tf_op jit(solution)/shard_map/ppermute | solution.py:303
  153.0 0.9 collective-permute-start.25
  153.9 1.2 collective-permute-start.24
  155.1 0.9 collective-permute-done.26.refs_3_
  156.0 2.0 %collective-permute-done.25.refs_2_ = f32[4,1,1664]{2,1,0:T(1,128)S(1)} collective-permute-done((f32[4,1,1664]{2,1,0:T(1,128)S(1)}, f32[4,1,1664]{2,1,0:T(1,128)S(1)}, u32[]{:S(2)}, u32[]{:S(2)}) %collective-permute-start.25) | collective-permute-done | bytes 26656 | tf_op jit(solution)/shard_map/ppermute | solution.py:303
  158.4 8.5 %all_to_all.47.total_ref = f32[32,1,1664]{2,1,0:T(1,128)S(1)} all-to-all(f32[32,1,1664]{2,1,0:T(1,128)S(1)} %spread.7), channel_id=1, replica_groups={{0,16,8,24,1,17,9,25},{2,18,10,26,3,19,11,27},{4,20,12,28,5,21,13,29},{..., dimensions={0} | all-to-all | bytes 425984 | tf_op jit(solution)/shard_map/all_to_all | solution.py:300
  166.9 0.9 other_columns.7
  167.9 3.4 %collective-permute-start.27 = (f32[16,1664]{1,0:T(8,128)S(1)}, f32[16,1664]{1,0:T(8,128)S(1)}, u32[]{:S(2)}, u32[]{:S(2)}) collective-permute-start(f32[16,1664]{1,0:T(8,128)S(1)} %other_columns.7), channel_id=1, source_target_pairs={{0,32},{32,0},{64,96},{96,64},{128,160},{160,128},{192,224},{224,1... | collective-permute-start | bytes 319496 | tf_op jit(solution)/shard_map/ppermute | solution.py:313
  171.3 0.9 mine_columns.7
  172.3 1.8 collective-permute-start.30
  174.1 1.8 collective-permute-start.29
  175.9 2.2 %collective-permute-done.30.refs_3_ = f32[16,1664]{1,0:T(8,128)S(1)} collective-permute-done((f32[16,1664]{1,0:T(8,128)S(1)}, f32[16,1664]{1,0:T(8,128)S(1)}, u32[]{:S(2)}, u32[]{:S(2)}) %collective-permute-start.30) | collective-permute-done | bytes 106528 | tf_op jit(solution)/shard_map/ppermute | solution.py:316
  178.0 2.8 %collective-permute-done.29.refs_2_ = f32[16,1664]{1,0:T(8,128)S(1)} collective-permute-done((f32[16,1664]{1,0:T(8,128)S(1)}, f32[16,1664]{1,0:T(8,128)S(1)}, u32[]{:S(2)}, u32[]{:S(2)}) %collective-permute-start.29) | collective-permute-done | bytes 106528 | tf_op jit(solution)/shard_map/ppermute | solution.py:316
  181.6 1.0 collective-permute-done.31.other_ref
  182.6 0.9 last.1
  (40 shorter events, 3.7 us)
Async XLA Ops:
  17.4 7.3 %collective-permute-start.2 = (f32[4,1,1664]{2,1,0:T(1,128)S(1)}, f32[4,1,1664]{2,1,0:T(1,128)S(1)}, u32[]{:S(2)}, u32[]{:S(2)}) collective-permute-start(f32[4,1,1664]{2,1,0:T(1,128)S(1)} %collect.4.refs_0_), channel_id=1, source_target_pairs={{0,4},{1,5},{2,6},{3,7},{4,0},{5,1},{6,2},{7,3},{8,12},{9,13},{10,... | collective-permute-start | bytes 79880 | tf_op jit(solution)/shard_map/ppermute | solution.py:303
  23.4 4.8 %collective-permute-start.1 = (f32[4,1,1664]{2,1,0:T(1,128)S(1)}, f32[4,1,1664]{2,1,0:T(1,128)S(1)}, u32[]{:S(2)}, u32[]{:S(2)}) collective-permute-start(f32[4,1,1664]{2,1,0:T(1,128)S(1)} %collect.4.refs_0_), channel_id=1, source_target_pairs={{0,6},{1,7},{2,4},{3,5},{4,2},{5,3},{6,0},{7,1},{8,14},{9,15},{10,... | collective-permute-start | bytes 79880 | tf_op jit(solution)/shard_map/ppermute | solution.py:303
  23.7 4.5 %collective-permute-start = (f32[4,1,1664]{2,1,0:T(1,128)S(1)}, f32[4,1,1664]{2,1,0:T(1,128)S(1)}, u32[]{:S(2)}, u32[]{:S(2)}) collective-permute-start(f32[4,1,1664]{2,1,0:T(1,128)S(1)} %collect.4.refs_0_), channel_id=1, source_target_pairs={{0,2},{1,3},{2,0},{3,1},{4,6},{5,7},{6,4},{7,5},{8,10},{9,11},{10,... | collective-permute-start | bytes 79880 | tf_op jit(solution)/shard_map/ppermute | solution.py:303
  37.6 5.6 %collective-permute-start.3 = (f32[16,1664]{1,0:T(8,128)S(1)}, f32[16,1664]{1,0:T(8,128)S(1)}, u32[]{:S(2)}, u32[]{:S(2)}) collective-permute-start(f32[16,1664]{1,0:T(8,128)S(1)} %other_columns.4), channel_id=1, source_target_pairs={{0,32},{32,0},{64,96},{96,64},{128,160},{160,128},{192,224},{224,1... | collective-permute-start | bytes 319496 | tf_op jit(solution)/shard_map/ppermute | solution.py:313
  43.3 5.8 %collective-permute-start.6 = (f32[16,1664]{1,0:T(8,128)S(1)}, f32[16,1664]{1,0:T(8,128)S(1)}, u32[]{:S(2)}, u32[]{:S(2)}) collective-permute-start(f32[16,1664]{1,0:T(8,128)S(1)} %add.8.refs_0_), channel_id=1, source_target_pairs={{0,128},{32,160},{64,192},{96,224},{128,0},{160,32},{192,64},{224,... | collective-permute-start | bytes 319496 | tf_op jit(solution)/shard_map/ppermute | solution.py:316
  46.1 5.1 %collective-permute-start.5 = (f32[16,1664]{1,0:T(8,128)S(1)}, f32[16,1664]{1,0:T(8,128)S(1)}, u32[]{:S(2)}, u32[]{:S(2)}) collective-permute-start(f32[16,1664]{1,0:T(8,128)S(1)} %add.8.refs_0_), channel_id=1, source_target_pairs={{0,192},{32,224},{64,128},{96,160},{128,64},{160,96},{192,0},{224,... | collective-permute-start | bytes 319496 | tf_op jit(solution)/shard_map/ppermute | solution.py:316
  47.0 4.3 %collective-permute-start.4 = (f32[16,1664]{1,0:T(8,128)S(1)}, f32[16,1664]{1,0:T(8,128)S(1)}, u32[]{:S(2)}, u32[]{:S(2)}) collective-permute-start(f32[16,1664]{1,0:T(8,128)S(1)} %add.8.refs_0_), channel_id=1, source_target_pairs={{0,64},{32,96},{64,0},{96,32},{128,192},{160,224},{192,128},{224,1... | collective-permute-start | bytes 319496 | tf_op jit(solution)/shard_map/ppermute | solution.py:316
  51.3 2.6 %collective-permute-start.7 = (f32[16,1664]{1,0:T(8,128)S(1)}, f32[16,1664]{1,0:T(8,128)S(1)}, u32[]{:S(2)}, u32[]{:S(2)}) collective-permute-start(f32[16,1664]{1,0:T(8,128)S(1)} %add.9.refs_0_), channel_id=1, source_target_pairs={{0,32},{32,0},{64,96},{96,64},{128,160},{160,128},{192,224},{224,1... | collective-permute-start | bytes 319496 | tf_op jit(solution)/shard_map/ppermute | solution.py:313
  63.3 6.7 %collective-permute-start.10 = (f32[4,1,1664]{2,1,0:T(1,128)S(1)}, f32[4,1,1664]{2,1,0:T(1,128)S(1)}, u32[]{:S(2)}, u32[]{:S(2)}) collective-permute-start(f32[4,1,1664]{2,1,0:T(1,128)S(1)} %collect.5.refs_0_), channel_id=1, source_target_pairs={{0,4},{1,5},{2,6},{3,7},{4,0},{5,1},{6,2},{7,3},{8,12},{9,13},{10,... | collective-permute-start | bytes 79880 | tf_op jit(solution)/shard_map/ppermute | solution.py:303
  67.0 5.1 %collective-permute-start.9 = (f32[4,1,1664]{2,1,0:T(1,128)S(1)}, f32[4,1,1664]{2,1,0:T(1,128)S(1)}, u32[]{:S(2)}, u32[]{:S(2)}) collective-permute-start(f32[4,1,1664]{2,1,0:T(1,128)S(1)} %collect.5.refs_0_), channel_id=1, source_target_pairs={{0,6},{1,7},{2,4},{3,5},{4,2},{5,3},{6,0},{7,1},{8,14},{9,15},{10,... | collective-permute-start | bytes 79880 | tf_op jit(solution)/shard_map/ppermute | solution.py:303
  67.9 4.5 %collective-permute-start.8 = (f32[4,1,1664]{2,1,0:T(1,128)S(1)}, f32[4,1,1664]{2,1,0:T(1,128)S(1)}, u32[]{:S(2)}, u32[]{:S(2)}) collective-permute-start(f32[4,1,1664]{2,1,0:T(1,128)S(1)} %collect.5.refs_0_), channel_id=1, source_target_pairs={{0,2},{1,3},{2,0},{3,1},{4,6},{5,7},{6,4},{7,5},{8,10},{9,11},{10,... | collective-permute-start | bytes 79880 | tf_op jit(solution)/shard_map/ppermute | solution.py:303
  81.8 4.5 %collective-permute-start.11 = (f32[16,1664]{1,0:T(8,128)S(1)}, f32[16,1664]{1,0:T(8,128)S(1)}, u32[]{:S(2)}, u32[]{:S(2)}) collective-permute-start(f32[16,1664]{1,0:T(8,128)S(1)} %other_columns.5), channel_id=1, source_target_pairs={{0,32},{32,0},{64,96},{96,64},{128,160},{160,128},{192,224},{224,1... | collective-permute-start | bytes 319496 | tf_op jit(solution)/shard_map/ppermute | solution.py:313
  86.4 5.8 %collective-permute-start.14 = (f32[16,1664]{1,0:T(8,128)S(1)}, f32[16,1664]{1,0:T(8,128)S(1)}, u32[]{:S(2)}, u32[]{:S(2)}) collective-permute-start(f32[16,1664]{1,0:T(8,128)S(1)} %add.10.refs_0_), channel_id=1, source_target_pairs={{0,128},{32,160},{64,192},{96,224},{128,0},{160,32},{192,64},{224,... | collective-permute-start | bytes 319496 | tf_op jit(solution)/shard_map/ppermute | solution.py:316
  88.2 6.9 %collective-permute-start.13 = (f32[16,1664]{1,0:T(8,128)S(1)}, f32[16,1664]{1,0:T(8,128)S(1)}, u32[]{:S(2)}, u32[]{:S(2)}) collective-permute-start(f32[16,1664]{1,0:T(8,128)S(1)} %add.10.refs_0_), channel_id=1, source_target_pairs={{0,192},{32,224},{64,128},{96,160},{128,64},{160,96},{192,0},{224,... | collective-permute-start | bytes 319496 | tf_op jit(solution)/shard_map/ppermute | solution.py:316
  90.0 5.1 %collective-permute-start.12 = (f32[16,1664]{1,0:T(8,128)S(1)}, f32[16,1664]{1,0:T(8,128)S(1)}, u32[]{:S(2)}, u32[]{:S(2)}) collective-permute-start(f32[16,1664]{1,0:T(8,128)S(1)} %add.10.refs_0_), channel_id=1, source_target_pairs={{0,64},{32,96},{64,0},{96,32},{128,192},{160,224},{192,128},{224,1... | collective-permute-start | bytes 319496 | tf_op jit(solution)/shard_map/ppermute | solution.py:316
  95.1 1.7 collective-permute-start.15
  106.3 6.7 %collective-permute-start.18 = (f32[4,1,1664]{2,1,0:T(1,128)S(1)}, f32[4,1,1664]{2,1,0:T(1,128)S(1)}, u32[]{:S(2)}, u32[]{:S(2)}) collective-permute-start(f32[4,1,1664]{2,1,0:T(1,128)S(1)} %collect.6.refs_0_), channel_id=1, source_target_pairs={{0,4},{1,5},{2,6},{3,7},{4,0},{5,1},{6,2},{7,3},{8,12},{9,13},{10,... | collective-permute-start | bytes 79880 | tf_op jit(solution)/shard_map/ppermute | solution.py:303
  109.9 5.1 %collective-permute-start.17 = (f32[4,1,1664]{2,1,0:T(1,128)S(1)}, f32[4,1,1664]{2,1,0:T(1,128)S(1)}, u32[]{:S(2)}, u32[]{:S(2)}) collective-permute-start(f32[4,1,1664]{2,1,0:T(1,128)S(1)} %collect.6.refs_0_), channel_id=1, source_target_pairs={{0,6},{1,7},{2,4},{3,5},{4,2},{5,3},{6,0},{7,1},{8,14},{9,15},{10,... | collective-permute-start | bytes 79880 | tf_op jit(solution)/shard_map/ppermute | solution.py:303
  110.9 4.5 %collective-permute-start.16 = (f32[4,1,1664]{2,1,0:T(1,128)S(1)}, f32[4,1,1664]{2,1,0:T(1,128)S(1)}, u32[]{:S(2)}, u32[]{:S(2)}) collective-permute-start(f32[4,1,1664]{2,1,0:T(1,128)S(1)} %collect.6.refs_0_), channel_id=1, source_target_pairs={{0,2},{1,3},{2,0},{3,1},{4,6},{5,7},{6,4},{7,5},{8,10},{9,11},{10,... | collective-permute-start | bytes 79880 | tf_op jit(solution)/shard_map/ppermute | solution.py:303
  124.8 4.4 %collective-permute-start.19 = (f32[16,1664]{1,0:T(8,128)S(1)}, f32[16,1664]{1,0:T(8,128)S(1)}, u32[]{:S(2)}, u32[]{:S(2)}) collective-permute-start(f32[16,1664]{1,0:T(8,128)S(1)} %other_columns.6), channel_id=1, source_target_pairs={{0,32},{32,0},{64,96},{96,64},{128,160},{160,128},{192,224},{224,1... | collective-permute-start | bytes 319496 | tf_op jit(solution)/shard_map/ppermute | solution.py:313
  129.3 5.8 %collective-permute-start.22 = (f32[16,1664]{1,0:T(8,128)S(1)}, f32[16,1664]{1,0:T(8,128)S(1)}, u32[]{:S(2)}, u32[]{:S(2)}) collective-permute-start(f32[16,1664]{1,0:T(8,128)S(1)} %add.12.refs_0_), channel_id=1, source_target_pairs={{0,128},{32,160},{64,192},{96,224},{128,0},{160,32},{192,64},{224,... | collective-permute-start | bytes 319496 | tf_op jit(solution)/shard_map/ppermute | solution.py:316
  131.1 6.9 %collective-permute-start.21 = (f32[16,1664]{1,0:T(8,128)S(1)}, f32[16,1664]{1,0:T(8,128)S(1)}, u32[]{:S(2)}, u32[]{:S(2)}) collective-permute-start(f32[16,1664]{1,0:T(8,128)S(1)} %add.12.refs_0_), channel_id=1, source_target_pairs={{0,192},{32,224},{64,128},{96,160},{128,64},{160,96},{192,0},{224,... | collective-permute-start | bytes 319496 | tf_op jit(solution)/shard_map/ppermute | solution.py:316
  132.8 5.1 %collective-permute-start.20 = (f32[16,1664]{1,0:T(8,128)S(1)}, f32[16,1664]{1,0:T(8,128)S(1)}, u32[]{:S(2)}, u32[]{:S(2)}) collective-permute-start(f32[16,1664]{1,0:T(8,128)S(1)} %add.12.refs_0_), channel_id=1, source_target_pairs={{0,64},{32,96},{64,0},{96,32},{128,192},{160,224},{192,128},{224,1... | collective-permute-start | bytes 319496 | tf_op jit(solution)/shard_map/ppermute | solution.py:316
  137.9 1.7 collective-permute-start.23
  149.1 6.9 %collective-permute-start.26 = (f32[4,1,1664]{2,1,0:T(1,128)S(1)}, f32[4,1,1664]{2,1,0:T(1,128)S(1)}, u32[]{:S(2)}, u32[]{:S(2)}) collective-permute-start(f32[4,1,1664]{2,1,0:T(1,128)S(1)} %collect.7.refs_0_), channel_id=1, source_target_pairs={{0,4},{1,5},{2,6},{3,7},{4,0},{5,1},{6,2},{7,3},{8,12},{9,13},{10,... | collective-permute-start | bytes 79880 | tf_op jit(solution)/shard_map/ppermute | solution.py:303
  153.0 5.1 %collective-permute-start.25 = (f32[4,1,1664]{2,1,0:T(1,128)S(1)}, f32[4,1,1664]{2,1,0:T(1,128)S(1)}, u32[]{:S(2)}, u32[]{:S(2)}) collective-permute-start(f32[4,1,1664]{2,1,0:T(1,128)S(1)} %collect.7.refs_0_), channel_id=1, source_target_pairs={{0,6},{1,7},{2,4},{3,5},{4,2},{5,3},{6,0},{7,1},{8,14},{9,15},{10,... | collective-permute-start | bytes 79880 | tf_op jit(solution)/shard_map/ppermute | solution.py:303
  153.9 4.5 %collective-permute-start.24 = (f32[4,1,1664]{2,1,0:T(1,128)S(1)}, f32[4,1,1664]{2,1,0:T(1,128)S(1)}, u32[]{:S(2)}, u32[]{:S(2)}) collective-permute-start(f32[4,1,1664]{2,1,0:T(1,128)S(1)} %collect.7.refs_0_), channel_id=1, source_target_pairs={{0,2},{1,3},{2,0},{3,1},{4,6},{5,7},{6,4},{7,5},{8,10},{9,11},{10,... | collective-permute-start | bytes 79880 | tf_op jit(solution)/shard_map/ppermute | solution.py:303
  167.9 4.4 %collective-permute-start.27 = (f32[16,1664]{1,0:T(8,128)S(1)}, f32[16,1664]{1,0:T(8,128)S(1)}, u32[]{:S(2)}, u32[]{:S(2)}) collective-permute-start(f32[16,1664]{1,0:T(8,128)S(1)} %other_columns.7), channel_id=1, source_target_pairs={{0,32},{32,0},{64,96},{96,64},{128,160},{160,128},{192,224},{224,1... | collective-permute-start | bytes 319496 | tf_op jit(solution)/shard_map/ppermute | solution.py:313
  172.3 5.8 %collective-permute-start.30 = (f32[16,1664]{1,0:T(8,128)S(1)}, f32[16,1664]{1,0:T(8,128)S(1)}, u32[]{:S(2)}, u32[]{:S(2)}) collective-permute-start(f32[16,1664]{1,0:T(8,128)S(1)} %add.14.refs_0_), channel_id=1, source_target_pairs={{0,128},{32,160},{64,192},{96,224},{128,0},{160,32},{192,64},{224,... | collective-permute-start | bytes 319496 | tf_op jit(solution)/shard_map/ppermute | solution.py:316
  174.1 6.8 %collective-permute-start.29 = (f32[16,1664]{1,0:T(8,128)S(1)}, f32[16,1664]{1,0:T(8,128)S(1)}, u32[]{:S(2)}, u32[]{:S(2)}) collective-permute-start(f32[16,1664]{1,0:T(8,128)S(1)} %add.14.refs_0_), channel_id=1, source_target_pairs={{0,192},{32,224},{64,128},{96,160},{128,64},{160,96},{192,0},{224,... | collective-permute-start | bytes 319496 | tf_op jit(solution)/shard_map/ppermute | solution.py:316
  175.9 5.0 %collective-permute-start.28 = (f32[16,1664]{1,0:T(8,128)S(1)}, f32[16,1664]{1,0:T(8,128)S(1)}, u32[]{:S(2)}, u32[]{:S(2)}) collective-permute-start(f32[16,1664]{1,0:T(8,128)S(1)} %add.14.refs_0_), channel_id=1, source_target_pairs={{0,64},{32,96},{64,0},{96,32},{128,192},{160,224},{192,128},{224,1... | collective-permute-start | bytes 319496 | tf_op jit(solution)/shard_map/ppermute | solution.py:316
  180.9 1.7 collective-permute-start.31

commit v6 on v5

--- a/solution.py
+++ b/solution.py
@@ -237,11 +237,18 @@
     )
 
 
-def last_kernel(inv_count, mine_ref, other_ref, shrink_ref, *refs):
+def last_mine(inv_count, mine_ref, *refs):
     *state, solution_out, residual_out = refs
-    half = mine_ref.shape[0]
-    for local, at, total_ref in zip((slice(0, half), slice(half, None)), half_slices(half), (mine_ref, other_ref)):
-        solution_out[at, :], residual_out[at, :], _ = update(inv_count, local, total_ref, shrink_ref, *state)
+    solution_out[...], residual_out[...], _ = update(inv_count, slice(0, mine_ref.shape[0]), mine_ref, *state)
+
+
+def last_other(inv_count, mine_solution, mine_residual, other_ref, *refs):
+    *state, solution_out, residual_out = refs
+    half = other_ref.shape[0]
+    mine, other = half_slices(half)
+    solution_out[mine, :] = mine_solution[...]
+    residual_out[mine, :] = mine_residual[...]
+    solution_out[other, :], residual_out[other, :], _ = update(inv_count, slice(half, None), other_ref, *state)
 
 
 def body(genotype, allele_freq, shrink, right_side):
@@ -337,7 +344,10 @@
         other = to_other(mine)
         state = [shrink, direction, residual, kept, *solution]
         if last:
-            return tuple(call(functools.partial(last_kernel, inv_count), "last", [vec, vec], [mine, other] + state))
+            outs = call(functools.partial(last_mine, inv_count), "last_mine", [halves, halves], [mine] + state)
+            return tuple(
+                call(functools.partial(last_other, inv_count), "last_other", [vec, vec], [*outs, other] + state)
+            )
         half_part = f32(half, 1, animals + EXTRA)
         outs = call(
             functools.partial(mine_rows, inv_count), "mine_rows", [halves, halves, halves, half_part],

time: 184 us -> 184 us (level)
    pallas_call x31 -> x32, Pallas kernels: 14.9 us -> 15.1 us  [call(): pl.pallas_call(kernel, in_specs=[VMEM] * len(args), out_specs=jax.tree.ma...]
where the time goes in v6:
time: 184 us; the launch traced here: 183 us
  blocking collectives  71.1 us (39%)
  starting transfers between devices  58 us (32%)
  waiting for transfers between devices  33.6 us (18%)
  Pallas kernels  20 us (11%)
    all_to_all x8, blocking collectives, exchange(): return lax.all_to_all(v, 'marker', 0, 0, tiled=True, axis_index_groups=near)  71.1 us
    ppermute x12, starting transfers between devices, far(): return lax.ppermute(v, 'marker', [(i, i ^ k) for i in range(ys * DEPTH)])  24.7 us
    ppermute x12, waiting for transfers between devices, shift(): lax.ppermute(v, 'animal', [(x * CORES + c, (x ^ d) * CORES + c) for x in...  19.4 us
    ppermute x8, starting transfers between devices, to_other(): return lax.ppermute(v, 'animal', swap)  18.8 us
    pallas_call x32, Pallas kernels, call(): pl.pallas_call(kernel, in_specs=[VMEM] * len(args), out_specs=jax.tree.ma...  15.1 us
    ppermute x12, starting transfers between devices, shift(): lax.ppermute(v, 'animal', [(x * CORES + c, (x ^ d) * CORES + c) for x in...  14.5 us
    ppermute x12, waiting for transfers between devices, far(): return lax.ppermute(v, 'marker', [(i, i ^ k) for i in range(ys * DEPTH)])  13.4 us
    pallas_call x1, Pallas kernels, body(): pl.pallas_call(first_kernel, in_specs=[ANY] * 4, out_specs=[VMEM] * 7, ou...  4.9 us
  transfers between devices with their start and end apart: 32, of which 19 were waited for; matrix products, arithmetic and copies ran while one was open for 0% of the time, Pallas kernels for 4%

profile of v6, /device:TPU:1, one launch (start us, length us, event | category | flops | bytes accessed | tf_op | source)
XLA Modules:
  0.0 183.5 jit_solution(16775185302084130690)
XLA Ops:
  0.6 4.9 %first_rows.1 = (bf16[1536,1536]{1,0:T(8,128)(2,1)S(1)}, bf16[1536,1536]{1,0:T(8,128)(2,1)S(1)}, f32[1,1536]{1,0:T(1,128)S(1)}, f32[1,1536]{1,0:T(1,128)S(1)}, f...) custom-call(f32[1536,1536]{1,0:T(8,128)} %geno_ref.1, f32[1536]{0:T(1024)} %freq_ref.1, ...), custom_call_target="tpu_custom_call" | custom-call | tf_op jit(solution)/shard_map/first_rows/pallas_call | solution.py:282
  5.5 11.8 %all_to_all.40.got_ref = f32[32,1,1664]{2,1,0:T(1,128)S(1)} all-to-all(f32[32,1,1664]{2,1,0:T(1,128)S(1)} %get-tuple-element.52), channel_id=1, replica_groups={{0,16,8,24,1,17,9,25},{2,18,10,26,3,19,11,27},{4,20,12,28,5,21,13,29},{..., dimensions={0} | all-to-all | bytes 425984 | tf_op jit(solution)/shard_map/all_to_all | solution.py:307
  17.4 6.1 %collective-permute-start.2 = (f32[4,1,1664]{2,1,0:T(1,128)S(1)}, f32[4,1,1664]{2,1,0:T(1,128)S(1)}, u32[]{:S(2)}, u32[]{:S(2)}) collective-permute-start(f32[4,1,1664]{2,1,0:T(1,128)S(1)} %collect.4.refs_0_), channel_id=1, source_target_pairs={{0,4},{1,5},{2,6},{3,7},{4,0},{5,1},{6,2},{7,3},{8,12},{9,13},{10,... | collective-permute-start | bytes 79880 | tf_op jit(solution)/shard_map/ppermute | solution.py:310
  23.7 0.9 collective-permute-start
  24.7 3.6 %collective-permute-done.1.refs_2_ = f32[4,1,1664]{2,1,0:T(1,128)S(1)} collective-permute-done((f32[4,1,1664]{2,1,0:T(1,128)S(1)}, f32[4,1,1664]{2,1,0:T(1,128)S(1)}, u32[]{:S(2)}, u32[]{:S(2)}) %collective-permute-start.1) | collective-permute-done | bytes 26656 | tf_op jit(solution)/shard_map/ppermute | solution.py:310
  28.3 8.4 %all_to_all.41.total_ref = f32[32,1,1664]{2,1,0:T(1,128)S(1)} all-to-all(f32[32,1,1664]{2,1,0:T(1,128)S(1)} %spread.4), channel_id=1, replica_groups={{0,16,8,24,1,17,9,25},{2,18,10,26,3,19,11,27},{4,20,12,28,5,21,13,29},{..., dimensions={0} | all-to-all | bytes 425984 | tf_op jit(solution)/shard_map/all_to_all | solution.py:307
  36.7 0.9 other_columns.4
  37.6 4.7 %collective-permute-start.3 = (f32[16,1664]{1,0:T(8,128)S(1)}, f32[16,1664]{1,0:T(8,128)S(1)}, u32[]{:S(2)}, u32[]{:S(2)}) collective-permute-start(f32[16,1664]{1,0:T(8,128)S(1)} %other_columns.4), channel_id=1, source_target_pairs={{0,32},{32,0},{64,96},{96,64},{128,160},{160,128},{192,224},{224,1... | collective-permute-start | bytes 319496 | tf_op jit(solution)/shard_map/ppermute | solution.py:320
  42.3 1.0 mine_columns.4
  43.3 2.8 %collective-permute-start.6 = (f32[16,1664]{1,0:T(8,128)S(1)}, f32[16,1664]{1,0:T(8,128)S(1)}, u32[]{:S(2)}, u32[]{:S(2)}) collective-permute-start(f32[16,1664]{1,0:T(8,128)S(1)} %add.8.refs_0_), channel_id=1, source_target_pairs={{0,128},{32,160},{64,192},{96,224},{128,0},{160,32},{192,64},{224,... | collective-permute-start | bytes 319496 | tf_op jit(solution)/shard_map/ppermute | solution.py:323
  46.1 0.9 collective-permute-start.5
  47.0 2.1 %collective-permute-done.6.refs_3_ = f32[16,1664]{1,0:T(8,128)S(1)} collective-permute-done((f32[16,1664]{1,0:T(8,128)S(1)}, f32[16,1664]{1,0:T(8,128)S(1)}, u32[]{:S(2)}, u32[]{:S(2)}) %collective-permute-start.6) | collective-permute-done | bytes 106528 | tf_op jit(solution)/shard_map/ppermute | solution.py:323
  49.1 2.1 %collective-permute-done.5.refs_2_ = f32[16,1664]{1,0:T(8,128)S(1)} collective-permute-done((f32[16,1664]{1,0:T(8,128)S(1)}, f32[16,1664]{1,0:T(8,128)S(1)}, u32[]{:S(2)}, u32[]{:S(2)}) %collective-permute-start.5) | collective-permute-done | bytes 106528 | tf_op jit(solution)/shard_map/ppermute | solution.py:323
  51.3 1.6 collective-permute-start.7
  52.8 1.0 mine_rows.3
  53.9 1.0 other_rows.3
  54.9 8.4 %all_to_all.42.got_ref = f32[32,1,1664]{2,1,0:T(1,128)S(1)} all-to-all(f32[32,1,1664]{2,1,0:T(1,128)S(1)} %get-tuple-element.64), channel_id=1, replica_groups={{0,16,8,24,1,17,9,25},{2,18,10,26,3,19,11,27},{4,20,12,28,5,21,13,29},{..., dimensions={0} | all-to-all | bytes 425984 | tf_op jit(solution)/shard_map/all_to_all | solution.py:307
  63.3 3.6 %collective-permute-start.10 = (f32[4,1,1664]{2,1,0:T(1,128)S(1)}, f32[4,1,1664]{2,1,0:T(1,128)S(1)}, u32[]{:S(2)}, u32[]{:S(2)}) collective-permute-start(f32[4,1,1664]{2,1,0:T(1,128)S(1)} %collect.5.refs_0_), channel_id=1, source_target_pairs={{0,4},{1,5},{2,6},{3,7},{4,0},{5,1},{6,2},{7,3},{8,12},{9,13},{10,... | collective-permute-start | bytes 79880 | tf_op jit(solution)/shard_map/ppermute | solution.py:310
  67.0 0.9 collective-permute-start.9
  67.9 1.2 collective-permute-start.8
  69.1 0.9 collective-permute-done.10.refs_3_
  70.0 2.1 %collective-permute-done.9.refs_2_ = f32[4,1,1664]{2,1,0:T(1,128)S(1)} collective-permute-done((f32[4,1,1664]{2,1,0:T(1,128)S(1)}, f32[4,1,1664]{2,1,0:T(1,128)S(1)}, u32[]{:S(2)}, u32[]{:S(2)}) %collective-permute-start.9) | collective-permute-done | bytes 26656 | tf_op jit(solution)/shard_map/ppermute | solution.py:310
  72.4 8.5 %all_to_all.43.total_ref = f32[32,1,1664]{2,1,0:T(1,128)S(1)} all-to-all(f32[32,1,1664]{2,1,0:T(1,128)S(1)} %spread.5), channel_id=1, replica_groups={{0,16,8,24,1,17,9,25},{2,18,10,26,3,19,11,27},{4,20,12,28,5,21,13,29},{..., dimensions={0} | all-to-all | bytes 425984 | tf_op jit(solution)/shard_map/all_to_all | solution.py:307
  80.9 0.9 other_columns.5
  81.8 3.6 %collective-permute-start.11 = (f32[16,1664]{1,0:T(8,128)S(1)}, f32[16,1664]{1,0:T(8,128)S(1)}, u32[]{:S(2)}, u32[]{:S(2)}) collective-permute-start(f32[16,1664]{1,0:T(8,128)S(1)} %other_columns.5), channel_id=1, source_target_pairs={{0,32},{32,0},{64,96},{96,64},{128,160},{160,128},{192,224},{224,1... | collective-permute-start | bytes 319496 | tf_op jit(solution)/shard_map/ppermute | solution.py:320
  85.4 1.0 mine_columns.5
  86.4 1.8 collective-permute-start.14
  88.2 1.8 collective-permute-start.13
  90.0 2.2 %collective-permute-done.14.refs_3_ = f32[16,1664]{1,0:T(8,128)S(1)} collective-permute-done((f32[16,1664]{1,0:T(8,128)S(1)}, f32[16,1664]{1,0:T(8,128)S(1)}, u32[]{:S(2)}, u32[]{:S(2)}) %collective-permute-start.14) | collective-permute-done | bytes 106528 | tf_op jit(solution)/shard_map/ppermute | solution.py:323
  92.2 2.8 %collective-permute-done.13.refs_2_ = f32[16,1664]{1,0:T(8,128)S(1)} collective-permute-done((f32[16,1664]{1,0:T(8,128)S(1)}, f32[16,1664]{1,0:T(8,128)S(1)}, u32[]{:S(2)}, u32[]{:S(2)}) %collective-permute-start.13) | collective-permute-done | bytes 106528 | tf_op jit(solution)/shard_map/ppermute | solution.py:323
  95.8 1.0 mine_rows.4
  96.8 1.0 other_rows.4
  97.9 8.4 %all_to_all.44.got_ref = f32[32,1,1664]{2,1,0:T(1,128)S(1)} all-to-all(f32[32,1,1664]{2,1,0:T(1,128)S(1)} %get-tuple-element.76), channel_id=1, replica_groups={{0,16,8,24,1,17,9,25},{2,18,10,26,3,19,11,27},{4,20,12,28,5,21,13,29},{..., dimensions={0} | all-to-all | bytes 425984 | tf_op jit(solution)/shard_map/all_to_all | solution.py:307
  106.3 3.6 %collective-permute-start.18 = (f32[4,1,1664]{2,1,0:T(1,128)S(1)}, f32[4,1,1664]{2,1,0:T(1,128)S(1)}, u32[]{:S(2)}, u32[]{:S(2)}) collective-permute-start(f32[4,1,1664]{2,1,0:T(1,128)S(1)} %collect.6.refs_0_), channel_id=1, source_target_pairs={{0,4},{1,5},{2,6},{3,7},{4,0},{5,1},{6,2},{7,3},{8,12},{9,13},{10,... | collective-permute-start | bytes 79880 | tf_op jit(solution)/shard_map/ppermute | solution.py:310
  109.9 0.9 collective-permute-start.17
  110.9 1.2 collective-permute-start.16
  112.0 0.9 collective-permute-done.18.refs_3_
  113.0 2.0 %collective-permute-done.17.refs_2_ = f32[4,1,1664]{2,1,0:T(1,128)S(1)} collective-permute-done((f32[4,1,1664]{2,1,0:T(1,128)S(1)}, f32[4,1,1664]{2,1,0:T(1,128)S(1)}, u32[]{:S(2)}, u32[]{:S(2)}) %collective-permute-start.17) | collective-permute-done | bytes 26656 | tf_op jit(solution)/shard_map/ppermute | solution.py:310
  115.3 8.5 %all_to_all.45.total_ref = f32[32,1,1664]{2,1,0:T(1,128)S(1)} all-to-all(f32[32,1,1664]{2,1,0:T(1,128)S(1)} %spread.6), channel_id=1, replica_groups={{0,16,8,24,1,17,9,25},{2,18,10,26,3,19,11,27},{4,20,12,28,5,21,13,29},{..., dimensions={0} | all-to-all | bytes 425984 | tf_op jit(solution)/shard_map/all_to_all | solution.py:307
  123.9 0.9 other_columns.6
  124.8 3.4 %collective-permute-start.19 = (f32[16,1664]{1,0:T(8,128)S(1)}, f32[16,1664]{1,0:T(8,128)S(1)}, u32[]{:S(2)}, u32[]{:S(2)}) collective-permute-start(f32[16,1664]{1,0:T(8,128)S(1)} %other_columns.6), channel_id=1, source_target_pairs={{0,32},{32,0},{64,96},{96,64},{128,160},{160,128},{192,224},{224,1... | collective-permute-start | bytes 319496 | tf_op jit(solution)/shard_map/ppermute | solution.py:320
  128.2 1.0 mine_columns.6
  129.3 1.8 collective-permute-start.22
  131.1 1.8 collective-permute-start.21
  132.9 2.2 %collective-permute-done.22.refs_3_ = f32[16,1664]{1,0:T(8,128)S(1)} collective-permute-done((f32[16,1664]{1,0:T(8,128)S(1)}, f32[16,1664]{1,0:T(8,128)S(1)}, u32[]{:S(2)}, u32[]{:S(2)}) %collective-permute-start.22) | collective-permute-done | bytes 106528 | tf_op jit(solution)/shard_map/ppermute | solution.py:323
  135.1 2.8 %collective-permute-done.21.refs_2_ = f32[16,1664]{1,0:T(8,128)S(1)} collective-permute-done((f32[16,1664]{1,0:T(8,128)S(1)}, f32[16,1664]{1,0:T(8,128)S(1)}, u32[]{:S(2)}, u32[]{:S(2)}) %collective-permute-start.21) | collective-permute-done | bytes 106528 | tf_op jit(solution)/shard_map/ppermute | solution.py:323
  138.6 1.0 mine_rows.5
  139.7 1.0 other_rows.5
  140.7 8.4 %all_to_all.46.got_ref = f32[32,1,1664]{2,1,0:T(1,128)S(1)} all-to-all(f32[32,1,1664]{2,1,0:T(1,128)S(1)} %get-tuple-element.88), channel_id=1, replica_groups={{0,16,8,24,1,17,9,25},{2,18,10,26,3,19,11,27},{4,20,12,28,5,21,13,29},{..., dimensions={0} | all-to-all | bytes 425984 | tf_op jit(solution)/shard_map/all_to_all | solution.py:307
  149.1 3.8 %collective-permute-start.26 = (f32[4,1,1664]{2,1,0:T(1,128)S(1)}, f32[4,1,1664]{2,1,0:T(1,128)S(1)}, u32[]{:S(2)}, u32[]{:S(2)}) collective-permute-start(f32[4,1,1664]{2,1,0:T(1,128)S(1)} %collect.7.refs_0_), channel_id=1, source_target_pairs={{0,4},{1,5},{2,6},{3,7},{4,0},{5,1},{6,2},{7,3},{8,12},{9,13},{10,... | collective-permute-start | bytes 79880 | tf_op jit(solution)/shard_map/ppermute | solution.py:310
  153.0 0.9 collective-permute-start.25
  153.9 1.2 collective-permute-start.24
  155.1 0.9 collective-permute-done.26.refs_3_
  156.0 2.0 %collective-permute-done.25.refs_2_ = f32[4,1,1664]{2,1,0:T(1,128)S(1)} collective-permute-done((f32[4,1,1664]{2,1,0:T(1,128)S(1)}, f32[4,1,1664]{2,1,0:T(1,128)S(1)}, u32[]{:S(2)}, u32[]{:S(2)}) %collective-permute-start.25) | collective-permute-done | bytes 26656 | tf_op jit(solution)/shard_map/ppermute | solution.py:310
  158.4 8.5 %all_to_all.47.total_ref = f32[32,1,1664]{2,1,0:T(1,128)S(1)} all-to-all(f32[32,1,1664]{2,1,0:T(1,128)S(1)} %spread.7), channel_id=1, replica_groups={{0,16,8,24,1,17,9,25},{2,18,10,26,3,19,11,27},{4,20,12,28,5,21,13,29},{..., dimensions={0} | all-to-all | bytes 425984 | tf_op jit(solution)/shard_map/all_to_all | solution.py:307
  166.9 0.9 other_columns.7
  167.9 3.4 %collective-permute-start.27 = (f32[16,1664]{1,0:T(8,128)S(1)}, f32[16,1664]{1,0:T(8,128)S(1)}, u32[]{:S(2)}, u32[]{:S(2)}) collective-permute-start(f32[16,1664]{1,0:T(8,128)S(1)} %other_columns.7), channel_id=1, source_target_pairs={{0,32},{32,0},{64,96},{96,64},{128,160},{160,128},{192,224},{224,1... | collective-permute-start | bytes 319496 | tf_op jit(solution)/shard_map/ppermute | solution.py:320
  171.3 0.9 mine_columns.7
  172.3 1.8 collective-permute-start.30
  174.1 1.8 collective-permute-start.29
  175.9 2.2 %collective-permute-done.30.refs_3_ = f32[16,1664]{1,0:T(8,128)S(1)} collective-permute-done((f32[16,1664]{1,0:T(8,128)S(1)}, f32[16,1664]{1,0:T(8,128)S(1)}, u32[]{:S(2)}, u32[]{:S(2)}) %collective-permute-start.30) | collective-permute-done | bytes 106528 | tf_op jit(solution)/shard_map/ppermute | solution.py:323
  178.0 2.8 %collective-permute-done.29.refs_2_ = f32[16,1664]{1,0:T(8,128)S(1)} collective-permute-done((f32[16,1664]{1,0:T(8,128)S(1)}, f32[16,1664]{1,0:T(8,128)S(1)}, u32[]{:S(2)}, u32[]{:S(2)}) %collective-permute-start.29) | collective-permute-done | bytes 106528 | tf_op jit(solution)/shard_map/ppermute | solution.py:323
  181.8 0.8 collective-permute-done.31.other_ref
  182.6 0.9 last_other.1
  (41 shorter events, 3.8 us)
Async XLA Ops:
  17.4 7.3 %collective-permute-start.2 = (f32[4,1,1664]{2,1,0:T(1,128)S(1)}, f32[4,1,1664]{2,1,0:T(1,128)S(1)}, u32[]{:S(2)}, u32[]{:S(2)}) collective-permute-start(f32[4,1,1664]{2,1,0:T(1,128)S(1)} %collect.4.refs_0_), channel_id=1, source_target_pairs={{0,4},{1,5},{2,6},{3,7},{4,0},{5,1},{6,2},{7,3},{8,12},{9,13},{10,... | collective-permute-start | bytes 79880 | tf_op jit(solution)/shard_map/ppermute | solution.py:310
  23.4 4.8 %collective-permute-start.1 = (f32[4,1,1664]{2,1,0:T(1,128)S(1)}, f32[4,1,1664]{2,1,0:T(1,128)S(1)}, u32[]{:S(2)}, u32[]{:S(2)}) collective-permute-start(f32[4,1,1664]{2,1,0:T(1,128)S(1)} %collect.4.refs_0_), channel_id=1, source_target_pairs={{0,6},{1,7},{2,4},{3,5},{4,2},{5,3},{6,0},{7,1},{8,14},{9,15},{10,... | collective-permute-start | bytes 79880 | tf_op jit(solution)/shard_map/ppermute | solution.py:310
  23.7 4.5 %collective-permute-start = (f32[4,1,1664]{2,1,0:T(1,128)S(1)}, f32[4,1,1664]{2,1,0:T(1,128)S(1)}, u32[]{:S(2)}, u32[]{:S(2)}) collective-permute-start(f32[4,1,1664]{2,1,0:T(1,128)S(1)} %collect.4.refs_0_), channel_id=1, source_target_pairs={{0,2},{1,3},{2,0},{3,1},{4,6},{5,7},{6,4},{7,5},{8,10},{9,11},{10,... | collective-permute-start | bytes 79880 | tf_op jit(solution)/shard_map/ppermute | solution.py:310
  37.6 5.6 %collective-permute-start.3 = (f32[16,1664]{1,0:T(8,128)S(1)}, f32[16,1664]{1,0:T(8,128)S(1)}, u32[]{:S(2)}, u32[]{:S(2)}) collective-permute-start(f32[16,1664]{1,0:T(8,128)S(1)} %other_columns.4), channel_id=1, source_target_pairs={{0,32},{32,0},{64,96},{96,64},{128,160},{160,128},{192,224},{224,1... | collective-permute-start | bytes 319496 | tf_op jit(solution)/shard_map/ppermute | solution.py:320
  43.3 5.8 %collective-permute-start.6 = (f32[16,1664]{1,0:T(8,128)S(1)}, f32[16,1664]{1,0:T(8,128)S(1)}, u32[]{:S(2)}, u32[]{:S(2)}) collective-permute-start(f32[16,1664]{1,0:T(8,128)S(1)} %add.8.refs_0_), channel_id=1, source_target_pairs={{0,128},{32,160},{64,192},{96,224},{128,0},{160,32},{192,64},{224,... | collective-permute-start | bytes 319496 | tf_op jit(solution)/shard_map/ppermute | solution.py:323
  46.1 5.1 %collective-permute-start.5 = (f32[16,1664]{1,0:T(8,128)S(1)}, f32[16,1664]{1,0:T(8,128)S(1)}, u32[]{:S(2)}, u32[]{:S(2)}) collective-permute-start(f32[16,1664]{1,0:T(8,128)S(1)} %add.8.refs_0_), channel_id=1, source_target_pairs={{0,192},{32,224},{64,128},{96,160},{128,64},{160,96},{192,0},{224,... | collective-permute-start | bytes 319496 | tf_op jit(solution)/shard_map/ppermute | solution.py:323
  47.0 4.3 %collective-permute-start.4 = (f32[16,1664]{1,0:T(8,128)S(1)}, f32[16,1664]{1,0:T(8,128)S(1)}, u32[]{:S(2)}, u32[]{:S(2)}) collective-permute-start(f32[16,1664]{1,0:T(8,128)S(1)} %add.8.refs_0_), channel_id=1, source_target_pairs={{0,64},{32,96},{64,0},{96,32},{128,192},{160,224},{192,128},{224,1... | collective-permute-start | bytes 319496 | tf_op jit(solution)/shard_map/ppermute | solution.py:323
  51.3 2.6 %collective-permute-start.7 = (f32[16,1664]{1,0:T(8,128)S(1)}, f32[16,1664]{1,0:T(8,128)S(1)}, u32[]{:S(2)}, u32[]{:S(2)}) collective-permute-start(f32[16,1664]{1,0:T(8,128)S(1)} %add.9.refs_0_), channel_id=1, source_target_pairs={{0,32},{32,0},{64,96},{96,64},{128,160},{160,128},{192,224},{224,1... | collective-permute-start | bytes 319496 | tf_op jit(solution)/shard_map/ppermute | solution.py:320
  63.3 6.7 %collective-permute-start.10 = (f32[4,1,1664]{2,1,0:T(1,128)S(1)}, f32[4,1,1664]{2,1,0:T(1,128)S(1)}, u32[]{:S(2)}, u32[]{:S(2)}) collective-permute-start(f32[4,1,1664]{2,1,0:T(1,128)S(1)} %collect.5.refs_0_), channel_id=1, source_target_pairs={{0,4},{1,5},{2,6},{3,7},{4,0},{5,1},{6,2},{7,3},{8,12},{9,13},{10,... | collective-permute-start | bytes 79880 | tf_op jit(solution)/shard_map/ppermute | solution.py:310
  67.0 5.1 %collective-permute-start.9 = (f32[4,1,1664]{2,1,0:T(1,128)S(1)}, f32[4,1,1664]{2,1,0:T(1,128)S(1)}, u32[]{:S(2)}, u32[]{:S(2)}) collective-permute-start(f32[4,1,1664]{2,1,0:T(1,128)S(1)} %collect.5.refs_0_), channel_id=1, source_target_pairs={{0,6},{1,7},{2,4},{3,5},{4,2},{5,3},{6,0},{7,1},{8,14},{9,15},{10,... | collective-permute-start | bytes 79880 | tf_op jit(solution)/shard_map/ppermute | solution.py:310
  67.9 4.5 %collective-permute-start.8 = (f32[4,1,1664]{2,1,0:T(1,128)S(1)}, f32[4,1,1664]{2,1,0:T(1,128)S(1)}, u32[]{:S(2)}, u32[]{:S(2)}) collective-permute-start(f32[4,1,1664]{2,1,0:T(1,128)S(1)} %collect.5.refs_0_), channel_id=1, source_target_pairs={{0,2},{1,3},{2,0},{3,1},{4,6},{5,7},{6,4},{7,5},{8,10},{9,11},{10,... | collective-permute-start | bytes 79880 | tf_op jit(solution)/shard_map/ppermute | solution.py:310
  81.8 4.5 %collective-permute-start.11 = (f32[16,1664]{1,0:T(8,128)S(1)}, f32[16,1664]{1,0:T(8,128)S(1)}, u32[]{:S(2)}, u32[]{:S(2)}) collective-permute-start(f32[16,1664]{1,0:T(8,128)S(1)} %other_columns.5), channel_id=1, source_target_pairs={{0,32},{32,0},{64,96},{96,64},{128,160},{160,128},{192,224},{224,1... | collective-permute-start | bytes 319496 | tf_op jit(solution)/shard_map/ppermute | solution.py:320
  86.4 5.8 %collective-permute-start.14 = (f32[16,1664]{1,0:T(8,128)S(1)}, f32[16,1664]{1,0:T(8,128)S(1)}, u32[]{:S(2)}, u32[]{:S(2)}) collective-permute-start(f32[16,1664]{1,0:T(8,128)S(1)} %add.10.refs_0_), channel_id=1, source_target_pairs={{0,128},{32,160},{64,192},{96,224},{128,0},{160,32},{192,64},{224,... | collective-permute-start | bytes 319496 | tf_op jit(solution)/shard_map/ppermute | solution.py:323
  88.2 6.9 %collective-permute-start.13 = (f32[16,1664]{1,0:T(8,128)S(1)}, f32[16,1664]{1,0:T(8,128)S(1)}, u32[]{:S(2)}, u32[]{:S(2)}) collective-permute-start(f32[16,1664]{1,0:T(8,128)S(1)} %add.10.refs_0_), channel_id=1, source_target_pairs={{0,192},{32,224},{64,128},{96,160},{128,64},{160,96},{192,0},{224,... | collective-permute-start | bytes 319496 | tf_op jit(solution)/shard_map/ppermute | solution.py:323
  90.0 5.1 %collective-permute-start.12 = (f32[16,1664]{1,0:T(8,128)S(1)}, f32[16,1664]{1,0:T(8,128)S(1)}, u32[]{:S(2)}, u32[]{:S(2)}) collective-permute-start(f32[16,1664]{1,0:T(8,128)S(1)} %add.10.refs_0_), channel_id=1, source_target_pairs={{0,64},{32,96},{64,0},{96,32},{128,192},{160,224},{192,128},{224,1... | collective-permute-start | bytes 319496 | tf_op jit(solution)/shard_map/ppermute | solution.py:323
  95.1 1.7 collective-permute-start.15
  106.3 6.7 %collective-permute-start.18 = (f32[4,1,1664]{2,1,0:T(1,128)S(1)}, f32[4,1,1664]{2,1,0:T(1,128)S(1)}, u32[]{:S(2)}, u32[]{:S(2)}) collective-permute-start(f32[4,1,1664]{2,1,0:T(1,128)S(1)} %collect.6.refs_0_), channel_id=1, source_target_pairs={{0,4},{1,5},{2,6},{3,7},{4,0},{5,1},{6,2},{7,3},{8,12},{9,13},{10,... | collective-permute-start | bytes 79880 | tf_op jit(solution)/shard_map/ppermute | solution.py:310
  109.9 5.1 %collective-permute-start.17 = (f32[4,1,1664]{2,1,0:T(1,128)S(1)}, f32[4,1,1664]{2,1,0:T(1,128)S(1)}, u32[]{:S(2)}, u32[]{:S(2)}) collective-permute-start(f32[4,1,1664]{2,1,0:T(1,128)S(1)} %collect.6.refs_0_), channel_id=1, source_target_pairs={{0,6},{1,7},{2,4},{3,5},{4,2},{5,3},{6,0},{7,1},{8,14},{9,15},{10,... | collective-permute-start | bytes 79880 | tf_op jit(solution)/shard_map/ppermute | solution.py:310
  110.9 4.5 %collective-permute-start.16 = (f32[4,1,1664]{2,1,0:T(1,128)S(1)}, f32[4,1,1664]{2,1,0:T(1,128)S(1)}, u32[]{:S(2)}, u32[]{:S(2)}) collective-permute-start(f32[4,1,1664]{2,1,0:T(1,128)S(1)} %collect.6.refs_0_), channel_id=1, source_target_pairs={{0,2},{1,3},{2,0},{3,1},{4,6},{5,7},{6,4},{7,5},{8,10},{9,11},{10,... | collective-permute-start | bytes 79880 | tf_op jit(solution)/shard_map/ppermute | solution.py:310
  124.8 4.4 %collective-permute-start.19 = (f32[16,1664]{1,0:T(8,128)S(1)}, f32[16,1664]{1,0:T(8,128)S(1)}, u32[]{:S(2)}, u32[]{:S(2)}) collective-permute-start(f32[16,1664]{1,0:T(8,128)S(1)} %other_columns.6), channel_id=1, source_target_pairs={{0,32},{32,0},{64,96},{96,64},{128,160},{160,128},{192,224},{224,1... | collective-permute-start | bytes 319496 | tf_op jit(solution)/shard_map/ppermute | solution.py:320
  129.3 5.8 %collective-permute-start.22 = (f32[16,1664]{1,0:T(8,128)S(1)}, f32[16,1664]{1,0:T(8,128)S(1)}, u32[]{:S(2)}, u32[]{:S(2)}) collective-permute-start(f32[16,1664]{1,0:T(8,128)S(1)} %add.12.refs_0_), channel_id=1, source_target_pairs={{0,128},{32,160},{64,192},{96,224},{128,0},{160,32},{192,64},{224,... | collective-permute-start | bytes 319496 | tf_op jit(solution)/shard_map/ppermute | solution.py:323
  131.1 6.9 %collective-permute-start.21 = (f32[16,1664]{1,0:T(8,128)S(1)}, f32[16,1664]{1,0:T(8,128)S(1)}, u32[]{:S(2)}, u32[]{:S(2)}) collective-permute-start(f32[16,1664]{1,0:T(8,128)S(1)} %add.12.refs_0_), channel_id=1, source_target_pairs={{0,192},{32,224},{64,128},{96,160},{128,64},{160,96},{192,0},{224,... | collective-permute-start | bytes 319496 | tf_op jit(solution)/shard_map/ppermute | solution.py:323
  132.8 5.1 %collective-permute-start.20 = (f32[16,1664]{1,0:T(8,128)S(1)}, f32[16,1664]{1,0:T(8,128)S(1)}, u32[]{:S(2)}, u32[]{:S(2)}) collective-permute-start(f32[16,1664]{1,0:T(8,128)S(1)} %add.12.refs_0_), channel_id=1, source_target_pairs={{0,64},{32,96},{64,0},{96,32},{128,192},{160,224},{192,128},{224,1... | collective-permute-start | bytes 319496 | tf_op jit(solution)/shard_map/ppermute | solution.py:323
  137.9 1.7 collective-permute-start.23
  149.1 6.9 %collective-permute-start.26 = (f32[4,1,1664]{2,1,0:T(1,128)S(1)}, f32[4,1,1664]{2,1,0:T(1,128)S(1)}, u32[]{:S(2)}, u32[]{:S(2)}) collective-permute-start(f32[4,1,1664]{2,1,0:T(1,128)S(1)} %collect.7.refs_0_), channel_id=1, source_target_pairs={{0,4},{1,5},{2,6},{3,7},{4,0},{5,1},{6,2},{7,3},{8,12},{9,13},{10,... | collective-permute-start | bytes 79880 | tf_op jit(solution)/shard_map/ppermute | solution.py:310
  153.0 5.1 %collective-permute-start.25 = (f32[4,1,1664]{2,1,0:T(1,128)S(1)}, f32[4,1,1664]{2,1,0:T(1,128)S(1)}, u32[]{:S(2)}, u32[]{:S(2)}) collective-permute-start(f32[4,1,1664]{2,1,0:T(1,128)S(1)} %collect.7.refs_0_), channel_id=1, source_target_pairs={{0,6},{1,7},{2,4},{3,5},{4,2},{5,3},{6,0},{7,1},{8,14},{9,15},{10,... | collective-permute-start | bytes 79880 | tf_op jit(solution)/shard_map/ppermute | solution.py:310
  153.9 4.5 %collective-permute-start.24 = (f32[4,1,1664]{2,1,0:T(1,128)S(1)}, f32[4,1,1664]{2,1,0:T(1,128)S(1)}, u32[]{:S(2)}, u32[]{:S(2)}) collective-permute-start(f32[4,1,1664]{2,1,0:T(1,128)S(1)} %collect.7.refs_0_), channel_id=1, source_target_pairs={{0,2},{1,3},{2,0},{3,1},{4,6},{5,7},{6,4},{7,5},{8,10},{9,11},{10,... | collective-permute-start | bytes 79880 | tf_op jit(solution)/shard_map/ppermute | solution.py:310
  167.9 4.4 %collective-permute-start.27 = (f32[16,1664]{1,0:T(8,128)S(1)}, f32[16,1664]{1,0:T(8,128)S(1)}, u32[]{:S(2)}, u32[]{:S(2)}) collective-permute-start(f32[16,1664]{1,0:T(8,128)S(1)} %other_columns.7), channel_id=1, source_target_pairs={{0,32},{32,0},{64,96},{96,64},{128,160},{160,128},{192,224},{224,1... | collective-permute-start | bytes 319496 | tf_op jit(solution)/shard_map/ppermute | solution.py:320
  172.3 5.8 %collective-permute-start.30 = (f32[16,1664]{1,0:T(8,128)S(1)}, f32[16,1664]{1,0:T(8,128)S(1)}, u32[]{:S(2)}, u32[]{:S(2)}) collective-permute-start(f32[16,1664]{1,0:T(8,128)S(1)} %add.14.refs_0_), channel_id=1, source_target_pairs={{0,128},{32,160},{64,192},{96,224},{128,0},{160,32},{192,64},{224,... | collective-permute-start | bytes 319496 | tf_op jit(solution)/shard_map/ppermute | solution.py:323
  174.1 6.8 %collective-permute-start.29 = (f32[16,1664]{1,0:T(8,128)S(1)}, f32[16,1664]{1,0:T(8,128)S(1)}, u32[]{:S(2)}, u32[]{:S(2)}) collective-permute-start(f32[16,1664]{1,0:T(8,128)S(1)} %add.14.refs_0_), channel_id=1, source_target_pairs={{0,192},{32,224},{64,128},{96,160},{128,64},{160,96},{192,0},{224,... | collective-permute-start | bytes 319496 | tf_op jit(solution)/shard_map/ppermute | solution.py:323
  175.9 5.0 %collective-permute-start.28 = (f32[16,1664]{1,0:T(8,128)S(1)}, f32[16,1664]{1,0:T(8,128)S(1)}, u32[]{:S(2)}, u32[]{:S(2)}) collective-permute-start(f32[16,1664]{1,0:T(8,128)S(1)} %add.14.refs_0_), channel_id=1, source_target_pairs={{0,64},{32,96},{64,0},{96,32},{128,192},{160,224},{192,128},{224,1... | collective-permute-start | bytes 319496 | tf_op jit(solution)/shard_map/ppermute | solution.py:323
  180.9 1.7 collective-permute-start.31
